TPU v7x, 32 devices: a whole 2x2x4 slice. The times are simulated.
32 devices in a mesh: pool: 4 (over y, x), expert: 8 (over z, core).
Axes of the slice: x: 2, y: 2, z: 4, core: 2. Of those that a mesh axis runs over, the one named last changes fastest.
Arguments:
- queries: bfloat16 [1024, 4096], P(('pool', 'expert')), may hold values from -6 to 6
- kv_cache: bfloat16 [1024, 64, 1024], P(('pool', 'expert')), may hold values from -6 to 6
- block_index: int32 [1024, 8], P(('pool', 'expert')), may hold values from 0 to 31, as said below
- lengths: int32 [1024], P(('pool', 'expert')), may hold values from 2 to 512, as said below
- residual: bfloat16 [1024, 2048], P('pool', 'expert'), may hold values from -21 to 21
- out_weight: bfloat16 [4096, 2048], P(None, 'expert'), may hold values from -0.09375 to 0.09375
- norm_gain: float32 [2048], P('expert'), may hold values from 0.25 to 1.75
- expert_ids: int32 [1024, 8], P('pool'), may hold values from 0 to 31, all different within a row; in each aligned block of 256 rows (0 to 255, 256 to 511, ...) at most 128 rows name the same one
- route_weights: float32 [1024, 8], P('pool'), may hold values from 0.02 to 0.25
- gate_weight: bfloat16 [32, 2048, 768], P(('pool', 'expert')), may hold values from -0.125 to 0.125
- up_weight: bfloat16 [32, 2048, 768], P(('pool', 'expert')), may hold values from -0.125 to 0.125
- down_weight: bfloat16 [32, 768, 2048], P(('pool', 'expert')), may hold values from -0.21875 to 0.21875
Outputs:
- attended: bfloat16 [1024, 2048], P('pool', 'expert')
- expert_mix: bfloat16 [1024, 2048], P('pool', 'expert')
Inputs may be any that keep to these rules, and one draw needn't show every extreme that they name: Sequence t reads blocks of the pool of 32 blocks held with it: block (t // 32) * 32 + block_index[t, j] of kv_cache. The first lengths[t] of the sequence's 8 * 64 positions are live. `expert_ids`: each row names 8 different experts; within the 256 rows of one index of pool no expert is named by more than 128 rows.
All inputs are finite; a program needn't handle non-finite values.
Results may differ from a plain program's by a relative error of at most 0.01.
Values may be sent and summed in bfloat16 or wider, within the bound.
No kernel may reach another device: no remote copies, remote signals or barrier semaphores. Data moves between devices by JAX's collectives and lax.ppermute only.
A program may use at most 128 MiB of HBM per device.

v0:
```python
import jax
import jax.numpy as jnp
from jax import lax
from jax.sharding import PartitionSpec as P

HEAD_DIM = 128


epsilon = 1e-06


def shards(
    queries,
    kv_cache,
    block_index,
    lengths,
    residual,
    out_weight,
    norm_gain,
    expert_ids,
    route_weights,
    gate_weight,
    up_weight,
    down_weight,
):
    rows_dev = queries.shape[0]
    pool_blocks, block_len, kv_width = kv_cache.shape
    blocks_row = block_index.shape[1]
    context = blocks_row * block_len
    kv_half = kv_width // 2
    kv_heads = kv_half // HEAD_DIM
    head_count = queries.shape[1] // HEAD_DIM
    group_size = head_count // kv_heads
    step_rows = 4
    kv_flat = kv_cache.reshape(pool_blocks, block_len * kv_width)
    positions = jnp.arange(context, dtype=jnp.int32)
    block_ids = jnp.arange(pool_blocks, dtype=jnp.int32)

    def attend(inputs):
        query_rows, index_rows, length_rows = inputs
        selector = (index_rows.reshape(-1)[:, None] == block_ids[None, :]).astype(jnp.bfloat16)
        gathered = jnp.dot(selector, kv_flat, preferred_element_type=jnp.bfloat16)
        gathered = gathered.reshape(step_rows, context, kv_width)
        key_part = gathered[:, :, :kv_half].reshape(step_rows, context, kv_heads, HEAD_DIM)
        value_part = gathered[:, :, kv_half:].reshape(step_rows, context, kv_heads, HEAD_DIM)
        query_split = query_rows.reshape(step_rows, kv_heads, group_size, HEAD_DIM)
        scores = jnp.einsum(
            "rgqd,rpgd->rgqp", query_split, key_part, preferred_element_type=jnp.float32
        ) * HEAD_DIM ** (-0.5)
        live_mask = positions[None, :] < length_rows[:, None]
        scores = jnp.where(live_mask[:, None, None, :], scores, -1e30)
        maximum = jnp.max(scores, axis=-1, keepdims=True)
        exponent = jnp.exp(scores - maximum)
        softmax_w = (exponent / jnp.sum(exponent, axis=-1, keepdims=True)).astype(jnp.bfloat16)
        attended_part = jnp.einsum(
            "rgqp,rpgd->rgqd", softmax_w, value_part, preferred_element_type=jnp.float32
        )
        return attended_part.astype(jnp.bfloat16).reshape(step_rows, head_count * HEAD_DIM)

    attention = lax.map(
        attend,
        (
            queries.reshape(rows_dev // step_rows, step_rows, -1),
            block_index.reshape(rows_dev // step_rows, step_rows, blocks_row),
            lengths.reshape(rows_dev // step_rows, step_rows),
        ),
    )
    attention = attention.reshape(rows_dev, head_count * HEAD_DIM)
    expert_size = lax.axis_size("expert")
    col_width = out_weight.shape[1]
    full_width = col_width * expert_size
    projected = jnp.dot(
        lax.all_gather(attention, "expert", axis=0, tiled=True),
        out_weight,
        preferred_element_type=jnp.float32,
    )
    attended = (residual.astype(jnp.float32) + projected).astype(jnp.bfloat16)
    attended_f = attended.astype(jnp.float32)
    part_sq = jnp.sum(attended_f * attended_f, axis=1)
    square_sum = lax.psum(part_sq, "expert")
    inverse_rms = lax.rsqrt(square_sum / full_width + epsilon)
    normed = (attended_f * inverse_rms[:, None] * norm_gain[None, :]).astype(jnp.bfloat16)
    group_rows, top_count = expert_ids.shape
    pool_size = lax.axis_size("pool")
    device_count = pool_size * expert_size
    local_count = gate_weight.shape[0]
    hidden_width = gate_weight.shape[2]
    experts = device_count * local_count
    capacity = 2 * group_rows * top_count // experts
    flat_ids = expert_ids.reshape(-1)
    onehot = (flat_ids[:, None] == jnp.arange(experts, dtype=jnp.int32)[None, :]).astype(jnp.int32)
    before = jnp.cumsum(onehot, axis=0) - onehot
    slot_ids = jnp.sum(before * onehot, axis=1)
    owner_dev = flat_ids // local_count
    within = flat_ids % local_count
    destination = ((owner_dev * capacity + slot_ids) * local_count + within).reshape(
        group_rows, top_count
    )
    slot_span = experts * capacity
    slots_all = jnp.arange(slot_span, dtype=jnp.int32)
    chosen = jnp.zeros((group_rows, slot_span), jnp.bfloat16)
    for position in range(top_count):
        chosen = chosen + (destination[:, position : position + 1] == slots_all[None, :]).astype(
            jnp.bfloat16
        )
    outgoing = lax.dot_general(
        chosen, normed, (((0,), (0,)), ((), ())), preferred_element_type=jnp.bfloat16
    )
    gate_split = gate_weight.reshape(local_count, expert_size, col_width, hidden_width)
    up_split = up_weight.reshape(local_count, expert_size, col_width, hidden_width)
    down_split = down_weight.reshape(local_count, hidden_width, expert_size, col_width)
    received = lax.all_to_all(
        outgoing.reshape(device_count, capacity, local_count, col_width),
        ("pool", "expert"),
        split_axis=0,
        concat_axis=0,
        tiled=True,
    )
    item_count = received.shape[1]
    shaped = received.reshape(pool_size, expert_size, item_count, local_count, col_width)
    gate_act = jnp.einsum(
        "peixc,xecf->xpif", shaped, gate_split, preferred_element_type=jnp.float32
    )
    upper = jnp.einsum("peixc,xecf->xpif", shaped, up_split, preferred_element_type=jnp.float32)
    hidden = (jax.nn.silu(gate_act) * upper).astype(jnp.bfloat16)
    result = (
        jnp.einsum("xpif,xfec->peixc", hidden, down_split, preferred_element_type=jnp.float32)
        .astype(jnp.bfloat16)
        .reshape(device_count, item_count, local_count, col_width)
    )
    returned = lax.all_to_all(result, ("pool", "expert"), split_axis=0, concat_axis=0, tiled=True)
    returned_flat = returned.reshape(slot_span, col_width)
    picked = jnp.take(returned_flat, destination.reshape(-1), axis=0).reshape(
        group_rows, top_count, col_width
    )
    expert_mix = jnp.sum(picked.astype(jnp.float32) * route_weights[:, :, None], axis=1).astype(
        jnp.bfloat16
    )
    return (attended, expert_mix)


def solution(mesh):
    return jax.shard_map(
        shards,
        mesh=mesh,
        in_specs=(
            P(("pool", "expert"), None),
            P(("pool", "expert"), None, None),
            P(("pool", "expert"), None),
            P(("pool", "expert")),
            P("pool", "expert"),
            P(None, "expert"),
            P("expert"),
            P("pool", None),
            P("pool", None),
            P(("pool", "expert"), None, None),
            P(("pool", "expert"), None, None),
            P(("pool", "expert"), None, None),
        ),
        out_specs=(P("pool", "expert"), P("pool", "expert")),
        check_vma=False,
    )
```

profile of v0, /device:TPU:0, one launch (start us, length us, event | category | flops | bytes accessed | tf_op | source)
XLA Modules:
  0.0 456.7 jit_solution(13713309935924834919)
XLA Ops:
  10.7 6.5 %copy.91 = bf16[4,8,64,1024]{3,1,2,0:T(8,128)(2,1)} copy(bf16[4,8,64,1024]{3,2,1,0:T(8,128)(2,1)} %bitcast.146) | data formatting | bytes 8388608
  17.1 239.5 %while.11 = (s32[]{:T(128)}, bf16[8,4,4096]{2,1,0:T(4,128)(2,1)}, s32[8,4]{1,0:T(8,128)S(1)}, bf16[8,4,4096]{2,1,0:T(4,128)(2,1)}, s32[8,4,8]{2,1,0:T(4,128)S(1)}, /*index=5*/bf16[32,65536]{1,0:T(8,128)(2,1)}, s32[]{:T(128)}) while((s32[]{:T(128)}, bf16[8,4,4096]{2,1,0:T(4,128)(2,1)}, s32[8,4]{1,0:T(8,128)S(1)}, ...), condition=%wide.region_3.4_spmd.clone, body=%wide.region_0.3_spmd.clone.sunk | while | flops 168251520 | bytes 38803220 | solution.py:60
  17.2 5.5 %fusion.103 = bf16[32,65536]{1,0:T(8,128)(2,1)} fusion(bf16[32,65536]{1,0:T(8,128)(2,1)} %get-tuple-element.156, s32[32]{0:T(128)S(1)} %eq.380), kind=kOutput, calls=%fused_computation.15.clone.1 | convolution fusion | flops 134218752 | bytes 8388736 | tf_op jit(solution)/shard_map/while/body/eval_jaxpr/dot_general | solution.py:42
  22.7 5.6 %reshape.213 = bf16[4,512,1024]{2,1,0:T(8,128)(2,1)} reshape(bf16[32,65536]{1,0:T(8,128)(2,1)} %fusion.103) | data formatting | bytes 8388608 | tf_op jit(solution)/shard_map/while/body/eval_jaxpr/reshape | solution.py:43
  28.3 4.5 fusion.104
  32.8 4.1 copy.109
  36.9 4.2 copy.110
  44.1 2.3 convolution_convert_fusion.2
  47.2 5.4 %fusion.103 = bf16[32,65536]{1,0:T(8,128)(2,1)} fusion(bf16[32,65536]{1,0:T(8,128)(2,1)} %get-tuple-element.156, s32[32]{0:T(128)S(1)} %eq.380), kind=kOutput, calls=%fused_computation.15.clone.1 | convolution fusion | flops 134218752 | bytes 8388736 | tf_op jit(solution)/shard_map/while/body/eval_jaxpr/dot_general | solution.py:42
  52.6 5.6 %reshape.213 = bf16[4,512,1024]{2,1,0:T(8,128)(2,1)} reshape(bf16[32,65536]{1,0:T(8,128)(2,1)} %fusion.103) | data formatting | bytes 8388608 | tf_op jit(solution)/shard_map/while/body/eval_jaxpr/reshape | solution.py:43
  58.2 4.5 fusion.104
  62.7 4.1 copy.109
  66.8 4.2 copy.110
  74.1 2.3 convolution_convert_fusion.2
  77.1 5.5 %fusion.103 = bf16[32,65536]{1,0:T(8,128)(2,1)} fusion(bf16[32,65536]{1,0:T(8,128)(2,1)} %get-tuple-element.156, s32[32]{0:T(128)S(1)} %eq.380), kind=kOutput, calls=%fused_computation.15.clone.1 | convolution fusion | flops 134218752 | bytes 8388736 | tf_op jit(solution)/shard_map/while/body/eval_jaxpr/dot_general | solution.py:42
  82.6 5.6 %reshape.213 = bf16[4,512,1024]{2,1,0:T(8,128)(2,1)} reshape(bf16[32,65536]{1,0:T(8,128)(2,1)} %fusion.103) | data formatting | bytes 8388608 | tf_op jit(solution)/shard_map/while/body/eval_jaxpr/reshape | solution.py:43
  88.2 4.5 fusion.104
  92.6 4.1 copy.109
  96.8 4.2 copy.110
  104.0 2.3 convolution_convert_fusion.2
  107.0 5.4 %fusion.103 = bf16[32,65536]{1,0:T(8,128)(2,1)} fusion(bf16[32,65536]{1,0:T(8,128)(2,1)} %get-tuple-element.156, s32[32]{0:T(128)S(1)} %eq.380), kind=kOutput, calls=%fused_computation.15.clone.1 | convolution fusion | flops 134218752 | bytes 8388736 | tf_op jit(solution)/shard_map/while/body/eval_jaxpr/dot_general | solution.py:42
  112.5 5.6 %reshape.213 = bf16[4,512,1024]{2,1,0:T(8,128)(2,1)} reshape(bf16[32,65536]{1,0:T(8,128)(2,1)} %fusion.103) | data formatting | bytes 8388608 | tf_op jit(solution)/shard_map/while/body/eval_jaxpr/reshape | solution.py:43
  118.1 4.5 fusion.104
  122.6 4.1 copy.109
  126.7 4.2 copy.110
  133.9 2.3 convolution_convert_fusion.2
  137.0 5.5 %fusion.103 = bf16[32,65536]{1,0:T(8,128)(2,1)} fusion(bf16[32,65536]{1,0:T(8,128)(2,1)} %get-tuple-element.156, s32[32]{0:T(128)S(1)} %eq.380), kind=kOutput, calls=%fused_computation.15.clone.1 | convolution fusion | flops 134218752 | bytes 8388736 | tf_op jit(solution)/shard_map/while/body/eval_jaxpr/dot_general | solution.py:42
  142.4 5.6 %reshape.213 = bf16[4,512,1024]{2,1,0:T(8,128)(2,1)} reshape(bf16[32,65536]{1,0:T(8,128)(2,1)} %fusion.103) | data formatting | bytes 8388608 | tf_op jit(solution)/shard_map/while/body/eval_jaxpr/reshape | solution.py:43
  148.1 4.5 fusion.104
  152.5 4.1 copy.109
  156.7 4.2 copy.110
  163.9 2.3 convolution_convert_fusion.2
  166.9 5.5 %fusion.103 = bf16[32,65536]{1,0:T(8,128)(2,1)} fusion(bf16[32,65536]{1,0:T(8,128)(2,1)} %get-tuple-element.156, s32[32]{0:T(128)S(1)} %eq.380), kind=kOutput, calls=%fused_computation.15.clone.1 | convolution fusion | flops 134218752 | bytes 8388736 | tf_op jit(solution)/shard_map/while/body/eval_jaxpr/dot_general | solution.py:42
  172.4 5.6 %reshape.213 = bf16[4,512,1024]{2,1,0:T(8,128)(2,1)} reshape(bf16[32,65536]{1,0:T(8,128)(2,1)} %fusion.103) | data formatting | bytes 8388608 | tf_op jit(solution)/shard_map/while/body/eval_jaxpr/reshape | solution.py:43
  178.0 4.5 fusion.104
  182.5 4.1 copy.109
  186.6 4.2 copy.110
  193.8 2.3 convolution_convert_fusion.2
  196.9 5.5 %fusion.103 = bf16[32,65536]{1,0:T(8,128)(2,1)} fusion(bf16[32,65536]{1,0:T(8,128)(2,1)} %get-tuple-element.156, s32[32]{0:T(128)S(1)} %eq.380), kind=kOutput, calls=%fused_computation.15.clone.1 | convolution fusion | flops 134218752 | bytes 8388736 | tf_op jit(solution)/shard_map/while/body/eval_jaxpr/dot_general | solution.py:42
  202.3 5.6 %reshape.213 = bf16[4,512,1024]{2,1,0:T(8,128)(2,1)} reshape(bf16[32,65536]{1,0:T(8,128)(2,1)} %fusion.103) | data formatting | bytes 8388608 | tf_op jit(solution)/shard_map/while/body/eval_jaxpr/reshape | solution.py:43
  207.9 4.5 fusion.104
  212.4 4.1 copy.109
  216.6 4.2 copy.110
  223.8 2.3 convolution_convert_fusion.2
  226.8 5.5 %fusion.103 = bf16[32,65536]{1,0:T(8,128)(2,1)} fusion(bf16[32,65536]{1,0:T(8,128)(2,1)} %get-tuple-element.156, s32[32]{0:T(128)S(1)} %eq.380), kind=kOutput, calls=%fused_computation.15.clone.1 | convolution fusion | flops 134218752 | bytes 8388736 | tf_op jit(solution)/shard_map/while/body/eval_jaxpr/dot_general | solution.py:42
  232.3 5.6 %reshape.213 = bf16[4,512,1024]{2,1,0:T(8,128)(2,1)} reshape(bf16[32,65536]{1,0:T(8,128)(2,1)} %fusion.103) | data formatting | bytes 8388608 | tf_op jit(solution)/shard_map/while/body/eval_jaxpr/reshape | solution.py:43
  237.9 4.5 fusion.104
  242.4 4.1 copy.109
  246.5 4.2 copy.110
  253.7 2.3 convolution_convert_fusion.2
  261.1 15.9 %reduce-window.6 = s32[32,16,128]{2,1,0:T(8,128)S(1)} reduce-window(s32[32,16,128]{2,1,0:T(8,128)} %fusion.64, s32[]{:T(128)} %constant.76.clone.1), window={size=1x1x128 pad=0_0x0_0x127_0}, to_apply=%region_4.5 | reduce-window | flops 8323072 | bytes 524292 | tf_op jit(solution)/shard_map/reduce-window
  283.6 6.8 %all-gather.2.cloned.1.call-done = bf16[256,4096]{1,0:T(8,128)(2,1)} async-done(((bf16[32,4096]{1,0:T(8,128)(2,1)}), bf16[256,4096]{1,0:T(8,128)(2,1)}) %all-gather.2.cloned.1.call-update) | async-done | bytes 2097168 | tf_op jit(solution)/shard_map/all_gather | solution.py:73
  290.5 3.2 fusion.58
  293.6 15.5 %psum.7 = f32[256]{0:T(256)S(1)} all-reduce(f32[256]{0:T(256)S(1)} %get-tuple-element.94), channel_id=1, replica_groups=mesh['pool'=4,'expert'=8] {'expert'}, use_global_device_ids=true, to_apply=%region_8.9 | all-reduce | flops 256 | bytes 2048 | tf_op jit(solution)/shard_map/psum | solution.py:80
  309.2 6.0 %fusion.26 = bf16[4096,256]{1,0:T(8,128)(2,1)} fusion(s32[256]{0:T(256)S(1)} %bitcast.164, s32[256]{0:T(256)S(1)} %bitcast.163, s32[256]{0:T(256)S(1)} %bitcast.162, s32[256]{0:T(256)S(1)} %bitcast.158, s32[256]{0:T(256)S(1)} %bitcast.159, s32[256]{0:T(256)S(1)} %bitcast.160, s32[256]{0:T(256)S(1)} %bitcast.161, s32[256]{0:T(256)S(1)} %bitcast.157, ...), kind=kOutput, calls=%fused_computation.42 | convolution fusion | flops 570687488 | bytes 2238464 | tf_op jit(solution)/shard_map/dot_general | solution.py:106
  315.2 3.5 all-to-all-start
  318.7 4.6 %copy.93 = bf16[96,8,8,256]{3,2,1,0:T(8,128)(2,1)} copy(bf16[96,8,8,256]{3,1,2,0:T(8,128)(2,1)} %bitcast.147) | data formatting | bytes 6291456
  323.3 45.4 %all-to-all-done = bf16[32,128,1,256]{3,1,2,0:T(8,128)(2,1)} async-done(((bf16[32,128,1,256]{3,1,2,0:T(8,128)(2,1)}), bf16[32,128,1,256]{3,1,2,0:T(8,128)(2,1)}, u32[]{:S(2)}, u32[]{:S(2)}) %all-to-all-start) | async-done | bytes 2097184 | tf_op jit(solution)/shard_map/all_to_all | solution.py:112
  368.8 5.5 %fusion.74 = f32[4,128,768,1]{2,1,3,0:T(8,128)} fusion(bf16[4,8,128,256]{3,2,1,0:T(8,128)(2,1)} %bitcast.14, bf16[8,256,768,1]{2,1,0,3:T(8,128)(2,1)} %bitcast.165), kind=kOutput, calls=%fused_computation.96 | convolution fusion | flops 1610612736 | bytes 6815744 | tf_op jit(solution)/shard_map/peixc,xecf->xpif/dot_general | solution.py:121
  374.3 8.4 %fusion.49 = bf16[4,128,8,256]{3,1,2,0:T(8,128)(2,1)} fusion(bf16[768,8,256]{2,1,0:T(8,128)(2,1)} %bitcast.148, bf16[4,8,128,256]{3,2,1,0:T(8,128)(2,1)} %bitcast.14, bf16[8,256,768,1]{2,1,0,3:T(8,128)(2,1)S(1)} %bitcast.142, f32[4,128,768,1]{2,1,3,0:T(8,128)} %fusion.74), kind=kOutput, calls=%fused_computation.58 | convolution fusion | flops 3224633344 | bytes 12058624 | tf_op jit(solution)/shard_map/xpif,xfec->peixc/dot_general | solution.py:127
  382.7 3.6 all-to-all-start.1
  387.7 48.7 %all-to-all-done.1 = bf16[32,128,1,256]{3,1,2,0:T(8,128)(2,1)} async-done(((bf16[32,128,1,256]{3,1,2,0:T(8,128)(2,1)}), bf16[32,128,1,256]{3,1,2,0:T(8,128)(2,1)}, u32[]{:S(2)}, u32[]{:S(2)}) %all-to-all-start.1) | async-done | bytes 2097184 | tf_op jit(solution)/shard_map/all_to_all | solution.py:131
  436.4 10.3 %gather_fusion = bf16[2048,256]{1,0:T(8,128)(2,1)} fusion(bf16[4096,256]{1,0:T(8,128)(2,1)} %bitcast.31, s32[2048]{0:T(1024)S(1)} %broadcast_clamp_fusion), kind=kCustom, calls=%fused_computation | custom fusion | bytes 2105344 | tf_op jit(solution)/shard_map/jit(_take)/gather | solution.py:133
  446.7 3.2 multiply_reduce_fusion
  (112 shorter events, 46.0 us)
Async XLA Ops:
  7.2 367.1 %copy-start = (bf16[1,2048,768]{2,1,0:T(8,128)(2,1)S(1)}, bf16[1,2048,768]{2,1,0:T(8,128)(2,1)}, u32[]{:S(2)}) copy-start(bf16[1,2048,768]{2,1,0:T(8,128)(2,1)} %param.24) | copy-start | bytes 9437188
  7.2 283.3 %all-gather.2.cloned.1.call-start = ((), (), s32[]{:S(2)}) async-start(), calls=%async_computation.2 | async-start | bytes 2359296 | tf_op jit(solution)/shard_map/all_gather | solution.py:73
  17.1 241.3 %copy-start.1 = (s32[256,8]{0,1:T(8,128)S(1)}, s32[256,8]{0,1:T(8,128)}, u32[]{:S(2)}) copy-start(s32[256,8]{0,1:T(8,128)} %param.21) | copy-start | bytes 24580
  283.6 25.5 %copy-start.4 = (f32[256]{0:T(256)S(1)}, f32[256]{0:T(256)}, u32[]{:S(2)}) copy-start(f32[256]{0:T(256)} %param.20) | copy-start | bytes 3076
  315.2 53.6 %all-to-all-start = ((bf16[32,128,1,256]{3,1,2,0:T(8,128)(2,1)}), bf16[32,128,1,256]{3,1,2,0:T(8,128)(2,1)}, u32[]{:S(2)}, u32[]{:S(2)}) async-start(bf16[32,128,1,256]{3,1,2,0:T(8,128)(2,1)} %bitcast.150), calls=%async_computation | async-start | bytes 4194304 | tf_op jit(solution)/shard_map/all_to_all | solution.py:112
  382.7 3.9 copy-start.2
  382.7 4.0 copy-start.3
  382.7 53.7 %all-to-all-start.1 = ((bf16[32,128,1,256]{3,1,2,0:T(8,128)(2,1)}), bf16[32,128,1,256]{3,1,2,0:T(8,128)(2,1)}, u32[]{:S(2)}, u32[]{:S(2)}) async-start(bf16[32,128,1,256]{3,1,2,0:T(8,128)(2,1)} %bitcast.149), calls=%async_computation.1 | async-start | bytes 4194304 | tf_op jit(solution)/shard_map/all_to_all | solution.py:131
Sparse Core Ops, SparseCore 0:
  258.5 31.8 all-gather.1
where the time goes:
time: 461 us; the launch traced here: 457 us
  local copies, waits for them, and re-layouts  192 us (42%)
  matrix products  101 us (22%)
  waiting for transfers between devices  101 us (22%)
  other arithmetic  25.9 us (6%)
  blocking collectives  15.5 us (3%)
  between operations  14.2 us (3%)
  starting transfers between devices  7.12 us (2%)
    while x24, local copies, waits for them, and re-layouts  72.6 us
    all_to_all x1, waiting for transfers between devices, shards(): lax.all_to_all(result, ('pool', 'expert'), split_axis=0, concat_axis=0, t...  48.7 us
    all_to_all x1, waiting for transfers between devices, shards(): lax.all_to_all(outgoing.reshape(device_count, capacity, local_count, col_...  45.4 us
    reshape x8, local copies, waits for them, and re-layouts, attend(): gathered = gathered.reshape(step_rows, context, kv_width)  45 us
    dot_general x8, matrix products, attend(): gathered = jnp.dot(selector, kv_flat, preferred_element_type=jnp.bfloat16)  43.7 us
    slice x8, local copies, waits for them, and re-layouts, attend(): gathered[:, :, :kv_half].reshape(step_rows, context, kv_heads, HEAD_DIM)  35.7 us
    dot_general x8, matrix products, attend(): jnp.einsum('rgqp,rpgd->rgqd', softmax_w, value_part, preferred_element_ty...  18.3 us
    another operation x3, other arithmetic  18.3 us
  transfers between devices with their start and end apart: 3, of which 3 were waited for; matrix products, arithmetic and copies ran while one was open for 7% of the time, Pallas kernels for 0%

commit v1 on v0

v1 whole, which is shorter than its diff:
```python
import functools
import math

import jax
import jax.numpy as jnp
from jax import lax
from jax.experimental import pallas as pl
from jax.experimental.pallas import tpu as pltpu
from jax.sharding import PartitionSpec as P

HEAD_DIM = 128
CORES = 2
MASKED = -1e30
GAIN_COLUMNS = 128
TURN_ROWS = 16
ID_COLUMNS = 128
LARGE_VMEM = 60 * 2**20
SMALL_VMEM = 24 * 2**20
FETCH_VMEM = 46 * 2**20

epsilon = 1e-06


def prepare(residual_ref, gain_ref, out_ref, columns_ref):
    member = lax.axis_index("expert")
    core = member - member // CORES * CORES
    line = lax.axis_size("expert") // CORES
    rows = out_ref.shape[0] // line
    for z in range(line):
        at = pl.ds(pl.multiple_of((z * CORES + 1 - core) * rows, rows), rows)
        out_ref[z * rows : (z + 1) * rows, :] = residual_ref[at, :]
    lines = [
        term[:, at : at + GAIN_COLUMNS]
        for term in three_terms(gain_ref[...])
        for at in range(0, gain_ref.shape[1], GAIN_COLUMNS)
    ]
    lines.append(jnp.zeros((columns_ref.shape[0] - len(lines), GAIN_COLUMNS), jnp.float32))
    columns_ref[...] = jnp.concatenate(lines, axis=0).astype(jnp.bfloat16)


def attend_kernel(index_ref, length_ref, query_ref, kv_hbm, *refs, block_len, first, prepares):
    if prepares:
        residual_ref, gain_ref, out_ref, extra_ref, bias_ref, key_ref, value_ref, sems = refs
    else:
        out_ref, bias_ref, key_ref, value_ref, sems = refs
    blocks_row, rows = index_ref.shape
    positions, width = key_ref.shape
    heads = width // HEAD_DIM
    kv_half = kv_hbm.shape[1] // 2
    group_size = query_ref.shape[1] // heads // HEAD_DIM
    scale = HEAD_DIM ** (-0.5)
    base2 = scale * math.log2(math.e)
    pieces = sems.shape[1]
    copies = []
    for kind, (start, target) in enumerate(((0, key_ref), (kv_half, value_ref))):
        columns = pl.ds(start + first * HEAD_DIM, width)
        for piece in range(pieces):
            at = pl.ds(piece * (positions // pieces), positions // pieces)
            copies.append(
                pltpu.make_async_copy(
                    kv_hbm.at[at, columns], target.at[at, :], sems.at[kind, piece]
                )
            )
    for copy in copies[:pieces]:
        copy.start()
    if prepares:
        columns_ref = out_ref.at[:, pl.ds(query_ref.shape[1], GAIN_COLUMNS)]
        prepare(residual_ref, gain_ref, extra_ref, columns_ref)

    length = length_ref[...].astype(jnp.float32)
    high = jnp.floor(length * (1.0 / 16)) * 16.0
    pad = jnp.zeros((TURN_ROWS - blocks_row - 2, rows), jnp.float32)
    table = jnp.concatenate(
        [
            index_ref[...].astype(jnp.float32),
            high,
            length - high,
            pad,
        ],
        axis=0,
    ).astype(jnp.bfloat16)
    same = lax.broadcasted_iota(jnp.int32, (rows, rows), 0) == lax.broadcasted_iota(
        jnp.int32, (rows, rows), 1
    )
    table = lax.dot_general(
        same.astype(jnp.float32).astype(jnp.bfloat16),
        table,
        (((1,), (1,)), ((), ())),
        preferred_element_type=jnp.float32,
    )
    limit = table[:, blocks_row : blocks_row + 1] + table[:, blocks_row + 1 : blocks_row + 2]
    place = lax.broadcasted_iota(jnp.int32, (rows, positions), 1).astype(jnp.float32)
    block = jnp.floor((place + 0.5) * (1.0 / block_len))
    offset = place - block * block_len
    count = jnp.zeros((rows, positions), jnp.float32)
    for j in range(blocks_row):
        live = (table[:, j : j + 1] == block) & (offset < limit - j * block_len)
        count = count + jnp.where(live, 1.0, 0.0)
    bias_ref[...] = jnp.where(
        count > 0.0, jnp.log(jnp.maximum(count, 1.0)) * (1.0 / scale), MASKED
    )

    for g in range(heads):
        columns = [
            slice((g * group_size + h) * HEAD_DIM, (g * group_size + h + 1) * HEAD_DIM)
            for h in range(group_size)
        ]
        head = slice(g * HEAD_DIM, (g + 1) * HEAD_DIM)
        query = jnp.concatenate([query_ref[:, at] for at in columns], axis=0)
        if g == 0:
            for copy in copies[:pieces]:
                copy.wait()
            for copy in copies[pieces:]:
                copy.start()
        scores = lax.dot_general(
            query, key_ref[:, head], (((1,), (1,)), ((), ())), preferred_element_type=jnp.float32
        )
        scores = scores.reshape(group_size, rows, positions) + bias_ref[...][None]
        maximum = jnp.max(scores, axis=-1, keepdims=True)
        exponent = jnp.exp2((scores - maximum) * base2)
        total = jnp.sum(exponent, axis=-1, keepdims=True)
        weights = exponent.astype(jnp.bfloat16).reshape(group_size * rows, positions)
        if g == 0:
            for copy in copies[pieces:]:
                copy.wait()
        mixed = jnp.dot(weights, value_ref[:, head], preferred_element_type=jnp.float32)
        mixed = mixed.reshape(group_size, rows, HEAD_DIM) / total
        for h, at in enumerate(columns):
            out_ref[:, at] = mixed[h].astype(jnp.bfloat16)


def attend(queries, kv_cache, block_index, lengths, part, parts, prepared=None):
    rows = queries.shape[0]
    pool_blocks, block_len, kv_width = kv_cache.shape
    positions = pool_blocks * block_len
    kv_heads = kv_width // 2 // HEAD_DIM
    width = queries.shape[1] // kv_heads
    kv_flat = kv_cache.reshape(positions, kv_width)
    heads = kv_heads // parts
    first = part * heads
    operands = []
    columns = 0 if prepared is None else GAIN_COLUMNS
    out_shape = [pltpu.VMEM((rows, heads * width + columns), jnp.bfloat16)]
    if prepared is not None:
        residual, gain = prepared
        operands = [residual, gain.reshape(1, -1)]
        extra = (residual.shape[0] // CORES, residual.shape[1])
        out_shape.append(pltpu.VMEM(extra, jnp.bfloat16))
    return pl.pallas_call(
        functools.partial(
            attend_kernel, block_len=block_len, first=first, prepares=prepared is not None
        ),
        grid=(1,),
        in_specs=[
            pl.BlockSpec((block_index.shape[1], rows), lambda g: (0, 0)),
            pl.BlockSpec((1, rows), lambda g: (0, 0)),
            pl.BlockSpec((rows, heads * width), lambda g: (0, part)),
            pl.BlockSpec(memory_space=pl.ANY),
        ]
        + [pl.BlockSpec(operand.shape, lambda g: (0, 0)) for operand in operands],
        out_specs=[pl.BlockSpec(shape.shape, lambda g: (0, 0)) for shape in out_shape],
        out_shape=out_shape,
        scratch_shapes=[
            pltpu.VMEM((rows, positions), jnp.float32),
            pltpu.VMEM((positions, heads * HEAD_DIM), jnp.bfloat16),
            pltpu.VMEM((positions, heads * HEAD_DIM), jnp.bfloat16),
            pltpu.SemaphoreType.DMA((2, 2)),
        ],
        compiler_params=pltpu.CompilerParams(vmem_limit_bytes=LARGE_VMEM),
        name="attend",
    )(block_index.T, lengths.reshape(1, rows), queries, kv_flat, *operands)


def fetch_kernel(*refs, count):
    sems = refs[2 * count]
    copies = [
        pltpu.make_async_copy(refs[i], refs[count + i], sems.at[i]) for i in range(count)
    ]
    for copy in copies:
        copy.start()
    for copy in copies:
        copy.wait()


def fetch(*arrays):
    count = len(arrays)
    return pl.pallas_call(
        functools.partial(fetch_kernel, count=count),
        in_specs=[pl.BlockSpec(memory_space=pltpu.HBM)] * count,
        out_specs=[pl.BlockSpec(memory_space=pltpu.VMEM)] * count,
        out_shape=[pltpu.VMEM(array.shape, array.dtype) for array in arrays],
        scratch_shapes=[pltpu.SemaphoreType.DMA((count,))],
        compiler_params=pltpu.CompilerParams(vmem_limit_bytes=FETCH_VMEM),
        cost_estimate=pl.CostEstimate(
            flops=0, transcendentals=0, bytes_accessed=2 * sum(a.size * 2 for a in arrays)
        ),
        name="fetch",
    )(*arrays)


def project_kernel(*refs, line, parts):
    blocks = refs[: line * parts]
    (
        weight_ref,
        other_weight_ref,
        residual_ref,
        extra_ref,
        message_ref,
        mine_ref,
        give_ref,
    ) = refs[line * parts :]
    rows = blocks[0].shape[0]
    core_rows = line * rows
    width = weight_ref.shape[1]
    member = lax.axis_index("expert")
    layer = member // CORES
    core = member - layer * CORES
    depth = blocks[-1].shape[1]
    product = other_product = 0.0
    for part in range(parts):
        gathered = [ref[:, :depth] for ref in blocks[part * line : (part + 1) * line]]
        gathered = jnp.concatenate(gathered, axis=0)
        at = slice(part * depth, (part + 1) * depth)
        product += jnp.dot(gathered, weight_ref[at, :], preferred_element_type=jnp.float32)
        other_product += jnp.dot(
            gathered, other_weight_ref[at, :], preferred_element_type=jnp.float32
        )
    here = pl.ds(pl.multiple_of(core * width, width), width)
    there = pl.ds(pl.multiple_of((1 - core) * width, width), width)
    for k in range(line):
        z = layer - k
        z = jnp.where(z < 0, z + line, z)
        at = pl.ds(pl.multiple_of(z * rows, rows), rows)
        held = pl.ds(pl.multiple_of((z * CORES + core) * rows, rows), rows)
        arrived = slice(k * rows, (k + 1) * rows)
        mine = residual_ref[held, :].astype(jnp.float32) + product[arrived, :]
        mine = mine.astype(jnp.bfloat16)
        mine_ref[at, :] = mine
        message_ref[at, here] = mine
        other = extra_ref[at, :].astype(jnp.float32) + other_product[arrived, :]
        other = other.astype(jnp.bfloat16)
        give_ref[at, :] = other
        message_ref[at, there] = other
    gains = []
    pieces = width // GAIN_COLUMNS
    for k in range(line):
        lines = blocks[k][:16, depth:].astype(jnp.float32)
        for term in range(3):
            gains.append(
                jnp.concatenate(
                    [lines[term * pieces + p : term * pieces + p + 1] for p in range(pieces)], axis=1
                )
            )
    gains.append(jnp.zeros((give_ref.shape[0] - core_rows - len(gains), width), jnp.float32))
    give_ref[core_rows:, :] = jnp.concatenate(gains, axis=0).astype(jnp.bfloat16)


def project(blocks, weight, other_weight, residual, extra, parts):
    line = len(blocks) // parts
    core_rows = blocks[0].shape[0] * line
    width = weight.shape[1]
    vmem = pl.BlockSpec(memory_space=pltpu.VMEM)
    return pl.pallas_call(
        functools.partial(project_kernel, line=line, parts=parts),
        in_specs=[vmem] * (line * parts + 4),
        out_specs=[vmem] * 3,
        out_shape=[
            jax.ShapeDtypeStruct((core_rows, CORES * width), jnp.bfloat16),
            jax.ShapeDtypeStruct((core_rows, width), jnp.bfloat16),
            jax.ShapeDtypeStruct((core_rows + pl.cdiv(3 * line, 16) * 16, width), jnp.bfloat16),
        ],
        compiler_params=pltpu.CompilerParams(vmem_limit_bytes=SMALL_VMEM),
        name="project",
    )(*blocks, weight, other_weight, residual, extra)


def three_terms(value):
    terms = []
    for _ in range(3):
        terms.append(value.astype(jnp.bfloat16).astype(jnp.float32))
        value = value - terms[-1]
    return terms


def lines_kernel(ids_ref, route_ref, out_ref, *chosen, line):
    core_rows = out_ref.shape[0]
    top_count, group_rows = ids_ref.shape
    rows = group_rows // (line * CORES)
    lines = []
    terms = [ids_ref[...].astype(jnp.float32), *three_terms(route_ref[...])]
    for value in terms:
        value = jnp.concatenate(
            [
                value[:, (z * CORES + c) * rows : (z * CORES + c + 1) * rows]
                for c in range(CORES)
                for z in range(line)
            ],
            axis=1,
        )
        lines += [value[:, at : at + ID_COLUMNS] for at in range(0, group_rows, ID_COLUMNS)]
    used = top_count * len(lines)
    if used < core_rows:
        lines.append(jnp.zeros((core_rows - used, ID_COLUMNS), jnp.float32))
    out_ref[...] = jnp.concatenate(lines, axis=0).astype(jnp.bfloat16)
    pool = lax.axis_index("pool")
    member = lax.axis_index("expert")
    core = member - member // CORES * CORES
    owners = []
    for j in range(len(chosen)):
        step = pair_step(lax.axis_size("pool"), j, core)
        owners.append((pool ^ step) * lax.axis_size("expert") + member)
    for ref, matrix in zip(chosen, plan(terms, owners, chosen[0].shape[1], line)):
        ref[...] = matrix


def routing_lines(ids, route_weights, line, near_count, capacity):
    vmem = pl.BlockSpec(memory_space=pltpu.VMEM)
    return pl.pallas_call(
        functools.partial(lines_kernel, line=line),
        in_specs=[vmem] * 2,
        out_specs=[vmem] * (1 + near_count),
        out_shape=[jax.ShapeDtypeStruct((ids.shape[1] // CORES, ID_COLUMNS), jnp.bfloat16)]
        + [jax.ShapeDtypeStruct((ids.shape[1], capacity), jnp.bfloat16)] * near_count,
        compiler_params=pltpu.CompilerParams(vmem_limit_bytes=SMALL_VMEM),
        name="lines",
    )(ids, route_weights)


def normalize_kernel(lines_ref, give_ref, taken_ref, *refs):
    blocks = refs[:-1]
    out_ref = refs[-1]
    line = len(blocks)
    width = blocks[0].shape[1]
    core_rows = out_ref.shape[0]
    features = line * width
    member = lax.axis_index("expert")
    layer = member // CORES
    core = member - layer * CORES
    gains = [ref[core_rows:, :].astype(jnp.float32) for ref in (give_ref, taken_ref)]
    squares = jnp.zeros((core_rows, 1), jnp.float32)
    for block in blocks:
        attended = block[...].astype(jnp.float32)
        squares = squares + jnp.sum(attended * attended, axis=1, keepdims=True)
    inverse = lax.rsqrt(squares / features + epsilon)
    for k, block in enumerate(blocks):
        z = layer - k
        z = jnp.where(z < 0, z + line, z)
        at = pl.ds(pl.multiple_of(z * width, width), width)
        attended = block[...].astype(jnp.float32)
        mine, other = [jnp.sum(gain[3 * k : 3 * k + 3], axis=0, keepdims=True) for gain in gains]
        gain = jnp.where(
            core == 0,
            jnp.concatenate([mine, other], axis=1),
            jnp.concatenate([other, mine], axis=1),
        )
        out_ref[:, at] = (attended * inverse * gain).astype(jnp.bfloat16)

    out_ref[:, features:] = lines_ref[...]


def assemble_kernel(mine_ref, taken_ref, out_ref, *, line):
    rows = mine_ref.shape[0] // line
    member = lax.axis_index("expert")
    core = member - member // CORES * CORES
    for z in range(line):
        at = slice(z * rows, (z + 1) * rows)
        here = pl.ds(pl.multiple_of((z * CORES + core) * rows, rows), rows)
        there = pl.ds(pl.multiple_of((z * CORES + 1 - core) * rows, rows), rows)
        out_ref[here, :] = mine_ref[at, :]
        out_ref[there, :] = taken_ref[at, :]


def assemble(mine, taken, line):
    vmem = pl.BlockSpec(memory_space=pltpu.VMEM)
    return pl.pallas_call(
        functools.partial(assemble_kernel, line=line),
        in_specs=[vmem] * 2,
        out_specs=vmem,
        out_shape=jax.ShapeDtypeStruct((CORES * mine.shape[0], mine.shape[1]), mine.dtype),
        compiler_params=pltpu.CompilerParams(vmem_limit_bytes=SMALL_VMEM),
        name="assemble",
    )(mine, taken)


def normalize(blocks, lines, give, taken):
    rows, width = blocks[0].shape
    features = len(blocks) * width
    vmem = pl.BlockSpec(memory_space=pltpu.VMEM)
    return pl.pallas_call(
        normalize_kernel,
        in_specs=[vmem] * (len(blocks) + 3),
        out_specs=vmem,
        out_shape=jax.ShapeDtypeStruct((rows, features + ID_COLUMNS), jnp.bfloat16),
        compiler_params=pltpu.CompilerParams(vmem_limit_bytes=SMALL_VMEM),
        name="normalize",
    )(lines, give, taken, *blocks)


def routing(rows_ref, features, top_count, kinds):
    group_rows = CORES * rows_ref.shape[0]
    pieces = group_rows // ID_COLUMNS
    lines = rows_ref[: kinds * top_count * pieces, features:].astype(jnp.float32)
    found = []
    for kind in range(kinds):
        first = kind * pieces * top_count
        found.append(
            jnp.concatenate(
                [lines[first + p * top_count : first + (p + 1) * top_count] for p in range(pieces)],
                axis=1,
            )
        )
    return found


def expert_kernel(*refs, count, top_count, line, parts):
    inputs = [(refs[2 * i], refs[2 * i + 1]) for i in range(count)]
    gate_ref, up_ref, down_ref = refs[2 * count : 2 * count + 3]
    outs = refs[2 * count + 3 :]
    capacity = outs[0].shape[0]
    features = gate_ref.shape[1]
    width = features // (CORES * line)
    pool = lax.axis_index("pool")
    member = lax.axis_index("expert")
    layer = member // CORES
    core = member - layer * CORES
    owner = (pool * lax.axis_size("expert") + member).astype(jnp.float32)

    half = inputs[0][0].shape[0]
    group_rows = CORES * half
    before = (
        lax.broadcasted_iota(jnp.int32, (group_rows, group_rows), 0)
        < lax.broadcasted_iota(jnp.int32, (group_rows, group_rows), 1)
    ).astype(jnp.bfloat16)
    slots = lax.broadcasted_iota(jnp.int32, (capacity, group_rows), 0)
    rows = []
    for mine_ref, other_ref in inputs:
        (ids,) = routing(mine_ref, features, top_count, 1)
        routed = jnp.max((ids == owner).astype(jnp.float32), axis=0, keepdims=True)
        mask = jnp.broadcast_to(routed, (16, group_rows)).astype(jnp.bfloat16)
        slot = jnp.dot(mask, before, preferred_element_type=jnp.float32)[0:1, :]
        slot = jnp.where(routed > 0.0, slot, -1.0).astype(jnp.int32)
        chosen = (slot == slots).astype(jnp.float32)
        first, second = chosen[:, :half], chosen[:, half:]
        mine = jnp.where(core == 0, first, second).astype(jnp.bfloat16)
        other = jnp.where(core == 0, second, first).astype(jnp.bfloat16)
        picked = jnp.dot(mine, mine_ref[:, :features], preferred_element_type=jnp.float32)
        picked += jnp.dot(other, other_ref[:, :features], preferred_element_type=jnp.float32)
        rows.append(picked.astype(jnp.bfloat16))
    rows = rows[0] if count == 1 else jnp.concatenate(rows, axis=0)
    gate = jnp.dot(rows, gate_ref[0], preferred_element_type=jnp.float32)
    upper = jnp.dot(rows, up_ref[0], preferred_element_type=jnp.float32)
    hidden = (gate / (1.0 + jnp.exp(-gate)) * upper).astype(jnp.bfloat16)
    for part, ahead in enumerate(parts):
        for b, k in enumerate(ahead):
            z = layer + k
            z = jnp.where(z >= line, z - line, z)
            for c in range(CORES):
                place = z * CORES + (core if c == 0 else 1 - core)
                at = pl.ds(pl.multiple_of(place * width, width), width)
                to = slice((b * CORES + c) * width, (b * CORES + c + 1) * width)
                result = jnp.dot(hidden, down_ref[0, :, at], preferred_element_type=jnp.float32)
                result = result.astype(jnp.bfloat16)
                for i in range(count):
                    outs[len(parts) * i + part][:, to] = result[i * capacity : (i + 1) * capacity]


def run_expert(inputs, weights, capacity, top_count, line, parts):
    count = len(inputs)
    operands = [rows for pair in inputs for rows in pair]
    _, features, hidden_width = weights[0].shape
    vmem = pl.BlockSpec(memory_space=pltpu.VMEM)
    outs = pl.pallas_call(
        functools.partial(
            expert_kernel, count=count, top_count=top_count, line=line, parts=parts
        ),
        in_specs=[vmem] * (len(operands) + 3),
        out_specs=[vmem] * (len(parts) * count),
        out_shape=[
            jax.ShapeDtypeStruct((capacity, features // line * len(ahead)), jnp.bfloat16)
            for _ in range(count)
            for ahead in parts
        ],
        compiler_params=pltpu.CompilerParams(vmem_limit_bytes=SMALL_VMEM),
        cost_estimate=pl.CostEstimate(
            flops=6 * count * capacity * features * hidden_width,
            bytes_accessed=6 * features * hidden_width + 8 * count * capacity * features,
            transcendentals=count * capacity * hidden_width,
        ),
        name="expert",
    )(*operands, *weights)
    return [outs[len(parts) * i : len(parts) * (i + 1)] for i in range(count)]


def pair_step(pool_size, j, core):
    if pool_size == 4 and j in (1, 2):
        return jnp.where(core == 0, j, 3 - j)
    return j


def combine_kernel(*refs, line, near_count, far_count):
    mine, other = refs[-2:]
    near = refs[:near_count]
    chosen = [ref[...] for ref in refs[near_count : 2 * near_count]]
    combine_part(near, chosen, mine, other, 0, line, line)
    far = refs[2 * near_count : 2 * near_count + far_count]
    chosen = [ref[...] for ref in refs[2 * near_count + far_count : -2]]
    combine_part(far, chosen, mine, other, line, 1, line)


def plan_kernel(rows_ref, *outs, features, top_count, line):
    terms = routing(rows_ref, features, top_count, 4)
    pool = lax.axis_index("pool")
    member = lax.axis_index("expert")
    layer = member // CORES
    core = member - layer * CORES
    owners = []
    for k in range(line):
        z = layer - k
        z = jnp.where(z < 0, z + line, z)
        owners.append(pool * lax.axis_size("expert") + z * CORES + core)
    for ref, matrix in zip(outs, plan(terms, owners, outs[0].shape[1], None)):
        ref[...] = matrix


def plan_far(rows, features, top_count, line, capacity):
    vmem = pl.BlockSpec(memory_space=pltpu.VMEM)
    shape = (CORES * rows.shape[0], capacity)
    return pl.pallas_call(
        functools.partial(plan_kernel, features=features, top_count=top_count, line=line),
        in_specs=[vmem],
        out_specs=[vmem] * line,
        out_shape=[jax.ShapeDtypeStruct(shape, jnp.bfloat16)] * line,
        compiler_params=pltpu.CompilerParams(vmem_limit_bytes=SMALL_VMEM),
        name="plan",
    )(rows)


def plan(terms, owners, capacity, line):
    top_count, group_rows = terms[0].shape
    row = lax.broadcasted_iota(jnp.int32, (group_rows, group_rows), 0)
    column = lax.broadcasted_iota(jnp.int32, (group_rows, group_rows), 1)
    source = row
    if line is not None:
        rows = group_rows // (CORES * line)
        place = row.astype(jnp.float32)
        c = jnp.floor((place + 0.5) * (1.0 / (line * rows)))
        z = jnp.floor((place - c * (line * rows) + 0.5) * (1.0 / rows))
        source = (place + (z * CORES + c - c * line - z) * rows).astype(jnp.int32)
    table = jnp.concatenate(terms, axis=0).astype(jnp.bfloat16)
    order = (column == source).astype(jnp.float32).astype(jnp.bfloat16)
    table = lax.dot_general(
        order, table, (((1,), (1,)), ((), ())), preferred_element_type=jnp.float32
    )
    ids = table[:, :top_count]
    route = table[:, top_count : 2 * top_count]
    for k in (2, 3):
        route = route + table[:, k * top_count : (k + 1) * top_count]
    before = (column < row).astype(jnp.float32).astype(jnp.bfloat16)
    slots = lax.broadcasted_iota(jnp.int32, (group_rows, capacity), 1)
    chosen = []
    for owner in owners:
        named = ids == owner.astype(jnp.float32)
        share = jnp.sum(jnp.where(named, route, 0.0), axis=1, keepdims=True)
        routed = jnp.max(named.astype(jnp.float32), axis=1, keepdims=True)
        mask = jnp.broadcast_to(routed, (group_rows, capacity))
        slot = jnp.dot(before, mask.astype(jnp.bfloat16), preferred_element_type=jnp.float32)
        slot = jnp.where(mask > 0.0, slot, -1.0).astype(jnp.int32)
        chosen.append(jnp.where(slot == slots, share, 0.0).astype(jnp.bfloat16))
    return chosen


def combine_part(inputs, chosen, mine, other, first, steps, line):
    capacity = inputs[0].shape[0]
    _, group_rows, width = mine.shape
    rows = group_rows // (CORES * line)
    whole_lanes = capacity % 128 == 0
    if whole_lanes:
        chosen = [jnp.concatenate(chosen, axis=1)]
    for b in range(CORES * steps):
        at = slice(b * width, (b + 1) * width)
        results = [ref[:, at] for ref in inputs]
        if whole_lanes:
            results = [jnp.concatenate(results, axis=0)]
        total = sum(
            jnp.dot(matrix, result, preferred_element_type=jnp.float32)
            for matrix, result in zip(chosen, results)
        )
        total = total.astype(jnp.bfloat16)
        for z in range(line):
            for c in range(CORES):
                source = slice((c * line + z) * rows, (c * line + z + 1) * rows)
                to = slice((z * CORES + c) * rows, (z * CORES + c + 1) * rows)
                (mine if b % CORES == 0 else other)[first + b // CORES, to, :] = total[source]


def combine(near, chosen, far, far_chosen, line):
    operands = [*near, *chosen, *far, *far_chosen]
    group_rows = chosen[0].shape[0]
    shape = (line + 1, group_rows, near[0].shape[1] // (CORES * line))
    vmem = pl.BlockSpec(memory_space=pltpu.VMEM)
    return pl.pallas_call(
        functools.partial(
            combine_kernel,
            line=line,
            near_count=len(near),
            far_count=len(far),
        ),
        in_specs=[vmem] * len(operands),
        out_specs=[vmem] * 2,
        out_shape=[jax.ShapeDtypeStruct(shape, jnp.bfloat16)] * 2,
        compiler_params=pltpu.CompilerParams(vmem_limit_bytes=FETCH_VMEM),
        cost_estimate=pl.CostEstimate(
            flops=2 * group_rows * sum(rows.size for rows in near + far),
            bytes_accessed=2 * sum(rows.size for rows in near + far),
            transcendentals=0,
        ),
        name="combine",
    )(*operands)


def add_kernel(mine_ref, other_ref, *outs):
    for k, out in enumerate(outs):
        total = mine_ref[k].astype(jnp.float32) + other_ref[k].astype(jnp.float32)
        out[...] = total.astype(jnp.bfloat16)


def add(mine, other):
    steps, group_rows, width = mine.shape
    vmem = pl.BlockSpec(memory_space=pltpu.VMEM)
    return pl.pallas_call(
        add_kernel,
        in_specs=[vmem] * 2,
        out_specs=[vmem] * steps,
        out_shape=[jax.ShapeDtypeStruct((group_rows, width), jnp.bfloat16)] * steps,
        compiler_params=pltpu.CompilerParams(vmem_limit_bytes=SMALL_VMEM),
        cost_estimate=pl.CostEstimate(
            flops=mine.size, bytes_accessed=6 * mine.size, transcendentals=0
        ),
        name="add",
    )(mine, other)


def finish_kernel(*refs):
    total = refs[0][...].astype(jnp.float32)
    for ref in refs[1:-1]:
        total = total + ref[...].astype(jnp.float32)
    refs[-1][...] = total.astype(jnp.bfloat16)


def finish(parts):
    vmem = pl.BlockSpec(memory_space=pltpu.VMEM)
    return pl.pallas_call(
        finish_kernel,
        in_specs=[vmem] * len(parts),
        out_specs=vmem,
        out_shape=jax.ShapeDtypeStruct(parts[0].shape, jnp.bfloat16),
        compiler_params=pltpu.CompilerParams(vmem_limit_bytes=SMALL_VMEM),
        name="finish",
    )(*parts)


def shards(
    queries,
    kv_cache,
    block_index,
    lengths,
    residual,
    out_weight,
    norm_gain,
    expert_ids,
    route_weights,
    gate_weight,
    up_weight,
    down_weight,
    *,
    pool_size,
    expert_size,
):
    line = expert_size // CORES
    core = lax.axis_index("expert") % CORES
    group_rows, top_count = expert_ids.shape
    experts = pool_size * expert_size * gate_weight.shape[0]
    capacity = 2 * group_rows * top_count // experts
    rows = queries.shape[0]
    width = out_weight.shape[1]

    def turn(value, k):
        pairs = [
            (z * CORES + c, (z + k) % line * CORES + c) for z in range(line) for c in range(CORES)
        ]
        return lax.ppermute(value, "expert", pairs)

    def across_cores(value):
        return lax.ppermute(value, "expert", [(e, e ^ 1) for e in range(expert_size)])

    def across_pool(value, j):
        pairs = []
        for p in range(pool_size):
            for e in range(expert_size):
                step = j
                if pool_size == 4 and j in (1, 2):
                    step = j if e % CORES == 0 else 3 - j
                pairs.append((p * expert_size + e, (p ^ step) * expert_size + e))
        return lax.ppermute(value, ("pool", "expert"), pairs)

    other_weight = across_cores(out_weight)

    parts = 2
    blocks = []
    for part in range(parts):
        prepared = None if part else (residual, norm_gain)
        attention, *prepared = attend(
            queries, kv_cache, block_index, lengths, part, parts, prepared
        )
        if prepared:
            extra = across_cores(prepared[0])
        if part + 1 < parts:
            attention, queries = lax.optimization_barrier((attention, queries))
        else:
            attention, other_weight, extra = lax.optimization_barrier(
                (attention, other_weight, extra)
            )
        blocks += [attention] + [turn(attention, k) for k in range(1, line)]

    attention, held = lax.optimization_barrier((attention, (out_weight, other_weight)))
    weight, other_weight = fetch(*held)
    message, mine_rows, give = project(
        blocks, weight, other_weight, residual, extra, parts
    )

    message, held = lax.optimization_barrier((message, (gate_weight, up_weight, down_weight)))
    weights = fetch(*held)
    blocks = [message] + [turn(message, k) for k in range(1, line)]
    taken = across_cores(give)
    routed, message = lax.optimization_barrier(((expert_ids.T, route_weights.T), message))
    lines, *chosen = routing_lines(*routed, line, pool_size - 1, capacity)
    blocks, taken, weights, lines = lax.optimization_barrier((blocks, taken, weights, lines))
    normed = normalize(blocks, lines, give, taken)
    attended = assemble(mine_rows, taken, line)

    last = pool_size - 1
    arrived = [normed] + [across_pool(normed, j) for j in range(1, last)]
    if pool_size == 4:
        arrived.append(across_pool(arrived[1], 2))
    else:
        arrived.append(across_pool(normed, last))
    crossed = [across_cores(rows) for rows in arrived[:last]]
    if pool_size == 4:
        crossed = [crossed[0], crossed[2], crossed[1]]
    pairs = list(zip(arrived[:last], crossed))
    steps = list(range(line))
    near = run_expert(pairs, weights, capacity, top_count, line, [steps])
    near = [part for (part,) in near]
    far, _ = lax.optimization_barrier((arrived[last], near))
    results = run_expert(
        [(far, across_cores(far))], weights, capacity, top_count, line, [[k] for k in steps]
    )[0]
    far_results = [turn(part, k) if k else part for k, part in enumerate(results)]
    far_chosen = plan_far(far, normed.shape[1] - ID_COLUMNS, top_count, line, capacity)
    returned = [across_pool(near[j], j) for j in range(1, last)]
    returned, far_results = lax.optimization_barrier((returned, far_results))
    returned = [near[0]] + returned
    mine, other = combine(returned, chosen, far_results, far_chosen, line)
    *summed, far_sum = add(mine, across_cores(other))
    landed = [turn(rows, k) if k else rows for k, rows in enumerate(summed)]
    final = finish(landed + [across_pool(far_sum, last)])
    return (attended, final)


def solution(mesh):
    return jax.shard_map(
        functools.partial(
            shards, pool_size=mesh.shape["pool"], expert_size=mesh.shape["expert"]
        ),
        mesh=mesh,
        in_specs=(
            P(("pool", "expert"), None),
            P(("pool", "expert"), None, None),
            P(("pool", "expert"), None),
            P(("pool", "expert")),
            P("pool", "expert"),
            P(None, "expert"),
            P("expert"),
            P("pool", None),
            P("pool", None),
            P(("pool", "expert"), None, None),
            P(("pool", "expert"), None, None),
            P(("pool", "expert"), None, None),
        ),
        out_specs=(P("pool", "expert"), P("pool", "expert")),
        check_vma=False,
    )
```

time: 461 us -> 109 us (0.24)
  local copies, waits for them, and re-layouts: 192 us -> 0.03 us
  matrix products: 101 us -> 0 us
  waiting for transfers between devices: 101 us -> 42.2 us
  starting transfers between devices: 7.12 us -> 37.7 us
  Pallas kernels: 0 us -> 27.4 us
  other arithmetic: 25.9 us -> 0 us
  blocking collectives: 15.5 us -> 0 us
  between operations: 14.2 us -> 0.83 us
    dot_general x28 -> x0, matrix products: 101 us -> none  [the longest x8 43.7 us: attend(): gathered = jnp.dot(selector, kv_flat, preferred_element_type=jnp.bfloat16)]
    all_to_all x2 -> x0, waiting for transfers between devices: 94.1 us -> none  [the longest x1 48.7 us: shards(): lax.all_to_all(result, ('pool', 'expert'), split_axis=0, concat_axis=0, t...]
    while x24 -> x0, local copies, waits for them, and re-layouts: 72.6 us -> none
    reshape x12 -> x0, local copies, waits for them, and re-layouts: 50.1 us -> none  [the longest x8 45 us: attend(): gathered = gathered.reshape(step_rows, context, kv_width)]
    ppermute x0 -> x29, waiting for transfers between devices: none -> 42.2 us  [the longest x15 21.6 us: turn(): return lax.ppermute(value, 'expert', pairs)]
    ppermute x0 -> x29, starting transfers between devices: none -> 37.7 us  [the longest x15 27.9 us: turn(): return lax.ppermute(value, 'expert', pairs)]
    slice x10 -> x0, local copies, waits for them, and re-layouts: 36.6 us -> none  [the longest x8 35.7 us: attend(): gathered[:, :, :kv_half].reshape(step_rows, context, kv_heads, HEAD_DIM)]
    pallas_call x0 -> x14, Pallas kernels: none -> 27.4 us  [the longest x2 9.64 us: attend(): pl.pallas_call(functools.partial(attend_kernel, block_len=block_len, firs...]
  transfers between devices with their start and end apart: 3 -> 29, of which waited for: 3 -> 12; matrix products, arithmetic and copies ran while one was open for 7% -> 0% of each run, Pallas kernels for 0% -> 23%
where the time goes in v1:
time: 109 us; the launch traced here: 108 us
  waiting for transfers between devices  42.2 us (39%)
  starting transfers between devices  37.7 us (35%)
  Pallas kernels  27.4 us (25%)
    ppermute x15, starting transfers between devices, turn(): return lax.ppermute(value, 'expert', pairs)  27.9 us
    ppermute x15, waiting for transfers between devices, turn(): return lax.ppermute(value, 'expert', pairs)  21.6 us
    ppermute x6, waiting for transfers between devices, across_pool(): return lax.ppermute(value, ('pool', 'expert'), pairs)  17.8 us
    pallas_call x2, Pallas kernels, attend(): pl.pallas_call(functools.partial(attend_kernel, block_len=block_len, firs...  9.64 us
    ppermute x6, starting transfers between devices, across_pool(): return lax.ppermute(value, ('pool', 'expert'), pairs)  8.45 us
    pallas_call x2, Pallas kernels, run_expert(): pl.pallas_call(functools.partial(expert_kernel, count=count, top_count=to...  6.99 us
    pallas_call x2, Pallas kernels, fetch(): pl.pallas_call(functools.partial(fetch_kernel, count=count), in_specs=[pl...  5.53 us
    ppermute x8, waiting for transfers between devices, across_cores(): lax.ppermute(value, 'expert', [(e, e ^ 1) for e in range(expert_size)])  2.81 us
  transfers between devices with their start and end apart: 29, of which 12 were waited for; matrix products, arithmetic and copies ran while one was open for 0% of the time, Pallas kernels for 23%

profile of v1, /device:TPU:0, one launch (start us, length us, event | category | flops | bytes accessed | tf_op | source)
XLA Modules:
  0.0 108.1 jit_solution(17526771068960807188)
XLA Ops:
  0.6 0.5 collective-permute-start.3
  1.1 4.9 %attend.2 = (bf16[32,2176]{1,0:T(8,128)(2,1)S(1)}, bf16[128,256]{1,0:T(8,128)(2,1)S(1)}) custom-call(s32[8,32]{1,0:T(8,128)} %bitcast.10, s32[1,32]{1,0:T(1,128)} %bitcast.12, bf16[32,4096]{1,0:T(8,128)(2,1)} %query_ref.2, bf16[2048,1024]{1,0:T(8,128)(2,1)} %bitcast.8, bf16[256,256]{1,0:T(8,128)(2,1)} %refs_10_.1, f32[1,256]{1,0:T(1,128)} %bitcast.14), custom_call_target="tpu_custom_call" | custom-call | tf_op jit(solution)/shard_map/attend/pallas_call | solution.py:149
  6.0 0.0 copy-start
  6.0 2.6 %collective-permute-start = (bf16[32,2176]{1,0:T(8,128)(2,1)S(1)}, bf16[32,2176]{1,0:T(8,128)(2,1)S(1)}, u32[]{:S(2)}, u32[]{:S(2)}) collective-permute-start(bf16[32,2176]{1,0:T(8,128)(2,1)S(1)} %get-tuple-element.64.refs_0_), channel_id=1, source_target_pairs={{0,2},{1,3},{2,4},{3,5},{4,6},{5,7},{6,0},{7,1},{8,10},{9,11},{10,... | collective-permute-start | bytes 417800 | tf_op jit(solution)/shard_map/ppermute | solution.py:691
  8.7 0.2 collective-permute-start.4
  8.9 2.6 %collective-permute-start.1 = (bf16[32,2176]{1,0:T(8,128)(2,1)S(1)}, bf16[32,2176]{1,0:T(8,128)(2,1)S(1)}, u32[]{:S(2)}, u32[]{:S(2)}) collective-permute-start(bf16[32,2176]{1,0:T(8,128)(2,1)S(1)} %get-tuple-element.64.refs_0_), channel_id=1, source_target_pairs={{0,4},{1,5},{2,6},{3,7},{4,0},{5,1},{6,2},{7,3},{8,12},{9,13},{10,... | collective-permute-start | bytes 417800 | tf_op jit(solution)/shard_map/ppermute | solution.py:691
  11.5 1.4 %collective-permute-start.2 = (bf16[32,2176]{1,0:T(8,128)(2,1)S(1)}, bf16[32,2176]{1,0:T(8,128)(2,1)S(1)}, u32[]{:S(2)}, u32[]{:S(2)}) collective-permute-start(bf16[32,2176]{1,0:T(8,128)(2,1)S(1)} %get-tuple-element.64.refs_0_), channel_id=1, source_target_pairs={{0,6},{1,7},{2,0},{3,1},{4,2},{5,3},{6,4},{7,5},{8,14},{9,15},{10,... | collective-permute-start | bytes 417800 | tf_op jit(solution)/shard_map/ppermute | solution.py:691
  12.8 4.8 %attend.3.refs_4_ = bf16[32,2048]{1,0:T(8,128)(2,1)S(1)} custom-call(s32[8,32]{1,0:T(8,128)} %bitcast.11, s32[1,32]{1,0:T(1,128)} %bitcast.13, bf16[32,4096]{1,0:T(8,128)(2,1)} %query_ref.2, bf16[2048,1024]{1,0:T(8,128)(2,1)} %bitcast.9), custom_call_target="tpu_custom_call" | custom-call | tf_op jit(solution)/shard_map/attend/pallas_call | solution.py:149
  17.6 0.0 copy-start.1
  17.6 0.0 collective-permute-done.4.refs_11_
  17.6 0.0 collective-permute-done.3.refs_1_
  17.6 0.7 collective-permute-start.5
  18.4 0.3 collective-permute-start.6
  18.7 2.8 %collective-permute-start.7 = (bf16[32,2048]{1,0:T(8,128)(2,1)S(1)}, bf16[32,2048]{1,0:T(8,128)(2,1)S(1)}, u32[]{:S(2)}, u32[]{:S(2)}) collective-permute-start(bf16[32,2048]{1,0:T(8,128)(2,1)S(1)} %attend.3.refs_4_), channel_id=1, source_target_pairs={{0,6},{1,7},{2,0},{3,1},{4,2},{5,3},{6,4},{7,5},{8,14},{9,15},{10,... | collective-permute-start | bytes 393224 | tf_op jit(solution)/shard_map/ppermute | solution.py:691
  21.5 1.7 %fetch.2 = (bf16[4096,256]{1,0:T(8,128)(2,1)S(1)}, bf16[4096,256]{1,0:T(8,128)(2,1)S(1)}) custom-call(bf16[4096,256]{1,0:T(8,128)(2,1)S(1)} %copy-done, bf16[4096,256]{1,0:T(8,128)(2,1)} %collective-permute-done.3.refs_1_), custom_call_target="tpu_custom_call" | custom-call | bytes 8388608 | tf_op jit(solution)/shard_map/fetch/pallas_call | solution.py:187
  23.3 0.0 copy-start.2
  23.3 0.0 copy-start.3
  23.3 0.0 collective-permute-done.2.refs_3_
  23.3 2.6 %collective-permute-done.5.refs_5_ = bf16[32,2048]{1,0:T(8,128)(2,1)S(1)} collective-permute-done((bf16[32,2048]{1,0:T(8,128)(2,1)S(1)}, bf16[32,2048]{1,0:T(8,128)(2,1)S(1)}, u32[]{:S(2)}, u32[]{:S(2)}) %collective-permute-start.5) | collective-permute-done | bytes 131104 | tf_op jit(solution)/shard_map/ppermute | solution.py:691
  25.9 6.5 %collective-permute-done.6.refs_6_ = bf16[32,2048]{1,0:T(8,128)(2,1)S(1)} collective-permute-done((bf16[32,2048]{1,0:T(8,128)(2,1)S(1)}, bf16[32,2048]{1,0:T(8,128)(2,1)S(1)}, u32[]{:S(2)}, u32[]{:S(2)}) %collective-permute-start.6) | collective-permute-done | bytes 131104 | tf_op jit(solution)/shard_map/ppermute | solution.py:691
  32.5 0.0 collective-permute-done.7.refs_7_
  32.5 0.7 project.1
  33.2 3.4 %collective-permute-start.8 = (bf16[128,512]{1,0:T(8,128)(2,1)S(1)}, bf16[128,512]{1,0:T(8,128)(2,1)S(1)}, u32[]{:S(2)}, u32[]{:S(2)}) collective-permute-start(bf16[128,512]{1,0:T(8,128)(2,1)S(1)} %get-tuple-element.89.refs_0_), channel_id=1, source_target_pairs={{0,2},{1,3},{2,4},{3,5},{4,6},{5,7},{6,0},{7,1},{8,10},{9,11},{10,... | collective-permute-start | bytes 393224 | tf_op jit(solution)/shard_map/ppermute | solution.py:691
  36.6 1.7 %collective-permute-start.9 = (bf16[128,512]{1,0:T(8,128)(2,1)S(1)}, bf16[128,512]{1,0:T(8,128)(2,1)S(1)}, u32[]{:S(2)}, u32[]{:S(2)}) collective-permute-start(bf16[128,512]{1,0:T(8,128)(2,1)S(1)} %get-tuple-element.89.refs_0_), channel_id=1, source_target_pairs={{0,4},{1,5},{2,6},{3,7},{4,0},{5,1},{6,2},{7,3},{8,12},{9,13},{10,... | collective-permute-start | bytes 393224 | tf_op jit(solution)/shard_map/ppermute | solution.py:691
  38.2 0.8 collective-permute-start.10
  39.0 0.9 lines.1
  39.9 3.8 %fetch.3 = (bf16[1,2048,768]{2,1,0:T(8,128)(2,1)S(1)}, bf16[1,2048,768]{2,1,0:T(8,128)(2,1)S(1)}, bf16[1,768,2048]{2,1,0:T(8,128)(2,1)S(1)}) custom-call(bf16[1,2048,768]{2,1,0:T(8,128)(2,1)} %refs_0_.3, bf16[1,2048,768]{2,1,0:T(8,128)(2,1)} %refs_1_, bf16[1,768,2048]{2,1,0:T(8,128)(2,1)} %refs_2_), custom_call_target="tpu_custom_call" | custom-call | bytes 18874368 | tf_op jit(solution)/shard_map/fetch/pallas_call | solution.py:187
  43.7 0.0 collective-permute-done.11.taken_ref
  43.7 3.0 %collective-permute-done.9.refs_2_ = bf16[128,512]{1,0:T(8,128)(2,1)S(1)} collective-permute-done((bf16[128,512]{1,0:T(8,128)(2,1)S(1)}, bf16[128,512]{1,0:T(8,128)(2,1)S(1)}, u32[]{:S(2)}, u32[]{:S(2)}) %collective-permute-start.9) | collective-permute-done | bytes 131104 | tf_op jit(solution)/shard_map/ppermute | solution.py:691
  46.7 0.3 normalize.1.refs_0_
  47.1 1.6 %collective-permute-start.14 = (bf16[128,2176]{1,0:T(8,128)(2,1)S(1)}, bf16[128,2176]{1,0:T(8,128)(2,1)S(1)}, u32[]{:S(2)}, u32[]{:S(2)}) collective-permute-start(bf16[128,2176]{1,0:T(8,128)(2,1)S(1)} %normalize.1.refs_0_), channel_id=1, source_target_pairs={{0,16},{1,9},{2,18},{3,11},{4,20},{5,13},{6,22},{7,15},{8,24},{9,1... | collective-permute-start | bytes 1671176 | tf_op jit(solution)/shard_map/ppermute | solution.py:704
  48.6 1.5 %collective-permute-start.13 = (bf16[128,2176]{1,0:T(8,128)(2,1)S(1)}, bf16[128,2176]{1,0:T(8,128)(2,1)S(1)}, u32[]{:S(2)}, u32[]{:S(2)}) collective-permute-start(bf16[128,2176]{1,0:T(8,128)(2,1)S(1)} %normalize.1.refs_0_), channel_id=1, source_target_pairs={{0,8},{1,17},{2,10},{3,19},{4,12},{5,21},{6,14},{7,23},{8,0},{9,25... | collective-permute-start | bytes 1671176 | tf_op jit(solution)/shard_map/ppermute | solution.py:704
  50.1 0.0 collective-permute-start.12
  50.1 12.3 %collective-permute-done.14.refs_4_ = bf16[128,2176]{1,0:T(8,128)(2,1)S(1)} collective-permute-done((bf16[128,2176]{1,0:T(8,128)(2,1)S(1)}, bf16[128,2176]{1,0:T(8,128)(2,1)S(1)}, u32[]{:S(2)}, u32[]{:S(2)}) %collective-permute-start.14) | collective-permute-done | bytes 557088 | tf_op jit(solution)/shard_map/ppermute | solution.py:704
  62.5 0.0 collective-permute-start.15
  62.5 0.0 collective-permute-done.13.refs_2_
  62.5 0.5 collective-permute-start.16
  63.0 1.5 %collective-permute-start.19 = (bf16[128,2176]{1,0:T(8,128)(2,1)S(1)}, bf16[128,2176]{1,0:T(8,128)(2,1)S(1)}, u32[]{:S(2)}, u32[]{:S(2)}) collective-permute-start(bf16[128,2176]{1,0:T(8,128)(2,1)S(1)} %collective-permute-done.13.refs_2_), channel_id=1, source_target_pairs={{0,16},{1,9},{2,18},{3,11},{4,20},{5,13},{6,22},{7,15},{8,24},{9,1... | collective-permute-start | bytes 1671176 | tf_op jit(solution)/shard_map/ppermute | solution.py:704
  64.5 0.7 collective-permute-done.16.refs_5_
  65.2 5.1 %expert.2 = (bf16[128,2048]{1,0:T(8,128)(2,1)S(1)}, bf16[128,2048]{1,0:T(8,128)(2,1)S(1)}, bf16[128,2048]{1,0:T(8,128)(2,1)S(1)}) custom-call(bf16[128,2176]{1,0:T(8,128)(2,1)S(1)} %normalize.1.refs_0_, bf16[128,2176]{1,0:T(8,128)(2,1)S(1)} %collective-permute-done.12.refs_1_, bf16[128,2176]{1,0:T(8,128)(2,1)S(1)} %collective-permute-done.13.refs_2_, ...), custom_call_target="tpu_custom_call" | custom-call | flops 3623878656 | bytes 15728640 | tf_op jit(solution)/shard_map/expert/pallas_call | solution.py:472
  70.3 2.2 %collective-permute-done.19.refs_0_.rows_ref = bf16[128,2176]{1,0:T(8,128)(2,1)S(1)} collective-permute-done((bf16[128,2176]{1,0:T(8,128)(2,1)S(1)}, bf16[128,2176]{1,0:T(8,128)(2,1)S(1)}, u32[]{:S(2)}, u32[]{:S(2)}) %collective-permute-start.19) | collective-permute-done | bytes 557088 | tf_op jit(solution)/shard_map/ppermute | solution.py:704
  72.5 0.9 collective-permute-start.17
  73.4 1.5 %collective-permute-start.18 = (bf16[128,2048]{1,0:T(8,128)(2,1)S(1)}, bf16[128,2048]{1,0:T(8,128)(2,1)S(1)}, u32[]{:S(2)}, u32[]{:S(2)}) collective-permute-start(bf16[128,2048]{1,0:T(8,128)(2,1)S(1)} %get-tuple-element.98), channel_id=1, source_target_pairs={{0,16},{1,9},{2,18},{3,11},{4,20},{5,13},{6,22},{7,15},{8,24},{9,1... | collective-permute-start | bytes 1572872 | tf_op jit(solution)/shard_map/ppermute | solution.py:704
  74.9 0.0 collective-permute-done.20.refs_1_
  74.9 1.9 %expert.3 = (bf16[128,512]{1,0:T(8,128)(2,1)S(1)}, bf16[128,512]{1,0:T(8,128)(2,1)S(1)}, bf16[128,512]{1,0:T(8,128)(2,1)S(1)}, bf16[128,512]{1,0:T(8,128)(2,1)S(1)}) custom-call(bf16[128,2176]{1,0:T(8,128)(2,1)S(1)} %collective-permute-done.19.refs_0_.rows_ref, bf16[128,2176]{1,0:T(8,128)(2,1)S(1)} %collective-permute-done.20.refs_1_, ...), custom_call_target="tpu_custom_call" | custom-call | flops 1207959552 | bytes 11534336 | tf_op jit(solution)/shard_map/expert/pallas_call | solution.py:472
  76.8 3.4 %collective-permute-start.21 = (bf16[128,512]{1,0:T(8,128)(2,1)S(1)}, bf16[128,512]{1,0:T(8,128)(2,1)S(1)}, u32[]{:S(2)}, u32[]{:S(2)}) collective-permute-start(bf16[128,512]{1,0:T(8,128)(2,1)S(1)} %get-tuple-element.101), channel_id=1, source_target_pairs={{0,2},{1,3},{2,4},{3,5},{4,6},{5,7},{6,0},{7,1},{8,10},{9,11},{10,... | collective-permute-start | bytes 393224 | tf_op jit(solution)/shard_map/ppermute | solution.py:691
  80.2 1.1 %collective-permute-start.22 = (bf16[128,512]{1,0:T(8,128)(2,1)S(1)}, bf16[128,512]{1,0:T(8,128)(2,1)S(1)}, u32[]{:S(2)}, u32[]{:S(2)}) collective-permute-start(bf16[128,512]{1,0:T(8,128)(2,1)S(1)} %get-tuple-element.102), channel_id=1, source_target_pairs={{0,4},{1,5},{2,6},{3,7},{4,0},{5,1},{6,2},{7,3},{8,12},{9,13},{10,... | collective-permute-start | bytes 393224 | tf_op jit(solution)/shard_map/ppermute | solution.py:691
  81.3 1.3 %collective-permute-start.23 = (bf16[128,512]{1,0:T(8,128)(2,1)S(1)}, bf16[128,512]{1,0:T(8,128)(2,1)S(1)}, u32[]{:S(2)}, u32[]{:S(2)}) collective-permute-start(bf16[128,512]{1,0:T(8,128)(2,1)S(1)} %get-tuple-element.103), channel_id=1, source_target_pairs={{0,6},{1,7},{2,0},{3,1},{4,2},{5,3},{6,4},{7,5},{8,14},{9,15},{10,... | collective-permute-start | bytes 393224 | tf_op jit(solution)/shard_map/ppermute | solution.py:691
  82.7 0.9 plan.1
  83.6 3.0 %collective-permute-done.17.refs_1_ = bf16[128,2048]{1,0:T(8,128)(2,1)S(1)} collective-permute-done((bf16[128,2048]{1,0:T(8,128)(2,1)S(1)}, bf16[128,2048]{1,0:T(8,128)(2,1)S(1)}, u32[]{:S(2)}, u32[]{:S(2)}) %collective-permute-start.17) | collective-permute-done | bytes 524320 | tf_op jit(solution)/shard_map/ppermute | solution.py:704
  86.6 0.3 collective-permute-done.18.refs_2_
  86.9 3.3 %collective-permute-done.22.refs_8_ = bf16[128,512]{1,0:T(8,128)(2,1)S(1)} collective-permute-done((bf16[128,512]{1,0:T(8,128)(2,1)S(1)}, bf16[128,512]{1,0:T(8,128)(2,1)S(1)}, u32[]{:S(2)}, u32[]{:S(2)}) %collective-permute-start.22) | collective-permute-done | bytes 131104 | tf_op jit(solution)/shard_map/ppermute | solution.py:691
  90.2 0.8 combine.1
  91.1 0.1 collective-permute-start.24
  91.1 2.1 %collective-permute-done.24.other_ref = bf16[5,256,256]{2,1,0:T(8,128)(2,1)S(1)} collective-permute-done((bf16[5,256,256]{2,1,0:T(8,128)(2,1)S(1)}, bf16[5,256,256]{2,1,0:T(8,128)(2,1)S(1)}, u32[]{:S(2)}, u32[]{:S(2)}) %collective-permute-start.24) | collective-permute-done | bytes 655392 | tf_op jit(solution)/shard_map/ppermute | solution.py:694
  93.2 0.2 add.1
  93.4 3.3 %collective-permute-start.25 = (bf16[256,256]{1,0:T(8,128)(2,1)S(1)}, bf16[256,256]{1,0:T(8,128)(2,1)S(1)}, u32[]{:S(2)}, u32[]{:S(2)}) collective-permute-start(bf16[256,256]{1,0:T(8,128)(2,1)S(1)} %get-tuple-element.120), channel_id=1, source_target_pairs={{0,2},{1,3},{2,4},{3,5},{4,6},{5,7},{6,0},{7,1},{8,10},{9,11},{10,... | collective-permute-start | bytes 393224 | tf_op jit(solution)/shard_map/ppermute | solution.py:691
  96.7 1.7 %collective-permute-start.26 = (bf16[256,256]{1,0:T(8,128)(2,1)S(1)}, bf16[256,256]{1,0:T(8,128)(2,1)S(1)}, u32[]{:S(2)}, u32[]{:S(2)}) collective-permute-start(bf16[256,256]{1,0:T(8,128)(2,1)S(1)} %get-tuple-element.121), channel_id=1, source_target_pairs={{0,4},{1,5},{2,6},{3,7},{4,0},{5,1},{6,2},{7,3},{8,12},{9,13},{10,... | collective-permute-start | bytes 393224 | tf_op jit(solution)/shard_map/ppermute | solution.py:691
  98.4 0.7 collective-permute-start.27
  99.1 1.5 %collective-permute-start.28 = (bf16[256,256]{1,0:T(8,128)(2,1)S(1)}, bf16[256,256]{1,0:T(8,128)(2,1)S(1)}, u32[]{:S(2)}, u32[]{:S(2)}) collective-permute-start(bf16[256,256]{1,0:T(8,128)(2,1)S(1)} %get-tuple-element.123), channel_id=1, source_target_pairs={{0,24},{1,25},{2,26},{3,27},{4,28},{5,29},{6,30},{7,31},{8,16},{9,... | collective-permute-start | bytes 393224 | tf_op jit(solution)/shard_map/ppermute | solution.py:704
  100.6 0.7 assemble.1
  101.3 1.0 collective-permute-done.25.refs_1_
  102.3 5.1 %collective-permute-done.26.refs_2_ = bf16[256,256]{1,0:T(8,128)(2,1)S(1)} collective-permute-done((bf16[256,256]{1,0:T(8,128)(2,1)S(1)}, bf16[256,256]{1,0:T(8,128)(2,1)S(1)}, u32[]{:S(2)}, u32[]{:S(2)}) %collective-permute-start.26) | collective-permute-done | bytes 131104 | tf_op jit(solution)/shard_map/ppermute | solution.py:691
  107.4 0.7 finish.1
  (16 shorter events, 0.0 us)
Async XLA Ops:
  0.6 17.0 %collective-permute-start.3 = (bf16[4096,256]{1,0:T(8,128)(2,1)}, bf16[4096,256]{1,0:T(8,128)(2,1)}, u32[]{:S(2)}, u32[]{:S(2)}) collective-permute-start(bf16[4096,256]{1,0:T(8,128)(2,1)} %refs_0_.2), channel_id=1, source_target_pairs={{0,1},{1,0},{2,3},{3,2},{4,5},{5,4},{6,7},{7,6},{8,9},{9,8},{10,11... | collective-permute-start | bytes 6291464 | tf_op jit(solution)/shard_map/ppermute | solution.py:694
  6.0 15.5 %copy-start = (bf16[4096,256]{1,0:T(8,128)(2,1)S(1)}, bf16[4096,256]{1,0:T(8,128)(2,1)}, u32[]{:S(2)}) copy-start(bf16[4096,256]{1,0:T(8,128)(2,1)} %refs_0_.2) | copy-start | bytes 6291460
  6.0 12.7 %collective-permute-start = (bf16[32,2176]{1,0:T(8,128)(2,1)S(1)}, bf16[32,2176]{1,0:T(8,128)(2,1)S(1)}, u32[]{:S(2)}, u32[]{:S(2)}) collective-permute-start(bf16[32,2176]{1,0:T(8,128)(2,1)S(1)} %get-tuple-element.64.refs_0_), channel_id=1, source_target_pairs={{0,2},{1,3},{2,4},{3,5},{4,6},{5,7},{6,0},{7,1},{8,10},{9,11},{10,... | collective-permute-start | bytes 417800 | tf_op jit(solution)/shard_map/ppermute | solution.py:691
  8.7 9.0 %collective-permute-start.4 = (bf16[128,256]{1,0:T(8,128)(2,1)S(1)}, bf16[128,256]{1,0:T(8,128)(2,1)S(1)}, u32[]{:S(2)}, u32[]{:S(2)}) collective-permute-start(bf16[128,256]{1,0:T(8,128)(2,1)S(1)} %get-tuple-element.66), channel_id=1, source_target_pairs={{0,1},{1,0},{2,3},{3,2},{4,5},{5,4},{6,7},{7,6},{8,9},{9,8},{10,11... | collective-permute-start | bytes 196616 | tf_op jit(solution)/shard_map/ppermute | solution.py:694
  8.9 14.4 %collective-permute-start.1 = (bf16[32,2176]{1,0:T(8,128)(2,1)S(1)}, bf16[32,2176]{1,0:T(8,128)(2,1)S(1)}, u32[]{:S(2)}, u32[]{:S(2)}) collective-permute-start(bf16[32,2176]{1,0:T(8,128)(2,1)S(1)} %get-tuple-element.64.refs_0_), channel_id=1, source_target_pairs={{0,4},{1,5},{2,6},{3,7},{4,0},{5,1},{6,2},{7,3},{8,12},{9,13},{10,... | collective-permute-start | bytes 417800 | tf_op jit(solution)/shard_map/ppermute | solution.py:691
  11.5 11.9 %collective-permute-start.2 = (bf16[32,2176]{1,0:T(8,128)(2,1)S(1)}, bf16[32,2176]{1,0:T(8,128)(2,1)S(1)}, u32[]{:S(2)}, u32[]{:S(2)}) collective-permute-start(bf16[32,2176]{1,0:T(8,128)(2,1)S(1)} %get-tuple-element.64.refs_0_), channel_id=1, source_target_pairs={{0,6},{1,7},{2,0},{3,1},{4,2},{5,3},{6,4},{7,5},{8,14},{9,15},{10,... | collective-permute-start | bytes 417800 | tf_op jit(solution)/shard_map/ppermute | solution.py:691
  17.6 14.9 %copy-start.1 = (bf16[256,256]{1,0:T(8,128)(2,1)S(1)}, bf16[256,256]{1,0:T(8,128)(2,1)}, u32[]{:S(2)}) copy-start(bf16[256,256]{1,0:T(8,128)(2,1)} %refs_10_.1) | copy-start | bytes 393220
  17.6 8.3 %collective-permute-start.5 = (bf16[32,2048]{1,0:T(8,128)(2,1)S(1)}, bf16[32,2048]{1,0:T(8,128)(2,1)S(1)}, u32[]{:S(2)}, u32[]{:S(2)}) collective-permute-start(bf16[32,2048]{1,0:T(8,128)(2,1)S(1)} %attend.3.refs_4_), channel_id=1, source_target_pairs={{0,2},{1,3},{2,4},{3,5},{4,6},{5,7},{6,0},{7,1},{8,10},{9,11},{10,... | collective-permute-start | bytes 393224 | tf_op jit(solution)/shard_map/ppermute | solution.py:691
  18.4 14.1 %collective-permute-start.6 = (bf16[32,2048]{1,0:T(8,128)(2,1)S(1)}, bf16[32,2048]{1,0:T(8,128)(2,1)S(1)}, u32[]{:S(2)}, u32[]{:S(2)}) collective-permute-start(bf16[32,2048]{1,0:T(8,128)(2,1)S(1)} %attend.3.refs_4_), channel_id=1, source_target_pairs={{0,4},{1,5},{2,6},{3,7},{4,0},{5,1},{6,2},{7,3},{8,12},{9,13},{10,... | collective-permute-start | bytes 393224 | tf_op jit(solution)/shard_map/ppermute | solution.py:691
  18.7 13.8 %collective-permute-start.7 = (bf16[32,2048]{1,0:T(8,128)(2,1)S(1)}, bf16[32,2048]{1,0:T(8,128)(2,1)S(1)}, u32[]{:S(2)}, u32[]{:S(2)}) collective-permute-start(bf16[32,2048]{1,0:T(8,128)(2,1)S(1)} %attend.3.refs_4_), channel_id=1, source_target_pairs={{0,6},{1,7},{2,0},{3,1},{4,2},{5,3},{6,4},{7,5},{8,14},{9,15},{10,... | collective-permute-start | bytes 393224 | tf_op jit(solution)/shard_map/ppermute | solution.py:691
  23.3 15.7 %copy-start.2 = (s32[256,8]{0,1:T(8,128)S(1)}, s32[256,8]{0,1:T(8,128)}, u32[]{:S(2)}) copy-start(s32[256,8]{0,1:T(8,128)} %param.19) | copy-start | bytes 24580
  23.3 15.7 %copy-start.3 = (f32[256,8]{0,1:T(8,128)S(1)}, f32[256,8]{0,1:T(8,128)}, u32[]{:S(2)}) copy-start(f32[256,8]{0,1:T(8,128)} %param.20) | copy-start | bytes 24580
  33.2 10.5 %collective-permute-start.8 = (bf16[128,512]{1,0:T(8,128)(2,1)S(1)}, bf16[128,512]{1,0:T(8,128)(2,1)S(1)}, u32[]{:S(2)}, u32[]{:S(2)}) collective-permute-start(bf16[128,512]{1,0:T(8,128)(2,1)S(1)} %get-tuple-element.89.refs_0_), channel_id=1, source_target_pairs={{0,2},{1,3},{2,4},{3,5},{4,6},{5,7},{6,0},{7,1},{8,10},{9,11},{10,... | collective-permute-start | bytes 393224 | tf_op jit(solution)/shard_map/ppermute | solution.py:691
  36.6 10.2 %collective-permute-start.9 = (bf16[128,512]{1,0:T(8,128)(2,1)S(1)}, bf16[128,512]{1,0:T(8,128)(2,1)S(1)}, u32[]{:S(2)}, u32[]{:S(2)}) collective-permute-start(bf16[128,512]{1,0:T(8,128)(2,1)S(1)} %get-tuple-element.89.refs_0_), channel_id=1, source_target_pairs={{0,4},{1,5},{2,6},{3,7},{4,0},{5,1},{6,2},{7,3},{8,12},{9,13},{10,... | collective-permute-start | bytes 393224 | tf_op jit(solution)/shard_map/ppermute | solution.py:691
  38.2 8.5 %collective-permute-start.10 = (bf16[128,512]{1,0:T(8,128)(2,1)S(1)}, bf16[128,512]{1,0:T(8,128)(2,1)S(1)}, u32[]{:S(2)}, u32[]{:S(2)}) collective-permute-start(bf16[128,512]{1,0:T(8,128)(2,1)S(1)} %get-tuple-element.89.refs_0_), channel_id=1, source_target_pairs={{0,6},{1,7},{2,0},{3,1},{4,2},{5,3},{6,4},{7,5},{8,14},{9,15},{10,... | collective-permute-start | bytes 393224 | tf_op jit(solution)/shard_map/ppermute | solution.py:691
  39.0 4.7 %collective-permute-start.11 = (bf16[144,256]{1,0:T(8,128)(2,1)S(1)}, bf16[144,256]{1,0:T(8,128)(2,1)S(1)}, u32[]{:S(2)}, u32[]{:S(2)}) collective-permute-start(bf16[144,256]{1,0:T(8,128)(2,1)S(1)} %get-tuple-element.77.give_ref), channel_id=1, source_target_pairs={{0,1},{1,0},{2,3},{3,2},{4,5},{5,4},{6,7},{7,6},{8,9},{9,8},{10,11... | collective-permute-start | bytes 221192 | tf_op jit(solution)/shard_map/ppermute | solution.py:694
  47.1 15.4 %collective-permute-start.14 = (bf16[128,2176]{1,0:T(8,128)(2,1)S(1)}, bf16[128,2176]{1,0:T(8,128)(2,1)S(1)}, u32[]{:S(2)}, u32[]{:S(2)}) collective-permute-start(bf16[128,2176]{1,0:T(8,128)(2,1)S(1)} %normalize.1.refs_0_), channel_id=1, source_target_pairs={{0,16},{1,9},{2,18},{3,11},{4,20},{5,13},{6,22},{7,15},{8,24},{9,1... | collective-permute-start | bytes 1671176 | tf_op jit(solution)/shard_map/ppermute | solution.py:704
  48.6 13.8 %collective-permute-start.13 = (bf16[128,2176]{1,0:T(8,128)(2,1)S(1)}, bf16[128,2176]{1,0:T(8,128)(2,1)S(1)}, u32[]{:S(2)}, u32[]{:S(2)}) collective-permute-start(bf16[128,2176]{1,0:T(8,128)(2,1)S(1)} %normalize.1.refs_0_), channel_id=1, source_target_pairs={{0,8},{1,17},{2,10},{3,19},{4,12},{5,21},{6,14},{7,23},{8,0},{9,25... | collective-permute-start | bytes 1671176 | tf_op jit(solution)/shard_map/ppermute | solution.py:704
  50.1 14.4 %collective-permute-start.12 = (bf16[128,2176]{1,0:T(8,128)(2,1)S(1)}, bf16[128,2176]{1,0:T(8,128)(2,1)S(1)}, u32[]{:S(2)}, u32[]{:S(2)}) collective-permute-start(bf16[128,2176]{1,0:T(8,128)(2,1)S(1)} %normalize.1.refs_0_), channel_id=1, source_target_pairs={{0,1},{1,0},{2,3},{3,2},{4,5},{5,4},{6,7},{7,6},{8,9},{9,8},{10,11... | collective-permute-start | bytes 1671176 | tf_op jit(solution)/shard_map/ppermute | solution.py:694
  62.5 2.0 %collective-permute-start.15 = (bf16[128,2176]{1,0:T(8,128)(2,1)S(1)}, bf16[128,2176]{1,0:T(8,128)(2,1)S(1)}, u32[]{:S(2)}, u32[]{:S(2)}) collective-permute-start(bf16[128,2176]{1,0:T(8,128)(2,1)S(1)} %collective-permute-done.14.refs_4_), channel_id=1, source_target_pairs={{0,1},{1,0},{2,3},{3,2},{4,5},{5,4},{6,7},{7,6},{8,9},{9,8},{10,11... | collective-permute-start | bytes 1671176 | tf_op jit(solution)/shard_map/ppermute | solution.py:694
  62.5 2.7 %collective-permute-start.16 = (bf16[128,2176]{1,0:T(8,128)(2,1)S(1)}, bf16[128,2176]{1,0:T(8,128)(2,1)S(1)}, u32[]{:S(2)}, u32[]{:S(2)}) collective-permute-start(bf16[128,2176]{1,0:T(8,128)(2,1)S(1)} %collective-permute-done.13.refs_2_), channel_id=1, source_target_pairs={{0,1},{1,0},{2,3},{3,2},{4,5},{5,4},{6,7},{7,6},{8,9},{9,8},{10,11... | collective-permute-start | bytes 1671176 | tf_op jit(solution)/shard_map/ppermute | solution.py:694
  63.0 9.5 %collective-permute-start.19 = (bf16[128,2176]{1,0:T(8,128)(2,1)S(1)}, bf16[128,2176]{1,0:T(8,128)(2,1)S(1)}, u32[]{:S(2)}, u32[]{:S(2)}) collective-permute-start(bf16[128,2176]{1,0:T(8,128)(2,1)S(1)} %collective-permute-done.13.refs_2_), channel_id=1, source_target_pairs={{0,16},{1,9},{2,18},{3,11},{4,20},{5,13},{6,22},{7,15},{8,24},{9,1... | collective-permute-start | bytes 1671176 | tf_op jit(solution)/shard_map/ppermute | solution.py:704
  72.5 2.4 %collective-permute-start.20 = (bf16[128,2176]{1,0:T(8,128)(2,1)S(1)}, bf16[128,2176]{1,0:T(8,128)(2,1)S(1)}, u32[]{:S(2)}, u32[]{:S(2)}) collective-permute-start(bf16[128,2176]{1,0:T(8,128)(2,1)S(1)} %collective-permute-done.19.refs_0_.rows_ref), channel_id=1, source_target_pairs={{0,1},{1,0},{2,3},{3,2},{4,5},{5,4},{6,7},{7,6},{8,9},{9,8},{10,11... | collective-permute-start | bytes 1671176 | tf_op jit(solution)/shard_map/ppermute | solution.py:694
  72.5 14.1 %collective-permute-start.17 = (bf16[128,2048]{1,0:T(8,128)(2,1)S(1)}, bf16[128,2048]{1,0:T(8,128)(2,1)S(1)}, u32[]{:S(2)}, u32[]{:S(2)}) collective-permute-start(bf16[128,2048]{1,0:T(8,128)(2,1)S(1)} %get-tuple-element.97), channel_id=1, source_target_pairs={{0,8},{1,17},{2,10},{3,19},{4,12},{5,21},{6,14},{7,23},{8,0},{9,25... | collective-permute-start | bytes 1572872 | tf_op jit(solution)/shard_map/ppermute | solution.py:704
  73.4 13.5 %collective-permute-start.18 = (bf16[128,2048]{1,0:T(8,128)(2,1)S(1)}, bf16[128,2048]{1,0:T(8,128)(2,1)S(1)}, u32[]{:S(2)}, u32[]{:S(2)}) collective-permute-start(bf16[128,2048]{1,0:T(8,128)(2,1)S(1)} %get-tuple-element.98), channel_id=1, source_target_pairs={{0,16},{1,9},{2,18},{3,11},{4,20},{5,13},{6,22},{7,15},{8,24},{9,1... | collective-permute-start | bytes 1572872 | tf_op jit(solution)/shard_map/ppermute | solution.py:704
  76.8 10.1 %collective-permute-start.21 = (bf16[128,512]{1,0:T(8,128)(2,1)S(1)}, bf16[128,512]{1,0:T(8,128)(2,1)S(1)}, u32[]{:S(2)}, u32[]{:S(2)}) collective-permute-start(bf16[128,512]{1,0:T(8,128)(2,1)S(1)} %get-tuple-element.101), channel_id=1, source_target_pairs={{0,2},{1,3},{2,4},{3,5},{4,6},{5,7},{6,0},{7,1},{8,10},{9,11},{10,... | collective-permute-start | bytes 393224 | tf_op jit(solution)/shard_map/ppermute | solution.py:691
  80.2 10.0 %collective-permute-start.22 = (bf16[128,512]{1,0:T(8,128)(2,1)S(1)}, bf16[128,512]{1,0:T(8,128)(2,1)S(1)}, u32[]{:S(2)}, u32[]{:S(2)}) collective-permute-start(bf16[128,512]{1,0:T(8,128)(2,1)S(1)} %get-tuple-element.102), channel_id=1, source_target_pairs={{0,4},{1,5},{2,6},{3,7},{4,0},{5,1},{6,2},{7,3},{8,12},{9,13},{10,... | collective-permute-start | bytes 393224 | tf_op jit(solution)/shard_map/ppermute | solution.py:691
  81.3 8.9 %collective-permute-start.23 = (bf16[128,512]{1,0:T(8,128)(2,1)S(1)}, bf16[128,512]{1,0:T(8,128)(2,1)S(1)}, u32[]{:S(2)}, u32[]{:S(2)}) collective-permute-start(bf16[128,512]{1,0:T(8,128)(2,1)S(1)} %get-tuple-element.103), channel_id=1, source_target_pairs={{0,6},{1,7},{2,0},{3,1},{4,2},{5,3},{6,4},{7,5},{8,14},{9,15},{10,... | collective-permute-start | bytes 393224 | tf_op jit(solution)/shard_map/ppermute | solution.py:691
  91.1 2.2 %collective-permute-start.24 = (bf16[5,256,256]{2,1,0:T(8,128)(2,1)S(1)}, bf16[5,256,256]{2,1,0:T(8,128)(2,1)S(1)}, u32[]{:S(2)}, u32[]{:S(2)}) collective-permute-start(bf16[5,256,256]{2,1,0:T(8,128)(2,1)S(1)} %get-tuple-element.118), channel_id=1, source_target_pairs={{0,1},{1,0},{2,3},{3,2},{4,5},{5,4},{6,7},{7,6},{8,9},{9,8},{10,11... | collective-permute-start | bytes 1966088 | tf_op jit(solution)/shard_map/ppermute | solution.py:694
  93.4 8.9 %collective-permute-start.25 = (bf16[256,256]{1,0:T(8,128)(2,1)S(1)}, bf16[256,256]{1,0:T(8,128)(2,1)S(1)}, u32[]{:S(2)}, u32[]{:S(2)}) collective-permute-start(bf16[256,256]{1,0:T(8,128)(2,1)S(1)} %get-tuple-element.120), channel_id=1, source_target_pairs={{0,2},{1,3},{2,4},{3,5},{4,6},{5,7},{6,0},{7,1},{8,10},{9,11},{10,... | collective-permute-start | bytes 393224 | tf_op jit(solution)/shard_map/ppermute | solution.py:691
  96.7 10.7 %collective-permute-start.26 = (bf16[256,256]{1,0:T(8,128)(2,1)S(1)}, bf16[256,256]{1,0:T(8,128)(2,1)S(1)}, u32[]{:S(2)}, u32[]{:S(2)}) collective-permute-start(bf16[256,256]{1,0:T(8,128)(2,1)S(1)} %get-tuple-element.121), channel_id=1, source_target_pairs={{0,4},{1,5},{2,6},{3,7},{4,0},{5,1},{6,2},{7,3},{8,12},{9,13},{10,... | collective-permute-start | bytes 393224 | tf_op jit(solution)/shard_map/ppermute | solution.py:691
  98.4 8.9 %collective-permute-start.27 = (bf16[256,256]{1,0:T(8,128)(2,1)S(1)}, bf16[256,256]{1,0:T(8,128)(2,1)S(1)}, u32[]{:S(2)}, u32[]{:S(2)}) collective-permute-start(bf16[256,256]{1,0:T(8,128)(2,1)S(1)} %get-tuple-element.122), channel_id=1, source_target_pairs={{0,6},{1,7},{2,0},{3,1},{4,2},{5,3},{6,4},{7,5},{8,14},{9,15},{10,... | collective-permute-start | bytes 393224 | tf_op jit(solution)/shard_map/ppermute | solution.py:691
  99.1 8.2 %collective-permute-start.28 = (bf16[256,256]{1,0:T(8,128)(2,1)S(1)}, bf16[256,256]{1,0:T(8,128)(2,1)S(1)}, u32[]{:S(2)}, u32[]{:S(2)}) collective-permute-start(bf16[256,256]{1,0:T(8,128)(2,1)S(1)} %get-tuple-element.123), channel_id=1, source_target_pairs={{0,24},{1,25},{2,26},{3,27},{4,28},{5,29},{6,30},{7,31},{8,16},{9,... | collective-permute-start | bytes 393224 | tf_op jit(solution)/shard_map/ppermute | solution.py:704

commit v2 on v1

--- a/solution.py
+++ b/solution.py
@@ -61,7 +61,7 @@
                     kv_hbm.at[at, columns], target.at[at, :], sems.at[kind, piece]
                 )
             )
-    for copy in copies[:pieces]:
+    for copy in copies:
         copy.start()
     if prepares:
         columns_ref = out_ref.at[:, pl.ds(query_ref.shape[1], GAIN_COLUMNS)]
@@ -110,8 +110,6 @@
         if g == 0:
             for copy in copies[:pieces]:
                 copy.wait()
-            for copy in copies[pieces:]:
-                copy.start()
         scores = lax.dot_general(
             query, key_ref[:, head], (((1,), (1,)), ((), ())), preferred_element_type=jnp.float32
         )

time: 109 us -> 108 us (level)
  transfers between devices with their start and end apart: 29 -> 29, of which waited for: 12 -> 12; matrix products, arithmetic and copies ran while one was open for 0% -> 0% of each run, Pallas kernels for 23% -> 22%
where the time goes in v2:
time: 108 us
  waiting for transfers between devices  42.5 us (39%)
  starting transfers between devices  37.7 us (35%)
  Pallas kernels  26.7 us (25%)
    ppermute x15, starting transfers between devices, turn(): return lax.ppermute(value, 'expert', pairs)  27.9 us
    ppermute x15, waiting for transfers between devices, turn(): return lax.ppermute(value, 'expert', pairs)  22 us
    ppermute x6, waiting for transfers between devices, across_pool(): return lax.ppermute(value, ('pool', 'expert'), pairs)  17.7 us
    pallas_call x2, Pallas kernels, attend(): pl.pallas_call(functools.partial(attend_kernel, block_len=block_len, firs...  8.96 us
    ppermute x6, starting transfers between devices, across_pool(): return lax.ppermute(value, ('pool', 'expert'), pairs)  8.51 us
    pallas_call x2, Pallas kernels, run_expert(): pl.pallas_call(functools.partial(expert_kernel, count=count, top_count=to...  7 us
    pallas_call x2, Pallas kernels, fetch(): pl.pallas_call(functools.partial(fetch_kernel, count=count), in_specs=[pl...  5.53 us
    ppermute x8, waiting for transfers between devices, across_cores(): lax.ppermute(value, 'expert', [(e, e ^ 1) for e in range(expert_size)])  2.8 us
  transfers between devices with their start and end apart: 29, of which 12 were waited for; matrix products, arithmetic and copies ran while one was open for 0% of the time, Pallas kernels for 22%

profile of v2, /device:TPU:0, one launch (start us, length us, event | category | flops | bytes accessed | tf_op | source)
XLA Modules:
  0.0 107.8 jit_solution(6170157959224147637)
XLA Ops:
  0.6 0.5 collective-permute-start.3
  1.1 4.5 %attend.2 = (bf16[32,2176]{1,0:T(8,128)(2,1)S(1)}, bf16[128,256]{1,0:T(8,128)(2,1)S(1)}) custom-call(s32[8,32]{1,0:T(8,128)} %bitcast.10, s32[1,32]{1,0:T(1,128)} %bitcast.12, bf16[32,4096]{1,0:T(8,128)(2,1)} %query_ref.2, bf16[2048,1024]{1,0:T(8,128)(2,1)} %bitcast.8, bf16[256,256]{1,0:T(8,128)(2,1)} %refs_10_.1, f32[1,256]{1,0:T(1,128)} %bitcast.14), custom_call_target="tpu_custom_call" | custom-call | tf_op jit(solution)/shard_map/attend/pallas_call | solution.py:147
  5.7 0.0 copy-start
  5.7 2.6 %collective-permute-start = (bf16[32,2176]{1,0:T(8,128)(2,1)S(1)}, bf16[32,2176]{1,0:T(8,128)(2,1)S(1)}, u32[]{:S(2)}, u32[]{:S(2)}) collective-permute-start(bf16[32,2176]{1,0:T(8,128)(2,1)S(1)} %get-tuple-element.64.refs_0_), channel_id=1, source_target_pairs={{0,2},{1,3},{2,4},{3,5},{4,6},{5,7},{6,0},{7,1},{8,10},{9,11},{10,... | collective-permute-start | bytes 417800 | tf_op jit(solution)/shard_map/ppermute | solution.py:689
  8.3 0.2 collective-permute-start.4
  8.5 2.6 %collective-permute-start.1 = (bf16[32,2176]{1,0:T(8,128)(2,1)S(1)}, bf16[32,2176]{1,0:T(8,128)(2,1)S(1)}, u32[]{:S(2)}, u32[]{:S(2)}) collective-permute-start(bf16[32,2176]{1,0:T(8,128)(2,1)S(1)} %get-tuple-element.64.refs_0_), channel_id=1, source_target_pairs={{0,4},{1,5},{2,6},{3,7},{4,0},{5,1},{6,2},{7,3},{8,12},{9,13},{10,... | collective-permute-start | bytes 417800 | tf_op jit(solution)/shard_map/ppermute | solution.py:689
  11.1 1.4 %collective-permute-start.2 = (bf16[32,2176]{1,0:T(8,128)(2,1)S(1)}, bf16[32,2176]{1,0:T(8,128)(2,1)S(1)}, u32[]{:S(2)}, u32[]{:S(2)}) collective-permute-start(bf16[32,2176]{1,0:T(8,128)(2,1)S(1)} %get-tuple-element.64.refs_0_), channel_id=1, source_target_pairs={{0,6},{1,7},{2,0},{3,1},{4,2},{5,3},{6,4},{7,5},{8,14},{9,15},{10,... | collective-permute-start | bytes 417800 | tf_op jit(solution)/shard_map/ppermute | solution.py:689
  12.5 4.4 %attend.3.refs_4_ = bf16[32,2048]{1,0:T(8,128)(2,1)S(1)} custom-call(s32[8,32]{1,0:T(8,128)} %bitcast.11, s32[1,32]{1,0:T(1,128)} %bitcast.13, bf16[32,4096]{1,0:T(8,128)(2,1)} %query_ref.2, bf16[2048,1024]{1,0:T(8,128)(2,1)} %bitcast.9), custom_call_target="tpu_custom_call" | custom-call | tf_op jit(solution)/shard_map/attend/pallas_call | solution.py:147
  16.9 0.0 copy-start.1
  16.9 0.0 collective-permute-done.4.refs_11_
  17.0 0.7 collective-permute-start.5
  17.7 0.3 collective-permute-start.6
  18.0 0.0 collective-permute-done.refs_1_
  18.0 2.8 %collective-permute-start.7 = (bf16[32,2048]{1,0:T(8,128)(2,1)S(1)}, bf16[32,2048]{1,0:T(8,128)(2,1)S(1)}, u32[]{:S(2)}, u32[]{:S(2)}) collective-permute-start(bf16[32,2048]{1,0:T(8,128)(2,1)S(1)} %attend.3.refs_4_), channel_id=1, source_target_pairs={{0,6},{1,7},{2,0},{3,1},{4,2},{5,3},{6,4},{7,5},{8,14},{9,15},{10,... | collective-permute-start | bytes 393224 | tf_op jit(solution)/shard_map/ppermute | solution.py:689
  20.8 1.7 %fetch.2 = (bf16[4096,256]{1,0:T(8,128)(2,1)S(1)}, bf16[4096,256]{1,0:T(8,128)(2,1)S(1)}) custom-call(bf16[4096,256]{1,0:T(8,128)(2,1)S(1)} %copy-done, bf16[4096,256]{1,0:T(8,128)(2,1)} %collective-permute-done.3.refs_1_), custom_call_target="tpu_custom_call" | custom-call | bytes 8388608 | tf_op jit(solution)/shard_map/fetch/pallas_call | solution.py:185
  22.6 0.0 copy-start.2
  22.6 0.0 copy-start.3
  22.6 0.0 collective-permute-done.1.refs_2_
  22.6 0.0 collective-permute-done.2.refs_3_
  22.6 2.6 %collective-permute-done.5.refs_5_ = bf16[32,2048]{1,0:T(8,128)(2,1)S(1)} collective-permute-done((bf16[32,2048]{1,0:T(8,128)(2,1)S(1)}, bf16[32,2048]{1,0:T(8,128)(2,1)S(1)}, u32[]{:S(2)}, u32[]{:S(2)}) %collective-permute-start.5) | collective-permute-done | bytes 131104 | tf_op jit(solution)/shard_map/ppermute | solution.py:689
  25.3 6.9 %collective-permute-done.6.refs_6_ = bf16[32,2048]{1,0:T(8,128)(2,1)S(1)} collective-permute-done((bf16[32,2048]{1,0:T(8,128)(2,1)S(1)}, bf16[32,2048]{1,0:T(8,128)(2,1)S(1)}, u32[]{:S(2)}, u32[]{:S(2)}) %collective-permute-start.6) | collective-permute-done | bytes 131104 | tf_op jit(solution)/shard_map/ppermute | solution.py:689
  32.1 0.0 collective-permute-done.7.refs_7_
  32.1 0.7 project.1
  32.9 3.4 %collective-permute-start.8 = (bf16[128,512]{1,0:T(8,128)(2,1)S(1)}, bf16[128,512]{1,0:T(8,128)(2,1)S(1)}, u32[]{:S(2)}, u32[]{:S(2)}) collective-permute-start(bf16[128,512]{1,0:T(8,128)(2,1)S(1)} %get-tuple-element.89.refs_0_), channel_id=1, source_target_pairs={{0,2},{1,3},{2,4},{3,5},{4,6},{5,7},{6,0},{7,1},{8,10},{9,11},{10,... | collective-permute-start | bytes 393224 | tf_op jit(solution)/shard_map/ppermute | solution.py:689
  36.2 1.7 %collective-permute-start.9 = (bf16[128,512]{1,0:T(8,128)(2,1)S(1)}, bf16[128,512]{1,0:T(8,128)(2,1)S(1)}, u32[]{:S(2)}, u32[]{:S(2)}) collective-permute-start(bf16[128,512]{1,0:T(8,128)(2,1)S(1)} %get-tuple-element.89.refs_0_), channel_id=1, source_target_pairs={{0,4},{1,5},{2,6},{3,7},{4,0},{5,1},{6,2},{7,3},{8,12},{9,13},{10,... | collective-permute-start | bytes 393224 | tf_op jit(solution)/shard_map/ppermute | solution.py:689
  37.9 0.8 collective-permute-start.10
  38.7 0.0 collective-permute-start.11
  38.7 0.9 lines.1
  39.6 3.8 %fetch.3 = (bf16[1,2048,768]{2,1,0:T(8,128)(2,1)S(1)}, bf16[1,2048,768]{2,1,0:T(8,128)(2,1)S(1)}, bf16[1,768,2048]{2,1,0:T(8,128)(2,1)S(1)}) custom-call(bf16[1,2048,768]{2,1,0:T(8,128)(2,1)} %refs_0_.3, bf16[1,2048,768]{2,1,0:T(8,128)(2,1)} %refs_1_, bf16[1,768,2048]{2,1,0:T(8,128)(2,1)} %refs_2_), custom_call_target="tpu_custom_call" | custom-call | bytes 18874368 | tf_op jit(solution)/shard_map/fetch/pallas_call | solution.py:185
  43.3 0.0 collective-permute-done.11.taken_ref
  43.4 3.0 %collective-permute-done.9.refs_2_ = bf16[128,512]{1,0:T(8,128)(2,1)S(1)} collective-permute-done((bf16[128,512]{1,0:T(8,128)(2,1)S(1)}, bf16[128,512]{1,0:T(8,128)(2,1)S(1)}, u32[]{:S(2)}, u32[]{:S(2)}) %collective-permute-start.9) | collective-permute-done | bytes 131104 | tf_op jit(solution)/shard_map/ppermute | solution.py:689
  46.4 0.3 normalize.1.refs_0_
  46.7 1.6 %collective-permute-start.14 = (bf16[128,2176]{1,0:T(8,128)(2,1)S(1)}, bf16[128,2176]{1,0:T(8,128)(2,1)S(1)}, u32[]{:S(2)}, u32[]{:S(2)}) collective-permute-start(bf16[128,2176]{1,0:T(8,128)(2,1)S(1)} %normalize.1.refs_0_), channel_id=1, source_target_pairs={{0,16},{1,9},{2,18},{3,11},{4,20},{5,13},{6,22},{7,15},{8,24},{9,1... | collective-permute-start | bytes 1671176 | tf_op jit(solution)/shard_map/ppermute | solution.py:702
  48.3 1.5 %collective-permute-start.13 = (bf16[128,2176]{1,0:T(8,128)(2,1)S(1)}, bf16[128,2176]{1,0:T(8,128)(2,1)S(1)}, u32[]{:S(2)}, u32[]{:S(2)}) collective-permute-start(bf16[128,2176]{1,0:T(8,128)(2,1)S(1)} %normalize.1.refs_0_), channel_id=1, source_target_pairs={{0,8},{1,17},{2,10},{3,19},{4,12},{5,21},{6,14},{7,23},{8,0},{9,25... | collective-permute-start | bytes 1671176 | tf_op jit(solution)/shard_map/ppermute | solution.py:702
  49.8 0.0 collective-permute-start.12
  49.8 12.3 %collective-permute-done.14.refs_4_ = bf16[128,2176]{1,0:T(8,128)(2,1)S(1)} collective-permute-done((bf16[128,2176]{1,0:T(8,128)(2,1)S(1)}, bf16[128,2176]{1,0:T(8,128)(2,1)S(1)}, u32[]{:S(2)}, u32[]{:S(2)}) %collective-permute-start.14) | collective-permute-done | bytes 557088 | tf_op jit(solution)/shard_map/ppermute | solution.py:702
  62.1 0.0 collective-permute-start.15
  62.1 0.5 collective-permute-start.16
  62.6 1.5 %collective-permute-start.19 = (bf16[128,2176]{1,0:T(8,128)(2,1)S(1)}, bf16[128,2176]{1,0:T(8,128)(2,1)S(1)}, u32[]{:S(2)}, u32[]{:S(2)}) collective-permute-start(bf16[128,2176]{1,0:T(8,128)(2,1)S(1)} %collective-permute-done.13.refs_2_), channel_id=1, source_target_pairs={{0,16},{1,9},{2,18},{3,11},{4,20},{5,13},{6,22},{7,15},{8,24},{9,1... | collective-permute-start | bytes 1671176 | tf_op jit(solution)/shard_map/ppermute | solution.py:702
  64.2 0.7 collective-permute-done.16.refs_5_
  64.9 5.1 %expert.2 = (bf16[128,2048]{1,0:T(8,128)(2,1)S(1)}, bf16[128,2048]{1,0:T(8,128)(2,1)S(1)}, bf16[128,2048]{1,0:T(8,128)(2,1)S(1)}) custom-call(bf16[128,2176]{1,0:T(8,128)(2,1)S(1)} %normalize.1.refs_0_, bf16[128,2176]{1,0:T(8,128)(2,1)S(1)} %collective-permute-done.12.refs_1_, bf16[128,2176]{1,0:T(8,128)(2,1)S(1)} %collective-permute-done.13.refs_2_, ...), custom_call_target="tpu_custom_call" | custom-call | flops 3623878656 | bytes 15728640 | tf_op jit(solution)/shard_map/expert/pallas_call | solution.py:470
  70.0 2.2 %collective-permute-done.19.refs_0_.rows_ref = bf16[128,2176]{1,0:T(8,128)(2,1)S(1)} collective-permute-done((bf16[128,2176]{1,0:T(8,128)(2,1)S(1)}, bf16[128,2176]{1,0:T(8,128)(2,1)S(1)}, u32[]{:S(2)}, u32[]{:S(2)}) %collective-permute-start.19) | collective-permute-done | bytes 557088 | tf_op jit(solution)/shard_map/ppermute | solution.py:702
  72.2 0.9 collective-permute-start.17
  73.0 1.5 %collective-permute-start.18 = (bf16[128,2048]{1,0:T(8,128)(2,1)S(1)}, bf16[128,2048]{1,0:T(8,128)(2,1)S(1)}, u32[]{:S(2)}, u32[]{:S(2)}) collective-permute-start(bf16[128,2048]{1,0:T(8,128)(2,1)S(1)} %get-tuple-element.98), channel_id=1, source_target_pairs={{0,16},{1,9},{2,18},{3,11},{4,20},{5,13},{6,22},{7,15},{8,24},{9,1... | collective-permute-start | bytes 1572872 | tf_op jit(solution)/shard_map/ppermute | solution.py:702
  74.6 1.9 %expert.3 = (bf16[128,512]{1,0:T(8,128)(2,1)S(1)}, bf16[128,512]{1,0:T(8,128)(2,1)S(1)}, bf16[128,512]{1,0:T(8,128)(2,1)S(1)}, bf16[128,512]{1,0:T(8,128)(2,1)S(1)}) custom-call(bf16[128,2176]{1,0:T(8,128)(2,1)S(1)} %collective-permute-done.19.refs_0_.rows_ref, bf16[128,2176]{1,0:T(8,128)(2,1)S(1)} %collective-permute-done.20.refs_1_, ...), custom_call_target="tpu_custom_call" | custom-call | flops 1207959552 | bytes 11534336 | tf_op jit(solution)/shard_map/expert/pallas_call | solution.py:470
  76.5 3.4 %collective-permute-start.21 = (bf16[128,512]{1,0:T(8,128)(2,1)S(1)}, bf16[128,512]{1,0:T(8,128)(2,1)S(1)}, u32[]{:S(2)}, u32[]{:S(2)}) collective-permute-start(bf16[128,512]{1,0:T(8,128)(2,1)S(1)} %get-tuple-element.101), channel_id=1, source_target_pairs={{0,2},{1,3},{2,4},{3,5},{4,6},{5,7},{6,0},{7,1},{8,10},{9,11},{10,... | collective-permute-start | bytes 393224 | tf_op jit(solution)/shard_map/ppermute | solution.py:689
  79.9 1.1 %collective-permute-start.22 = (bf16[128,512]{1,0:T(8,128)(2,1)S(1)}, bf16[128,512]{1,0:T(8,128)(2,1)S(1)}, u32[]{:S(2)}, u32[]{:S(2)}) collective-permute-start(bf16[128,512]{1,0:T(8,128)(2,1)S(1)} %get-tuple-element.102), channel_id=1, source_target_pairs={{0,4},{1,5},{2,6},{3,7},{4,0},{5,1},{6,2},{7,3},{8,12},{9,13},{10,... | collective-permute-start | bytes 393224 | tf_op jit(solution)/shard_map/ppermute | solution.py:689
  81.0 1.3 %collective-permute-start.23 = (bf16[128,512]{1,0:T(8,128)(2,1)S(1)}, bf16[128,512]{1,0:T(8,128)(2,1)S(1)}, u32[]{:S(2)}, u32[]{:S(2)}) collective-permute-start(bf16[128,512]{1,0:T(8,128)(2,1)S(1)} %get-tuple-element.103), channel_id=1, source_target_pairs={{0,6},{1,7},{2,0},{3,1},{4,2},{5,3},{6,4},{7,5},{8,14},{9,15},{10,... | collective-permute-start | bytes 393224 | tf_op jit(solution)/shard_map/ppermute | solution.py:689
  82.3 0.9 plan.1
  83.3 2.9 %collective-permute-done.17.refs_1_ = bf16[128,2048]{1,0:T(8,128)(2,1)S(1)} collective-permute-done((bf16[128,2048]{1,0:T(8,128)(2,1)S(1)}, bf16[128,2048]{1,0:T(8,128)(2,1)S(1)}, u32[]{:S(2)}, u32[]{:S(2)}) %collective-permute-start.17) | collective-permute-done | bytes 524320 | tf_op jit(solution)/shard_map/ppermute | solution.py:702
  86.2 0.3 collective-permute-done.18.refs_2_
  86.5 3.3 %collective-permute-done.22.refs_8_ = bf16[128,512]{1,0:T(8,128)(2,1)S(1)} collective-permute-done((bf16[128,512]{1,0:T(8,128)(2,1)S(1)}, bf16[128,512]{1,0:T(8,128)(2,1)S(1)}, u32[]{:S(2)}, u32[]{:S(2)}) %collective-permute-start.22) | collective-permute-done | bytes 131104 | tf_op jit(solution)/shard_map/ppermute | solution.py:689
  89.8 0.8 combine.1
  90.7 0.1 collective-permute-start.24
  90.8 2.1 %collective-permute-done.24.other_ref = bf16[5,256,256]{2,1,0:T(8,128)(2,1)S(1)} collective-permute-done((bf16[5,256,256]{2,1,0:T(8,128)(2,1)S(1)}, bf16[5,256,256]{2,1,0:T(8,128)(2,1)S(1)}, u32[]{:S(2)}, u32[]{:S(2)}) %collective-permute-start.24) | collective-permute-done | bytes 655392 | tf_op jit(solution)/shard_map/ppermute | solution.py:692
  92.9 0.2 add.1
  93.0 3.3 %collective-permute-start.25 = (bf16[256,256]{1,0:T(8,128)(2,1)S(1)}, bf16[256,256]{1,0:T(8,128)(2,1)S(1)}, u32[]{:S(2)}, u32[]{:S(2)}) collective-permute-start(bf16[256,256]{1,0:T(8,128)(2,1)S(1)} %get-tuple-element.120), channel_id=1, source_target_pairs={{0,2},{1,3},{2,4},{3,5},{4,6},{5,7},{6,0},{7,1},{8,10},{9,11},{10,... | collective-permute-start | bytes 393224 | tf_op jit(solution)/shard_map/ppermute | solution.py:689
  96.3 1.8 %collective-permute-start.26 = (bf16[256,256]{1,0:T(8,128)(2,1)S(1)}, bf16[256,256]{1,0:T(8,128)(2,1)S(1)}, u32[]{:S(2)}, u32[]{:S(2)}) collective-permute-start(bf16[256,256]{1,0:T(8,128)(2,1)S(1)} %get-tuple-element.121), channel_id=1, source_target_pairs={{0,4},{1,5},{2,6},{3,7},{4,0},{5,1},{6,2},{7,3},{8,12},{9,13},{10,... | collective-permute-start | bytes 393224 | tf_op jit(solution)/shard_map/ppermute | solution.py:689
  98.1 0.7 collective-permute-start.27
  98.8 1.5 %collective-permute-start.28 = (bf16[256,256]{1,0:T(8,128)(2,1)S(1)}, bf16[256,256]{1,0:T(8,128)(2,1)S(1)}, u32[]{:S(2)}, u32[]{:S(2)}) collective-permute-start(bf16[256,256]{1,0:T(8,128)(2,1)S(1)} %get-tuple-element.123), channel_id=1, source_target_pairs={{0,24},{1,25},{2,26},{3,27},{4,28},{5,29},{6,30},{7,31},{8,16},{9,... | collective-permute-start | bytes 393224 | tf_op jit(solution)/shard_map/ppermute | solution.py:702
  100.3 0.7 assemble.1
  101.0 1.0 collective-permute-done.25.refs_1_
  101.9 5.1 %collective-permute-done.26.refs_2_ = bf16[256,256]{1,0:T(8,128)(2,1)S(1)} collective-permute-done((bf16[256,256]{1,0:T(8,128)(2,1)S(1)}, bf16[256,256]{1,0:T(8,128)(2,1)S(1)}, u32[]{:S(2)}, u32[]{:S(2)}) %collective-permute-start.26) | collective-permute-done | bytes 131104 | tf_op jit(solution)/shard_map/ppermute | solution.py:689
  107.1 0.7 finish.1
  (16 shorter events, 0.0 us)
Async XLA Ops:
  0.6 16.3 %collective-permute-start.3 = (bf16[4096,256]{1,0:T(8,128)(2,1)}, bf16[4096,256]{1,0:T(8,128)(2,1)}, u32[]{:S(2)}, u32[]{:S(2)}) collective-permute-start(bf16[4096,256]{1,0:T(8,128)(2,1)} %refs_0_.2), channel_id=1, source_target_pairs={{0,1},{1,0},{2,3},{3,2},{4,5},{5,4},{6,7},{7,6},{8,9},{9,8},{10,11... | collective-permute-start | bytes 6291464 | tf_op jit(solution)/shard_map/ppermute | solution.py:692
  5.7 15.2 %copy-start = (bf16[4096,256]{1,0:T(8,128)(2,1)S(1)}, bf16[4096,256]{1,0:T(8,128)(2,1)}, u32[]{:S(2)}) copy-start(bf16[4096,256]{1,0:T(8,128)(2,1)} %refs_0_.2) | copy-start | bytes 6291460
  5.7 12.3 %collective-permute-start = (bf16[32,2176]{1,0:T(8,128)(2,1)S(1)}, bf16[32,2176]{1,0:T(8,128)(2,1)S(1)}, u32[]{:S(2)}, u32[]{:S(2)}) collective-permute-start(bf16[32,2176]{1,0:T(8,128)(2,1)S(1)} %get-tuple-element.64.refs_0_), channel_id=1, source_target_pairs={{0,2},{1,3},{2,4},{3,5},{4,6},{5,7},{6,0},{7,1},{8,10},{9,11},{10,... | collective-permute-start | bytes 417800 | tf_op jit(solution)/shard_map/ppermute | solution.py:689
  8.3 8.6 %collective-permute-start.4 = (bf16[128,256]{1,0:T(8,128)(2,1)S(1)}, bf16[128,256]{1,0:T(8,128)(2,1)S(1)}, u32[]{:S(2)}, u32[]{:S(2)}) collective-permute-start(bf16[128,256]{1,0:T(8,128)(2,1)S(1)} %get-tuple-element.66), channel_id=1, source_target_pairs={{0,1},{1,0},{2,3},{3,2},{4,5},{5,4},{6,7},{7,6},{8,9},{9,8},{10,11... | collective-permute-start | bytes 196616 | tf_op jit(solution)/shard_map/ppermute | solution.py:692
  8.5 14.1 %collective-permute-start.1 = (bf16[32,2176]{1,0:T(8,128)(2,1)S(1)}, bf16[32,2176]{1,0:T(8,128)(2,1)S(1)}, u32[]{:S(2)}, u32[]{:S(2)}) collective-permute-start(bf16[32,2176]{1,0:T(8,128)(2,1)S(1)} %get-tuple-element.64.refs_0_), channel_id=1, source_target_pairs={{0,4},{1,5},{2,6},{3,7},{4,0},{5,1},{6,2},{7,3},{8,12},{9,13},{10,... | collective-permute-start | bytes 417800 | tf_op jit(solution)/shard_map/ppermute | solution.py:689
  11.1 11.5 %collective-permute-start.2 = (bf16[32,2176]{1,0:T(8,128)(2,1)S(1)}, bf16[32,2176]{1,0:T(8,128)(2,1)S(1)}, u32[]{:S(2)}, u32[]{:S(2)}) collective-permute-start(bf16[32,2176]{1,0:T(8,128)(2,1)S(1)} %get-tuple-element.64.refs_0_), channel_id=1, source_target_pairs={{0,6},{1,7},{2,0},{3,1},{4,2},{5,3},{6,4},{7,5},{8,14},{9,15},{10,... | collective-permute-start | bytes 417800 | tf_op jit(solution)/shard_map/ppermute | solution.py:689
  16.9 15.2 %copy-start.1 = (bf16[256,256]{1,0:T(8,128)(2,1)S(1)}, bf16[256,256]{1,0:T(8,128)(2,1)}, u32[]{:S(2)}) copy-start(bf16[256,256]{1,0:T(8,128)(2,1)} %refs_10_.1) | copy-start | bytes 393220
  17.0 8.3 %collective-permute-start.5 = (bf16[32,2048]{1,0:T(8,128)(2,1)S(1)}, bf16[32,2048]{1,0:T(8,128)(2,1)S(1)}, u32[]{:S(2)}, u32[]{:S(2)}) collective-permute-start(bf16[32,2048]{1,0:T(8,128)(2,1)S(1)} %attend.3.refs_4_), channel_id=1, source_target_pairs={{0,2},{1,3},{2,4},{3,5},{4,6},{5,7},{6,0},{7,1},{8,10},{9,11},{10,... | collective-permute-start | bytes 393224 | tf_op jit(solution)/shard_map/ppermute | solution.py:689
  17.7 14.4 %collective-permute-start.6 = (bf16[32,2048]{1,0:T(8,128)(2,1)S(1)}, bf16[32,2048]{1,0:T(8,128)(2,1)S(1)}, u32[]{:S(2)}, u32[]{:S(2)}) collective-permute-start(bf16[32,2048]{1,0:T(8,128)(2,1)S(1)} %attend.3.refs_4_), channel_id=1, source_target_pairs={{0,4},{1,5},{2,6},{3,7},{4,0},{5,1},{6,2},{7,3},{8,12},{9,13},{10,... | collective-permute-start | bytes 393224 | tf_op jit(solution)/shard_map/ppermute | solution.py:689
  18.0 14.1 %collective-permute-start.7 = (bf16[32,2048]{1,0:T(8,128)(2,1)S(1)}, bf16[32,2048]{1,0:T(8,128)(2,1)S(1)}, u32[]{:S(2)}, u32[]{:S(2)}) collective-permute-start(bf16[32,2048]{1,0:T(8,128)(2,1)S(1)} %attend.3.refs_4_), channel_id=1, source_target_pairs={{0,6},{1,7},{2,0},{3,1},{4,2},{5,3},{6,4},{7,5},{8,14},{9,15},{10,... | collective-permute-start | bytes 393224 | tf_op jit(solution)/shard_map/ppermute | solution.py:689
  22.6 16.1 %copy-start.2 = (s32[256,8]{0,1:T(8,128)S(1)}, s32[256,8]{0,1:T(8,128)}, u32[]{:S(2)}) copy-start(s32[256,8]{0,1:T(8,128)} %param.19) | copy-start | bytes 24580
  22.6 16.1 %copy-start.3 = (f32[256,8]{0,1:T(8,128)S(1)}, f32[256,8]{0,1:T(8,128)}, u32[]{:S(2)}) copy-start(f32[256,8]{0,1:T(8,128)} %param.20) | copy-start | bytes 24580
  32.9 10.5 %collective-permute-start.8 = (bf16[128,512]{1,0:T(8,128)(2,1)S(1)}, bf16[128,512]{1,0:T(8,128)(2,1)S(1)}, u32[]{:S(2)}, u32[]{:S(2)}) collective-permute-start(bf16[128,512]{1,0:T(8,128)(2,1)S(1)} %get-tuple-element.89.refs_0_), channel_id=1, source_target_pairs={{0,2},{1,3},{2,4},{3,5},{4,6},{5,7},{6,0},{7,1},{8,10},{9,11},{10,... | collective-permute-start | bytes 393224 | tf_op jit(solution)/shard_map/ppermute | solution.py:689
  36.2 10.2 %collective-permute-start.9 = (bf16[128,512]{1,0:T(8,128)(2,1)S(1)}, bf16[128,512]{1,0:T(8,128)(2,1)S(1)}, u32[]{:S(2)}, u32[]{:S(2)}) collective-permute-start(bf16[128,512]{1,0:T(8,128)(2,1)S(1)} %get-tuple-element.89.refs_0_), channel_id=1, source_target_pairs={{0,4},{1,5},{2,6},{3,7},{4,0},{5,1},{6,2},{7,3},{8,12},{9,13},{10,... | collective-permute-start | bytes 393224 | tf_op jit(solution)/shard_map/ppermute | solution.py:689
  37.9 8.5 %collective-permute-start.10 = (bf16[128,512]{1,0:T(8,128)(2,1)S(1)}, bf16[128,512]{1,0:T(8,128)(2,1)S(1)}, u32[]{:S(2)}, u32[]{:S(2)}) collective-permute-start(bf16[128,512]{1,0:T(8,128)(2,1)S(1)} %get-tuple-element.89.refs_0_), channel_id=1, source_target_pairs={{0,6},{1,7},{2,0},{3,1},{4,2},{5,3},{6,4},{7,5},{8,14},{9,15},{10,... | collective-permute-start | bytes 393224 | tf_op jit(solution)/shard_map/ppermute | solution.py:689
  38.7 4.7 %collective-permute-start.11 = (bf16[144,256]{1,0:T(8,128)(2,1)S(1)}, bf16[144,256]{1,0:T(8,128)(2,1)S(1)}, u32[]{:S(2)}, u32[]{:S(2)}) collective-permute-start(bf16[144,256]{1,0:T(8,128)(2,1)S(1)} %get-tuple-element.77.give_ref), channel_id=1, source_target_pairs={{0,1},{1,0},{2,3},{3,2},{4,5},{5,4},{6,7},{7,6},{8,9},{9,8},{10,11... | collective-permute-start | bytes 221192 | tf_op jit(solution)/shard_map/ppermute | solution.py:692
  46.7 15.4 %collective-permute-start.14 = (bf16[128,2176]{1,0:T(8,128)(2,1)S(1)}, bf16[128,2176]{1,0:T(8,128)(2,1)S(1)}, u32[]{:S(2)}, u32[]{:S(2)}) collective-permute-start(bf16[128,2176]{1,0:T(8,128)(2,1)S(1)} %normalize.1.refs_0_), channel_id=1, source_target_pairs={{0,16},{1,9},{2,18},{3,11},{4,20},{5,13},{6,22},{7,15},{8,24},{9,1... | collective-permute-start | bytes 1671176 | tf_op jit(solution)/shard_map/ppermute | solution.py:702
  48.3 13.8 %collective-permute-start.13 = (bf16[128,2176]{1,0:T(8,128)(2,1)S(1)}, bf16[128,2176]{1,0:T(8,128)(2,1)S(1)}, u32[]{:S(2)}, u32[]{:S(2)}) collective-permute-start(bf16[128,2176]{1,0:T(8,128)(2,1)S(1)} %normalize.1.refs_0_), channel_id=1, source_target_pairs={{0,8},{1,17},{2,10},{3,19},{4,12},{5,21},{6,14},{7,23},{8,0},{9,25... | collective-permute-start | bytes 1671176 | tf_op jit(solution)/shard_map/ppermute | solution.py:702
  49.8 14.4 %collective-permute-start.12 = (bf16[128,2176]{1,0:T(8,128)(2,1)S(1)}, bf16[128,2176]{1,0:T(8,128)(2,1)S(1)}, u32[]{:S(2)}, u32[]{:S(2)}) collective-permute-start(bf16[128,2176]{1,0:T(8,128)(2,1)S(1)} %normalize.1.refs_0_), channel_id=1, source_target_pairs={{0,1},{1,0},{2,3},{3,2},{4,5},{5,4},{6,7},{7,6},{8,9},{9,8},{10,11... | collective-permute-start | bytes 1671176 | tf_op jit(solution)/shard_map/ppermute | solution.py:692
  62.1 2.1 %collective-permute-start.15 = (bf16[128,2176]{1,0:T(8,128)(2,1)S(1)}, bf16[128,2176]{1,0:T(8,128)(2,1)S(1)}, u32[]{:S(2)}, u32[]{:S(2)}) collective-permute-start(bf16[128,2176]{1,0:T(8,128)(2,1)S(1)} %collective-permute-done.14.refs_4_), channel_id=1, source_target_pairs={{0,1},{1,0},{2,3},{3,2},{4,5},{5,4},{6,7},{7,6},{8,9},{9,8},{10,11... | collective-permute-start | bytes 1671176 | tf_op jit(solution)/shard_map/ppermute | solution.py:692
  62.1 2.7 %collective-permute-start.16 = (bf16[128,2176]{1,0:T(8,128)(2,1)S(1)}, bf16[128,2176]{1,0:T(8,128)(2,1)S(1)}, u32[]{:S(2)}, u32[]{:S(2)}) collective-permute-start(bf16[128,2176]{1,0:T(8,128)(2,1)S(1)} %collective-permute-done.13.refs_2_), channel_id=1, source_target_pairs={{0,1},{1,0},{2,3},{3,2},{4,5},{5,4},{6,7},{7,6},{8,9},{9,8},{10,11... | collective-permute-start | bytes 1671176 | tf_op jit(solution)/shard_map/ppermute | solution.py:692
  62.6 9.5 %collective-permute-start.19 = (bf16[128,2176]{1,0:T(8,128)(2,1)S(1)}, bf16[128,2176]{1,0:T(8,128)(2,1)S(1)}, u32[]{:S(2)}, u32[]{:S(2)}) collective-permute-start(bf16[128,2176]{1,0:T(8,128)(2,1)S(1)} %collective-permute-done.13.refs_2_), channel_id=1, source_target_pairs={{0,16},{1,9},{2,18},{3,11},{4,20},{5,13},{6,22},{7,15},{8,24},{9,1... | collective-permute-start | bytes 1671176 | tf_op jit(solution)/shard_map/ppermute | solution.py:702
  72.2 2.4 %collective-permute-start.20 = (bf16[128,2176]{1,0:T(8,128)(2,1)S(1)}, bf16[128,2176]{1,0:T(8,128)(2,1)S(1)}, u32[]{:S(2)}, u32[]{:S(2)}) collective-permute-start(bf16[128,2176]{1,0:T(8,128)(2,1)S(1)} %collective-permute-done.19.refs_0_.rows_ref), channel_id=1, source_target_pairs={{0,1},{1,0},{2,3},{3,2},{4,5},{5,4},{6,7},{7,6},{8,9},{9,8},{10,11... | collective-permute-start | bytes 1671176 | tf_op jit(solution)/shard_map/ppermute | solution.py:692
  72.2 14.0 %collective-permute-start.17 = (bf16[128,2048]{1,0:T(8,128)(2,1)S(1)}, bf16[128,2048]{1,0:T(8,128)(2,1)S(1)}, u32[]{:S(2)}, u32[]{:S(2)}) collective-permute-start(bf16[128,2048]{1,0:T(8,128)(2,1)S(1)} %get-tuple-element.97), channel_id=1, source_target_pairs={{0,8},{1,17},{2,10},{3,19},{4,12},{5,21},{6,14},{7,23},{8,0},{9,25... | collective-permute-start | bytes 1572872 | tf_op jit(solution)/shard_map/ppermute | solution.py:702
  73.0 13.5 %collective-permute-start.18 = (bf16[128,2048]{1,0:T(8,128)(2,1)S(1)}, bf16[128,2048]{1,0:T(8,128)(2,1)S(1)}, u32[]{:S(2)}, u32[]{:S(2)}) collective-permute-start(bf16[128,2048]{1,0:T(8,128)(2,1)S(1)} %get-tuple-element.98), channel_id=1, source_target_pairs={{0,16},{1,9},{2,18},{3,11},{4,20},{5,13},{6,22},{7,15},{8,24},{9,1... | collective-permute-start | bytes 1572872 | tf_op jit(solution)/shard_map/ppermute | solution.py:702
  76.5 10.0 %collective-permute-start.21 = (bf16[128,512]{1,0:T(8,128)(2,1)S(1)}, bf16[128,512]{1,0:T(8,128)(2,1)S(1)}, u32[]{:S(2)}, u32[]{:S(2)}) collective-permute-start(bf16[128,512]{1,0:T(8,128)(2,1)S(1)} %get-tuple-element.101), channel_id=1, source_target_pairs={{0,2},{1,3},{2,4},{3,5},{4,6},{5,7},{6,0},{7,1},{8,10},{9,11},{10,... | collective-permute-start | bytes 393224 | tf_op jit(solution)/shard_map/ppermute | solution.py:689
  79.9 10.0 %collective-permute-start.22 = (bf16[128,512]{1,0:T(8,128)(2,1)S(1)}, bf16[128,512]{1,0:T(8,128)(2,1)S(1)}, u32[]{:S(2)}, u32[]{:S(2)}) collective-permute-start(bf16[128,512]{1,0:T(8,128)(2,1)S(1)} %get-tuple-element.102), channel_id=1, source_target_pairs={{0,4},{1,5},{2,6},{3,7},{4,0},{5,1},{6,2},{7,3},{8,12},{9,13},{10,... | collective-permute-start | bytes 393224 | tf_op jit(solution)/shard_map/ppermute | solution.py:689
  81.0 8.9 %collective-permute-start.23 = (bf16[128,512]{1,0:T(8,128)(2,1)S(1)}, bf16[128,512]{1,0:T(8,128)(2,1)S(1)}, u32[]{:S(2)}, u32[]{:S(2)}) collective-permute-start(bf16[128,512]{1,0:T(8,128)(2,1)S(1)} %get-tuple-element.103), channel_id=1, source_target_pairs={{0,6},{1,7},{2,0},{3,1},{4,2},{5,3},{6,4},{7,5},{8,14},{9,15},{10,... | collective-permute-start | bytes 393224 | tf_op jit(solution)/shard_map/ppermute | solution.py:689
  90.7 2.2 %collective-permute-start.24 = (bf16[5,256,256]{2,1,0:T(8,128)(2,1)S(1)}, bf16[5,256,256]{2,1,0:T(8,128)(2,1)S(1)}, u32[]{:S(2)}, u32[]{:S(2)}) collective-permute-start(bf16[5,256,256]{2,1,0:T(8,128)(2,1)S(1)} %get-tuple-element.118), channel_id=1, source_target_pairs={{0,1},{1,0},{2,3},{3,2},{4,5},{5,4},{6,7},{7,6},{8,9},{9,8},{10,11... | collective-permute-start | bytes 1966088 | tf_op jit(solution)/shard_map/ppermute | solution.py:692
  93.0 8.9 %collective-permute-start.25 = (bf16[256,256]{1,0:T(8,128)(2,1)S(1)}, bf16[256,256]{1,0:T(8,128)(2,1)S(1)}, u32[]{:S(2)}, u32[]{:S(2)}) collective-permute-start(bf16[256,256]{1,0:T(8,128)(2,1)S(1)} %get-tuple-element.120), channel_id=1, source_target_pairs={{0,2},{1,3},{2,4},{3,5},{4,6},{5,7},{6,0},{7,1},{8,10},{9,11},{10,... | collective-permute-start | bytes 393224 | tf_op jit(solution)/shard_map/ppermute | solution.py:689
  96.3 10.7 %collective-permute-start.26 = (bf16[256,256]{1,0:T(8,128)(2,1)S(1)}, bf16[256,256]{1,0:T(8,128)(2,1)S(1)}, u32[]{:S(2)}, u32[]{:S(2)}) collective-permute-start(bf16[256,256]{1,0:T(8,128)(2,1)S(1)} %get-tuple-element.121), channel_id=1, source_target_pairs={{0,4},{1,5},{2,6},{3,7},{4,0},{5,1},{6,2},{7,3},{8,12},{9,13},{10,... | collective-permute-start | bytes 393224 | tf_op jit(solution)/shard_map/ppermute | solution.py:689
  98.1 8.9 %collective-permute-start.27 = (bf16[256,256]{1,0:T(8,128)(2,1)S(1)}, bf16[256,256]{1,0:T(8,128)(2,1)S(1)}, u32[]{:S(2)}, u32[]{:S(2)}) collective-permute-start(bf16[256,256]{1,0:T(8,128)(2,1)S(1)} %get-tuple-element.122), channel_id=1, source_target_pairs={{0,6},{1,7},{2,0},{3,1},{4,2},{5,3},{6,4},{7,5},{8,14},{9,15},{10,... | collective-permute-start | bytes 393224 | tf_op jit(solution)/shard_map/ppermute | solution.py:689
  98.8 8.3 %collective-permute-start.28 = (bf16[256,256]{1,0:T(8,128)(2,1)S(1)}, bf16[256,256]{1,0:T(8,128)(2,1)S(1)}, u32[]{:S(2)}, u32[]{:S(2)}) collective-permute-start(bf16[256,256]{1,0:T(8,128)(2,1)S(1)} %get-tuple-element.123), channel_id=1, source_target_pairs={{0,24},{1,25},{2,26},{3,27},{4,28},{5,29},{6,30},{7,31},{8,16},{9,... | collective-permute-start | bytes 393224 | tf_op jit(solution)/shard_map/ppermute | solution.py:702

commit v3 on v2

--- a/solution.py
+++ b/solution.py
@@ -162,7 +162,7 @@
             pltpu.VMEM((rows, positions), jnp.float32),
             pltpu.VMEM((positions, heads * HEAD_DIM), jnp.bfloat16),
             pltpu.VMEM((positions, heads * HEAD_DIM), jnp.bfloat16),
-            pltpu.SemaphoreType.DMA((2, 2)),
+            pltpu.SemaphoreType.DMA((2, 1)),
         ],
         compiler_params=pltpu.CompilerParams(vmem_limit_bytes=LARGE_VMEM),
         name="attend",
@@ -196,8 +196,9 @@
     )(*arrays)
 
 
-def project_kernel(*refs, line, parts):
+def project_kernel(*refs, line, parts, ends):
     blocks = refs[: line * parts]
+    ends_ref = refs[line * parts]
     (
         weight_ref,
         other_weight_ref,
@@ -206,7 +207,7 @@
         message_ref,
         mine_ref,
         give_ref,
-    ) = refs[line * parts :]
+    ) = refs[line * parts + ends :]
     rows = blocks[0].shape[0]
     core_rows = line * rows
     width = weight_ref.shape[1]
@@ -214,9 +215,17 @@
     layer = member // CORES
     core = member - layer * CORES
     depth = blocks[-1].shape[1]
+
+    def take(part, k):
+        value = blocks[part * line + k][...]
+        if ends and part == 0 and k in (1, line - 1):
+            value = jnp.where(layer == (0 if k == 1 else line - 1), ends_ref[...], value)
+        return value
+
+    first = [take(0, k) for k in range(line)]
     product = other_product = 0.0
     for part in range(parts):
-        gathered = [ref[:, :depth] for ref in blocks[part * line : (part + 1) * line]]
+        gathered = [value[:, :depth] for value in first] if part == 0 else [take(part, k) for k in range(line)]
         gathered = jnp.concatenate(gathered, axis=0)
         at = slice(part * depth, (part + 1) * depth)
         product += jnp.dot(gathered, weight_ref[at, :], preferred_element_type=jnp.float32)
@@ -242,7 +251,7 @@
     gains = []
     pieces = width // GAIN_COLUMNS
     for k in range(line):
-        lines = blocks[k][:16, depth:].astype(jnp.float32)
+        lines = first[k][:16, depth:].astype(jnp.float32)
         for term in range(3):
             gains.append(
                 jnp.concatenate(
@@ -253,14 +262,14 @@
     give_ref[core_rows:, :] = jnp.concatenate(gains, axis=0).astype(jnp.bfloat16)
 
 
-def project(blocks, weight, other_weight, residual, extra, parts):
+def project(blocks, ends, weight, other_weight, residual, extra, parts):
     line = len(blocks) // parts
     core_rows = blocks[0].shape[0] * line
     width = weight.shape[1]
     vmem = pl.BlockSpec(memory_space=pltpu.VMEM)
     return pl.pallas_call(
-        functools.partial(project_kernel, line=line, parts=parts),
-        in_specs=[vmem] * (line * parts + 4),
+        functools.partial(project_kernel, line=line, parts=parts, ends=len(ends)),
+        in_specs=[vmem] * (line * parts + len(ends) + 4),
         out_specs=[vmem] * 3,
         out_shape=[
             jax.ShapeDtypeStruct((core_rows, CORES * width), jnp.bfloat16),
@@ -269,7 +278,7 @@
         ],
         compiler_params=pltpu.CompilerParams(vmem_limit_bytes=SMALL_VMEM),
         name="project",
-    )(*blocks, weight, other_weight, residual, extra)
+    )(*blocks, *ends, weight, other_weight, residual, extra)
 
 
 def three_terms(value):
@@ -682,11 +691,12 @@
     rows = queries.shape[0]
     width = out_weight.shape[1]
 
+    def along_line(value, moves):
+        pairs = [(a * CORES + c, b * CORES + c) for a, b in moves for c in range(CORES)]
+        return lax.ppermute(value, "expert", pairs)
+
     def turn(value, k):
-        pairs = [
-            (z * CORES + c, (z + k) % line * CORES + c) for z in range(line) for c in range(CORES)
-        ]
-        return lax.ppermute(value, "expert", pairs)
+        return along_line(value, [(z, (z + k) % line) for z in range(line)])
 
     def across_cores(value):
         return lax.ppermute(value, "expert", [(e, e ^ 1) for e in range(expert_size)])
@@ -718,12 +728,22 @@
             attention, other_weight, extra = lax.optimization_barrier(
                 (attention, other_weight, extra)
             )
-        blocks += [attention] + [turn(attention, k) for k in range(1, line)]
+        if part == 0 and line == 4:
+            far = turn(attention, 2)
+            down = along_line(attention, [(0, 1), (1, 2), (2, 3)])
+            up = along_line(attention, [(3, 2), (2, 1), (1, 0)])
+            blocks += [attention, down, far, up]
+        else:
+            blocks += [attention] + [turn(attention, k) for k in range(1, line)]
+    ends = []
+    if line == 4:
+        far, blocks[line] = lax.optimization_barrier((blocks[2], blocks[line]))
+        ends = [along_line(far, [(1, 0), (2, 3)])]
 
     attention, held = lax.optimization_barrier((attention, (out_weight, other_weight)))
     weight, other_weight = fetch(*held)
     message, mine_rows, give = project(
-        blocks, weight, other_weight, residual, extra, parts
+        blocks, ends, weight, other_weight, residual, extra, parts
     )
 
     message, held = lax.optimization_barrier((message, (gate_weight, up_weight, down_weight)))

time: 108 us -> 111 us (1.028)
  starting transfers between devices: 37.7 us -> 42.2 us
  waiting for transfers between devices: 42.5 us -> 40.3 us
    ppermute x15 -> x16, starting transfers between devices: 27.9 us -> 32.4 us  [along_line(): return lax.ppermute(value, 'expert', pairs)]
    ppermute x15 -> x16, waiting for transfers between devices: 22 us -> 19.7 us  [along_line(): return lax.ppermute(value, 'expert', pairs)]
  transfers between devices with their start and end apart: 29 -> 30, of which waited for: 12 -> 12; matrix products, arithmetic and copies ran while one was open for 0% -> 0% of each run, Pallas kernels for 22% -> 22%
where the time goes in v3:
time: 111 us; the launch traced here: 110 us
  starting transfers between devices  42.2 us (38%)
  waiting for transfers between devices  40.3 us (36%)
  Pallas kernels  26.7 us (24%)
    ppermute x16, starting transfers between devices, along_line(): return lax.ppermute(value, 'expert', pairs)  32.4 us
    ppermute x16, waiting for transfers between devices, along_line(): return lax.ppermute(value, 'expert', pairs)  19.7 us
    ppermute x6, waiting for transfers between devices, across_pool(): return lax.ppermute(value, ('pool', 'expert'), pairs)  17.8 us
    pallas_call x2, Pallas kernels, attend(): pl.pallas_call(functools.partial(attend_kernel, block_len=block_len, firs...  8.96 us
    ppermute x6, starting transfers between devices, across_pool(): return lax.ppermute(value, ('pool', 'expert'), pairs)  8.56 us
    pallas_call x2, Pallas kernels, run_expert(): pl.pallas_call(functools.partial(expert_kernel, count=count, top_count=to...  6.99 us
    pallas_call x2, Pallas kernels, fetch(): pl.pallas_call(functools.partial(fetch_kernel, count=count), in_specs=[pl...  5.53 us
    ppermute x8, waiting for transfers between devices, across_cores(): lax.ppermute(value, 'expert', [(e, e ^ 1) for e in range(expert_size)])  2.81 us
  transfers between devices with their start and end apart: 30, of which 12 were waited for; matrix products, arithmetic and copies ran while one was open for 0% of the time, Pallas kernels for 22%

profile of v3, /device:TPU:0, one launch (start us, length us, event | category | flops | bytes accessed | tf_op | source)
XLA Modules:
  0.0 110.0 jit_solution(12845050172953720308)
XLA Ops:
  0.6 0.5 collective-permute-start.3
  1.1 4.5 %attend.2 = (bf16[32,2176]{1,0:T(8,128)(2,1)S(1)}, bf16[128,256]{1,0:T(8,128)(2,1)S(1)}) custom-call(s32[8,32]{1,0:T(8,128)} %bitcast.10, s32[1,32]{1,0:T(1,128)} %bitcast.12, bf16[32,4096]{1,0:T(8,128)(2,1)} %query_ref.2, bf16[2048,1024]{1,0:T(8,128)(2,1)} %bitcast.8, bf16[256,256]{1,0:T(8,128)(2,1)} %refs_11_.1, f32[1,256]{1,0:T(1,128)} %bitcast.14), custom_call_target="tpu_custom_call" | custom-call | tf_op jit(solution)/shard_map/attend/pallas_call | solution.py:147
  5.7 0.0 copy-start
  5.7 3.7 %collective-permute-start.1 = (bf16[32,2176]{1,0:T(8,128)(2,1)S(1)}, bf16[32,2176]{1,0:T(8,128)(2,1)S(1)}, u32[]{:S(2)}, u32[]{:S(2)}) collective-permute-start(bf16[32,2176]{1,0:T(8,128)(2,1)S(1)} %get-tuple-element.66.refs_0_), channel_id=1, source_target_pairs={{0,4},{1,5},{2,6},{3,7},{4,0},{5,1},{6,2},{7,3},{8,12},{9,13},{10,... | collective-permute-start | bytes 417800 | tf_op jit(solution)/shard_map/ppermute | solution.py:696
  9.4 3.5 %collective-permute-start = (bf16[32,2176]{1,0:T(8,128)(2,1)S(1)}, bf16[32,2176]{1,0:T(8,128)(2,1)S(1)}, u32[]{:S(2)}, u32[]{:S(2)}) collective-permute-start(bf16[32,2176]{1,0:T(8,128)(2,1)S(1)} %get-tuple-element.66.refs_0_), channel_id=1, source_target_pairs={{0,2},{1,3},{2,4},{3,5},{4,6},{5,7},{8,10},{9,11},{10,12},{11,13},... | collective-permute-start | bytes 417800 | tf_op jit(solution)/shard_map/ppermute | solution.py:696
  12.8 0.1 collective-permute-start.4
  12.9 1.3 %collective-permute-start.2 = (bf16[32,2176]{1,0:T(8,128)(2,1)S(1)}, bf16[32,2176]{1,0:T(8,128)(2,1)S(1)}, u32[]{:S(2)}, u32[]{:S(2)}) collective-permute-start(bf16[32,2176]{1,0:T(8,128)(2,1)S(1)} %get-tuple-element.66.refs_0_), channel_id=1, source_target_pairs={{6,4},{7,5},{4,2},{5,3},{2,0},{3,1},{14,12},{15,13},{12,10},{13,11... | collective-permute-start | bytes 417800 | tf_op jit(solution)/shard_map/ppermute | solution.py:696
  14.2 4.4 %attend.3.refs_4_ = bf16[32,2048]{1,0:T(8,128)(2,1)S(1)} custom-call(s32[8,32]{1,0:T(8,128)} %bitcast.11, s32[1,32]{1,0:T(1,128)} %bitcast.13, bf16[32,4096]{1,0:T(8,128)(2,1)} %query_ref.2, bf16[2048,1024]{1,0:T(8,128)(2,1)} %bitcast.9), custom_call_target="tpu_custom_call" | custom-call | tf_op jit(solution)/shard_map/attend/pallas_call | solution.py:147
  18.7 0.0 copy-start.1
  18.7 0.0 collective-permute-done.3.refs_1_
  18.7 0.0 collective-permute-done.1.refs_2_
  18.7 1.4 %collective-permute-start.8 = (bf16[32,2176]{1,0:T(8,128)(2,1)S(1)}, bf16[32,2176]{1,0:T(8,128)(2,1)S(1)}, u32[]{:S(2)}, u32[]{:S(2)}) collective-permute-start(bf16[32,2176]{1,0:T(8,128)(2,1)S(1)} %collective-permute-done.1.refs_2_), channel_id=1, source_target_pairs={{2,0},{3,1},{4,6},{5,7},{10,8},{11,9},{12,14},{13,15},{18,16},{19,... | collective-permute-start | bytes 417800 | tf_op jit(solution)/shard_map/ppermute | solution.py:696
  20.1 2.7 %collective-permute-start.5 = (bf16[32,2048]{1,0:T(8,128)(2,1)S(1)}, bf16[32,2048]{1,0:T(8,128)(2,1)S(1)}, u32[]{:S(2)}, u32[]{:S(2)}) collective-permute-start(bf16[32,2048]{1,0:T(8,128)(2,1)S(1)} %attend.3.refs_4_), channel_id=1, source_target_pairs={{0,2},{1,3},{2,4},{3,5},{4,6},{5,7},{6,0},{7,1},{8,10},{9,11},{10,... | collective-permute-start | bytes 393224 | tf_op jit(solution)/shard_map/ppermute | solution.py:696
  22.8 1.2 %collective-permute-start.6 = (bf16[32,2048]{1,0:T(8,128)(2,1)S(1)}, bf16[32,2048]{1,0:T(8,128)(2,1)S(1)}, u32[]{:S(2)}, u32[]{:S(2)}) collective-permute-start(bf16[32,2048]{1,0:T(8,128)(2,1)S(1)} %attend.3.refs_4_), channel_id=1, source_target_pairs={{0,4},{1,5},{2,6},{3,7},{4,0},{5,1},{6,2},{7,3},{8,12},{9,13},{10,... | collective-permute-start | bytes 393224 | tf_op jit(solution)/shard_map/ppermute | solution.py:696
  24.0 2.8 %collective-permute-start.7 = (bf16[32,2048]{1,0:T(8,128)(2,1)S(1)}, bf16[32,2048]{1,0:T(8,128)(2,1)S(1)}, u32[]{:S(2)}, u32[]{:S(2)}) collective-permute-start(bf16[32,2048]{1,0:T(8,128)(2,1)S(1)} %attend.3.refs_4_), channel_id=1, source_target_pairs={{0,6},{1,7},{2,0},{3,1},{4,2},{5,3},{6,4},{7,5},{8,14},{9,15},{10,... | collective-permute-start | bytes 393224 | tf_op jit(solution)/shard_map/ppermute | solution.py:696
  26.9 1.7 %fetch.2 = (bf16[4096,256]{1,0:T(8,128)(2,1)S(1)}, bf16[4096,256]{1,0:T(8,128)(2,1)S(1)}) custom-call(bf16[4096,256]{1,0:T(8,128)(2,1)S(1)} %copy-done, bf16[4096,256]{1,0:T(8,128)(2,1)} %collective-permute-done.3.refs_1_), custom_call_target="tpu_custom_call" | custom-call | bytes 8388608 | tf_op jit(solution)/shard_map/fetch/pallas_call | solution.py:185
  28.6 0.0 copy-start.2
  28.6 0.0 copy-start.3
  28.6 0.0 collective-permute-done.2.refs_3_
  28.7 0.0 collective-permute-done.5.refs_5_
  28.7 5.0 %collective-permute-done.6.refs_6_ = bf16[32,2048]{1,0:T(8,128)(2,1)S(1)} collective-permute-done((bf16[32,2048]{1,0:T(8,128)(2,1)S(1)}, bf16[32,2048]{1,0:T(8,128)(2,1)S(1)}, u32[]{:S(2)}, u32[]{:S(2)}) %collective-permute-start.6) | collective-permute-done | bytes 131104 | tf_op jit(solution)/shard_map/ppermute | solution.py:696
  33.7 1.6 %collective-permute-done.7.refs_7_ = bf16[32,2048]{1,0:T(8,128)(2,1)S(1)} collective-permute-done((bf16[32,2048]{1,0:T(8,128)(2,1)S(1)}, bf16[32,2048]{1,0:T(8,128)(2,1)S(1)}, u32[]{:S(2)}, u32[]{:S(2)}) %collective-permute-start.7) | collective-permute-done | bytes 131104 | tf_op jit(solution)/shard_map/ppermute | solution.py:696
  35.2 0.7 project.1
  36.0 1.8 %collective-permute-start.9 = (bf16[128,512]{1,0:T(8,128)(2,1)S(1)}, bf16[128,512]{1,0:T(8,128)(2,1)S(1)}, u32[]{:S(2)}, u32[]{:S(2)}) collective-permute-start(bf16[128,512]{1,0:T(8,128)(2,1)S(1)} %get-tuple-element.93.refs_0_), channel_id=1, source_target_pairs={{0,2},{1,3},{2,4},{3,5},{4,6},{5,7},{6,0},{7,1},{8,10},{9,11},{10,... | collective-permute-start | bytes 393224 | tf_op jit(solution)/shard_map/ppermute | solution.py:696
  37.8 2.2 %collective-permute-start.10 = (bf16[128,512]{1,0:T(8,128)(2,1)S(1)}, bf16[128,512]{1,0:T(8,128)(2,1)S(1)}, u32[]{:S(2)}, u32[]{:S(2)}) collective-permute-start(bf16[128,512]{1,0:T(8,128)(2,1)S(1)} %get-tuple-element.93.refs_0_), channel_id=1, source_target_pairs={{0,4},{1,5},{2,6},{3,7},{4,0},{5,1},{6,2},{7,3},{8,12},{9,13},{10,... | collective-permute-start | bytes 393224 | tf_op jit(solution)/shard_map/ppermute | solution.py:696
  40.0 0.2 collective-permute-start.11
  40.2 0.9 lines.1
  41.1 3.8 %fetch.3 = (bf16[1,2048,768]{2,1,0:T(8,128)(2,1)S(1)}, bf16[1,2048,768]{2,1,0:T(8,128)(2,1)S(1)}, bf16[1,768,2048]{2,1,0:T(8,128)(2,1)S(1)}) custom-call(bf16[1,2048,768]{2,1,0:T(8,128)(2,1)} %refs_0_.3, bf16[1,2048,768]{2,1,0:T(8,128)(2,1)} %refs_1_, bf16[1,768,2048]{2,1,0:T(8,128)(2,1)} %refs_2_), custom_call_target="tpu_custom_call" | custom-call | bytes 18874368 | tf_op jit(solution)/shard_map/fetch/pallas_call | solution.py:185
  44.9 0.0 collective-permute-done.12.taken_ref
  44.9 3.7 %collective-permute-done.10.refs_2_ = bf16[128,512]{1,0:T(8,128)(2,1)S(1)} collective-permute-done((bf16[128,512]{1,0:T(8,128)(2,1)S(1)}, bf16[128,512]{1,0:T(8,128)(2,1)S(1)}, u32[]{:S(2)}, u32[]{:S(2)}) %collective-permute-start.10) | collective-permute-done | bytes 131104 | tf_op jit(solution)/shard_map/ppermute | solution.py:696
  48.7 0.3 normalize.1.refs_0_
  49.0 1.6 %collective-permute-start.15 = (bf16[128,2176]{1,0:T(8,128)(2,1)S(1)}, bf16[128,2176]{1,0:T(8,128)(2,1)S(1)}, u32[]{:S(2)}, u32[]{:S(2)}) collective-permute-start(bf16[128,2176]{1,0:T(8,128)(2,1)S(1)} %normalize.1.refs_0_), channel_id=1, source_target_pairs={{0,16},{1,9},{2,18},{3,11},{4,20},{5,13},{6,22},{7,15},{8,24},{9,1... | collective-permute-start | bytes 1671176 | tf_op jit(solution)/shard_map/ppermute | solution.py:712
  50.6 1.5 %collective-permute-start.14 = (bf16[128,2176]{1,0:T(8,128)(2,1)S(1)}, bf16[128,2176]{1,0:T(8,128)(2,1)S(1)}, u32[]{:S(2)}, u32[]{:S(2)}) collective-permute-start(bf16[128,2176]{1,0:T(8,128)(2,1)S(1)} %normalize.1.refs_0_), channel_id=1, source_target_pairs={{0,8},{1,17},{2,10},{3,19},{4,12},{5,21},{6,14},{7,23},{8,0},{9,25... | collective-permute-start | bytes 1671176 | tf_op jit(solution)/shard_map/ppermute | solution.py:712
  52.1 12.3 %collective-permute-done.15.refs_4_ = bf16[128,2176]{1,0:T(8,128)(2,1)S(1)} collective-permute-done((bf16[128,2176]{1,0:T(8,128)(2,1)S(1)}, bf16[128,2176]{1,0:T(8,128)(2,1)S(1)}, u32[]{:S(2)}, u32[]{:S(2)}) %collective-permute-start.15) | collective-permute-done | bytes 557088 | tf_op jit(solution)/shard_map/ppermute | solution.py:712
  64.4 0.5 collective-permute-start.17
  64.9 1.5 %collective-permute-start.20 = (bf16[128,2176]{1,0:T(8,128)(2,1)S(1)}, bf16[128,2176]{1,0:T(8,128)(2,1)S(1)}, u32[]{:S(2)}, u32[]{:S(2)}) collective-permute-start(bf16[128,2176]{1,0:T(8,128)(2,1)S(1)} %collective-permute-done.14.refs_2_), channel_id=1, source_target_pairs={{0,16},{1,9},{2,18},{3,11},{4,20},{5,13},{6,22},{7,15},{8,24},{9,1... | collective-permute-start | bytes 1671176 | tf_op jit(solution)/shard_map/ppermute | solution.py:712
  66.4 0.0 collective-permute-done.13.refs_1_
  66.4 0.0 collective-permute-done.16.refs_3_
  66.4 0.7 collective-permute-done.17.refs_5_
  67.1 5.1 %expert.2 = (bf16[128,2048]{1,0:T(8,128)(2,1)S(1)}, bf16[128,2048]{1,0:T(8,128)(2,1)S(1)}, bf16[128,2048]{1,0:T(8,128)(2,1)S(1)}) custom-call(bf16[128,2176]{1,0:T(8,128)(2,1)S(1)} %normalize.1.refs_0_, bf16[128,2176]{1,0:T(8,128)(2,1)S(1)} %collective-permute-done.13.refs_1_, bf16[128,2176]{1,0:T(8,128)(2,1)S(1)} %collective-permute-done.14.refs_2_, ...), custom_call_target="tpu_custom_call" | custom-call | flops 3623878656 | bytes 15728640 | tf_op jit(solution)/shard_map/expert/pallas_call | solution.py:479
  72.2 2.2 %collective-permute-done.20.refs_0_.rows_ref = bf16[128,2176]{1,0:T(8,128)(2,1)S(1)} collective-permute-done((bf16[128,2176]{1,0:T(8,128)(2,1)S(1)}, bf16[128,2176]{1,0:T(8,128)(2,1)S(1)}, u32[]{:S(2)}, u32[]{:S(2)}) %collective-permute-start.20) | collective-permute-done | bytes 557088 | tf_op jit(solution)/shard_map/ppermute | solution.py:712
  74.4 0.0 collective-permute-start.21
  74.4 0.9 collective-permute-start.18
  75.3 1.5 %collective-permute-start.19 = (bf16[128,2048]{1,0:T(8,128)(2,1)S(1)}, bf16[128,2048]{1,0:T(8,128)(2,1)S(1)}, u32[]{:S(2)}, u32[]{:S(2)}) collective-permute-start(bf16[128,2048]{1,0:T(8,128)(2,1)S(1)} %get-tuple-element.102), channel_id=1, source_target_pairs={{0,16},{1,9},{2,18},{3,11},{4,20},{5,13},{6,22},{7,15},{8,24},{9,1... | collective-permute-start | bytes 1572872 | tf_op jit(solution)/shard_map/ppermute | solution.py:712
  76.8 1.9 %expert.3 = (bf16[128,512]{1,0:T(8,128)(2,1)S(1)}, bf16[128,512]{1,0:T(8,128)(2,1)S(1)}, bf16[128,512]{1,0:T(8,128)(2,1)S(1)}, bf16[128,512]{1,0:T(8,128)(2,1)S(1)}) custom-call(bf16[128,2176]{1,0:T(8,128)(2,1)S(1)} %collective-permute-done.20.refs_0_.rows_ref, bf16[128,2176]{1,0:T(8,128)(2,1)S(1)} %collective-permute-done.21.refs_1_, ...), custom_call_target="tpu_custom_call" | custom-call | flops 1207959552 | bytes 11534336 | tf_op jit(solution)/shard_map/expert/pallas_call | solution.py:479
  78.7 3.4 %collective-permute-start.22 = (bf16[128,512]{1,0:T(8,128)(2,1)S(1)}, bf16[128,512]{1,0:T(8,128)(2,1)S(1)}, u32[]{:S(2)}, u32[]{:S(2)}) collective-permute-start(bf16[128,512]{1,0:T(8,128)(2,1)S(1)} %get-tuple-element.105), channel_id=1, source_target_pairs={{0,2},{1,3},{2,4},{3,5},{4,6},{5,7},{6,0},{7,1},{8,10},{9,11},{10,... | collective-permute-start | bytes 393224 | tf_op jit(solution)/shard_map/ppermute | solution.py:696
  82.1 0.3 collective-permute-start.23
  82.5 2.1 %collective-permute-start.24 = (bf16[128,512]{1,0:T(8,128)(2,1)S(1)}, bf16[128,512]{1,0:T(8,128)(2,1)S(1)}, u32[]{:S(2)}, u32[]{:S(2)}) collective-permute-start(bf16[128,512]{1,0:T(8,128)(2,1)S(1)} %get-tuple-element.107), channel_id=1, source_target_pairs={{0,6},{1,7},{2,0},{3,1},{4,2},{5,3},{6,4},{7,5},{8,14},{9,15},{10,... | collective-permute-start | bytes 393224 | tf_op jit(solution)/shard_map/ppermute | solution.py:696
  84.6 0.9 plan.1
  85.5 3.0 %collective-permute-done.18.refs_1_ = bf16[128,2048]{1,0:T(8,128)(2,1)S(1)} collective-permute-done((bf16[128,2048]{1,0:T(8,128)(2,1)S(1)}, bf16[128,2048]{1,0:T(8,128)(2,1)S(1)}, u32[]{:S(2)}, u32[]{:S(2)}) %collective-permute-start.18) | collective-permute-done | bytes 524320 | tf_op jit(solution)/shard_map/ppermute | solution.py:712
  88.5 0.3 collective-permute-done.19.refs_2_
  88.8 2.9 %collective-permute-done.23.refs_8_ = bf16[128,512]{1,0:T(8,128)(2,1)S(1)} collective-permute-done((bf16[128,512]{1,0:T(8,128)(2,1)S(1)}, bf16[128,512]{1,0:T(8,128)(2,1)S(1)}, u32[]{:S(2)}, u32[]{:S(2)}) %collective-permute-start.23) | collective-permute-done | bytes 131104 | tf_op jit(solution)/shard_map/ppermute | solution.py:696
  91.6 0.8 combine.1
  92.5 0.1 collective-permute-start.25
  92.6 2.1 %collective-permute-done.25.other_ref = bf16[5,256,256]{2,1,0:T(8,128)(2,1)S(1)} collective-permute-done((bf16[5,256,256]{2,1,0:T(8,128)(2,1)S(1)}, bf16[5,256,256]{2,1,0:T(8,128)(2,1)S(1)}, u32[]{:S(2)}, u32[]{:S(2)}) %collective-permute-start.25) | collective-permute-done | bytes 655392 | tf_op jit(solution)/shard_map/ppermute | solution.py:702
  94.6 0.2 add.1
  94.8 3.3 %collective-permute-start.26 = (bf16[256,256]{1,0:T(8,128)(2,1)S(1)}, bf16[256,256]{1,0:T(8,128)(2,1)S(1)}, u32[]{:S(2)}, u32[]{:S(2)}) collective-permute-start(bf16[256,256]{1,0:T(8,128)(2,1)S(1)} %get-tuple-element.124), channel_id=1, source_target_pairs={{0,2},{1,3},{2,4},{3,5},{4,6},{5,7},{6,0},{7,1},{8,10},{9,11},{10,... | collective-permute-start | bytes 393224 | tf_op jit(solution)/shard_map/ppermute | solution.py:696
  98.1 2.2 %collective-permute-start.27 = (bf16[256,256]{1,0:T(8,128)(2,1)S(1)}, bf16[256,256]{1,0:T(8,128)(2,1)S(1)}, u32[]{:S(2)}, u32[]{:S(2)}) collective-permute-start(bf16[256,256]{1,0:T(8,128)(2,1)S(1)} %get-tuple-element.125), channel_id=1, source_target_pairs={{0,4},{1,5},{2,6},{3,7},{4,0},{5,1},{6,2},{7,3},{8,12},{9,13},{10,... | collective-permute-start | bytes 393224 | tf_op jit(solution)/shard_map/ppermute | solution.py:696
  100.4 0.2 collective-permute-start.28
  100.6 1.6 %collective-permute-start.29 = (bf16[256,256]{1,0:T(8,128)(2,1)S(1)}, bf16[256,256]{1,0:T(8,128)(2,1)S(1)}, u32[]{:S(2)}, u32[]{:S(2)}) collective-permute-start(bf16[256,256]{1,0:T(8,128)(2,1)S(1)} %get-tuple-element.127), channel_id=1, source_target_pairs={{0,24},{1,25},{2,26},{3,27},{4,28},{5,29},{6,30},{7,31},{8,16},{9,... | collective-permute-start | bytes 393224 | tf_op jit(solution)/shard_map/ppermute | solution.py:712
  102.1 0.7 assemble.1
  102.8 1.4 %collective-permute-done.26.refs_1_ = bf16[256,256]{1,0:T(8,128)(2,1)S(1)} collective-permute-done((bf16[256,256]{1,0:T(8,128)(2,1)S(1)}, bf16[256,256]{1,0:T(8,128)(2,1)S(1)}, u32[]{:S(2)}, u32[]{:S(2)}) %collective-permute-start.26) | collective-permute-done | bytes 131104 | tf_op jit(solution)/shard_map/ppermute | solution.py:696
  104.2 5.1 %collective-permute-done.27.refs_2_ = bf16[256,256]{1,0:T(8,128)(2,1)S(1)} collective-permute-done((bf16[256,256]{1,0:T(8,128)(2,1)S(1)}, bf16[256,256]{1,0:T(8,128)(2,1)S(1)}, u32[]{:S(2)}, u32[]{:S(2)}) %collective-permute-start.27) | collective-permute-done | bytes 131104 | tf_op jit(solution)/shard_map/ppermute | solution.py:696
  109.3 0.7 finish.1
  (18 shorter events, 0.0 us)
Async XLA Ops:
  0.6 18.1 %collective-permute-start.3 = (bf16[4096,256]{1,0:T(8,128)(2,1)}, bf16[4096,256]{1,0:T(8,128)(2,1)}, u32[]{:S(2)}, u32[]{:S(2)}) collective-permute-start(bf16[4096,256]{1,0:T(8,128)(2,1)} %refs_0_.2), channel_id=1, source_target_pairs={{0,1},{1,0},{2,3},{3,2},{4,5},{5,4},{6,7},{7,6},{8,9},{9,8},{10,11... | collective-permute-start | bytes 6291464 | tf_op jit(solution)/shard_map/ppermute | solution.py:702
  5.7 21.2 %copy-start = (bf16[4096,256]{1,0:T(8,128)(2,1)S(1)}, bf16[4096,256]{1,0:T(8,128)(2,1)}, u32[]{:S(2)}) copy-start(bf16[4096,256]{1,0:T(8,128)(2,1)} %refs_0_.2) | copy-start | bytes 6291460
  5.7 13.0 %collective-permute-start.1 = (bf16[32,2176]{1,0:T(8,128)(2,1)S(1)}, bf16[32,2176]{1,0:T(8,128)(2,1)S(1)}, u32[]{:S(2)}, u32[]{:S(2)}) collective-permute-start(bf16[32,2176]{1,0:T(8,128)(2,1)S(1)} %get-tuple-element.66.refs_0_), channel_id=1, source_target_pairs={{0,4},{1,5},{2,6},{3,7},{4,0},{5,1},{6,2},{7,3},{8,12},{9,13},{10,... | collective-permute-start | bytes 417800 | tf_op jit(solution)/shard_map/ppermute | solution.py:696
  9.4 14.7 %collective-permute-start = (bf16[32,2176]{1,0:T(8,128)(2,1)S(1)}, bf16[32,2176]{1,0:T(8,128)(2,1)S(1)}, u32[]{:S(2)}, u32[]{:S(2)}) collective-permute-start(bf16[32,2176]{1,0:T(8,128)(2,1)S(1)} %get-tuple-element.66.refs_0_), channel_id=1, source_target_pairs={{0,2},{1,3},{2,4},{3,5},{4,6},{5,7},{8,10},{9,11},{10,12},{11,13},... | collective-permute-start | bytes 417800 | tf_op jit(solution)/shard_map/ppermute | solution.py:696
  12.8 5.8 %collective-permute-start.4 = (bf16[128,256]{1,0:T(8,128)(2,1)S(1)}, bf16[128,256]{1,0:T(8,128)(2,1)S(1)}, u32[]{:S(2)}, u32[]{:S(2)}) collective-permute-start(bf16[128,256]{1,0:T(8,128)(2,1)S(1)} %get-tuple-element.68), channel_id=1, source_target_pairs={{0,1},{1,0},{2,3},{3,2},{4,5},{5,4},{6,7},{7,6},{8,9},{9,8},{10,11... | collective-permute-start | bytes 196616 | tf_op jit(solution)/shard_map/ppermute | solution.py:702
  12.9 15.7 %collective-permute-start.2 = (bf16[32,2176]{1,0:T(8,128)(2,1)S(1)}, bf16[32,2176]{1,0:T(8,128)(2,1)S(1)}, u32[]{:S(2)}, u32[]{:S(2)}) collective-permute-start(bf16[32,2176]{1,0:T(8,128)(2,1)S(1)} %get-tuple-element.66.refs_0_), channel_id=1, source_target_pairs={{6,4},{7,5},{4,2},{5,3},{2,0},{3,1},{14,12},{15,13},{12,10},{13,11... | collective-permute-start | bytes 417800 | tf_op jit(solution)/shard_map/ppermute | solution.py:696
  18.7 16.6 %copy-start.1 = (bf16[256,256]{1,0:T(8,128)(2,1)S(1)}, bf16[256,256]{1,0:T(8,128)(2,1)}, u32[]{:S(2)}) copy-start(bf16[256,256]{1,0:T(8,128)(2,1)} %refs_11_.1) | copy-start | bytes 393220
  18.7 16.5 %collective-permute-start.8 = (bf16[32,2176]{1,0:T(8,128)(2,1)S(1)}, bf16[32,2176]{1,0:T(8,128)(2,1)S(1)}, u32[]{:S(2)}, u32[]{:S(2)}) collective-permute-start(bf16[32,2176]{1,0:T(8,128)(2,1)S(1)} %collective-permute-done.1.refs_2_), channel_id=1, source_target_pairs={{2,0},{3,1},{4,6},{5,7},{10,8},{11,9},{12,14},{13,15},{18,16},{19,... | collective-permute-start | bytes 417800 | tf_op jit(solution)/shard_map/ppermute | solution.py:696
  20.1 8.5 %collective-permute-start.5 = (bf16[32,2048]{1,0:T(8,128)(2,1)S(1)}, bf16[32,2048]{1,0:T(8,128)(2,1)S(1)}, u32[]{:S(2)}, u32[]{:S(2)}) collective-permute-start(bf16[32,2048]{1,0:T(8,128)(2,1)S(1)} %attend.3.refs_4_), channel_id=1, source_target_pairs={{0,2},{1,3},{2,4},{3,5},{4,6},{5,7},{6,0},{7,1},{8,10},{9,11},{10,... | collective-permute-start | bytes 393224 | tf_op jit(solution)/shard_map/ppermute | solution.py:696
  22.8 10.8 %collective-permute-start.6 = (bf16[32,2048]{1,0:T(8,128)(2,1)S(1)}, bf16[32,2048]{1,0:T(8,128)(2,1)S(1)}, u32[]{:S(2)}, u32[]{:S(2)}) collective-permute-start(bf16[32,2048]{1,0:T(8,128)(2,1)S(1)} %attend.3.refs_4_), channel_id=1, source_target_pairs={{0,4},{1,5},{2,6},{3,7},{4,0},{5,1},{6,2},{7,3},{8,12},{9,13},{10,... | collective-permute-start | bytes 393224 | tf_op jit(solution)/shard_map/ppermute | solution.py:696
  24.0 11.2 %collective-permute-start.7 = (bf16[32,2048]{1,0:T(8,128)(2,1)S(1)}, bf16[32,2048]{1,0:T(8,128)(2,1)S(1)}, u32[]{:S(2)}, u32[]{:S(2)}) collective-permute-start(bf16[32,2048]{1,0:T(8,128)(2,1)S(1)} %attend.3.refs_4_), channel_id=1, source_target_pairs={{0,6},{1,7},{2,0},{3,1},{4,2},{5,3},{6,4},{7,5},{8,14},{9,15},{10,... | collective-permute-start | bytes 393224 | tf_op jit(solution)/shard_map/ppermute | solution.py:696
  28.6 11.6 %copy-start.2 = (s32[256,8]{0,1:T(8,128)S(1)}, s32[256,8]{0,1:T(8,128)}, u32[]{:S(2)}) copy-start(s32[256,8]{0,1:T(8,128)} %param.19) | copy-start | bytes 24580
  28.6 11.6 %copy-start.3 = (f32[256,8]{0,1:T(8,128)S(1)}, f32[256,8]{0,1:T(8,128)}, u32[]{:S(2)}) copy-start(f32[256,8]{0,1:T(8,128)} %param.20) | copy-start | bytes 24580
  36.0 8.9 %collective-permute-start.9 = (bf16[128,512]{1,0:T(8,128)(2,1)S(1)}, bf16[128,512]{1,0:T(8,128)(2,1)S(1)}, u32[]{:S(2)}, u32[]{:S(2)}) collective-permute-start(bf16[128,512]{1,0:T(8,128)(2,1)S(1)} %get-tuple-element.93.refs_0_), channel_id=1, source_target_pairs={{0,2},{1,3},{2,4},{3,5},{4,6},{5,7},{6,0},{7,1},{8,10},{9,11},{10,... | collective-permute-start | bytes 393224 | tf_op jit(solution)/shard_map/ppermute | solution.py:696
  37.8 10.9 %collective-permute-start.10 = (bf16[128,512]{1,0:T(8,128)(2,1)S(1)}, bf16[128,512]{1,0:T(8,128)(2,1)S(1)}, u32[]{:S(2)}, u32[]{:S(2)}) collective-permute-start(bf16[128,512]{1,0:T(8,128)(2,1)S(1)} %get-tuple-element.93.refs_0_), channel_id=1, source_target_pairs={{0,4},{1,5},{2,6},{3,7},{4,0},{5,1},{6,2},{7,3},{8,12},{9,13},{10,... | collective-permute-start | bytes 393224 | tf_op jit(solution)/shard_map/ppermute | solution.py:696
  40.0 8.7 %collective-permute-start.11 = (bf16[128,512]{1,0:T(8,128)(2,1)S(1)}, bf16[128,512]{1,0:T(8,128)(2,1)S(1)}, u32[]{:S(2)}, u32[]{:S(2)}) collective-permute-start(bf16[128,512]{1,0:T(8,128)(2,1)S(1)} %get-tuple-element.93.refs_0_), channel_id=1, source_target_pairs={{0,6},{1,7},{2,0},{3,1},{4,2},{5,3},{6,4},{7,5},{8,14},{9,15},{10,... | collective-permute-start | bytes 393224 | tf_op jit(solution)/shard_map/ppermute | solution.py:696
  40.2 4.7 %collective-permute-start.12 = (bf16[144,256]{1,0:T(8,128)(2,1)S(1)}, bf16[144,256]{1,0:T(8,128)(2,1)S(1)}, u32[]{:S(2)}, u32[]{:S(2)}) collective-permute-start(bf16[144,256]{1,0:T(8,128)(2,1)S(1)} %get-tuple-element.81.give_ref), channel_id=1, source_target_pairs={{0,1},{1,0},{2,3},{3,2},{4,5},{5,4},{6,7},{7,6},{8,9},{9,8},{10,11... | collective-permute-start | bytes 221192 | tf_op jit(solution)/shard_map/ppermute | solution.py:702
  49.0 15.4 %collective-permute-start.15 = (bf16[128,2176]{1,0:T(8,128)(2,1)S(1)}, bf16[128,2176]{1,0:T(8,128)(2,1)S(1)}, u32[]{:S(2)}, u32[]{:S(2)}) collective-permute-start(bf16[128,2176]{1,0:T(8,128)(2,1)S(1)} %normalize.1.refs_0_), channel_id=1, source_target_pairs={{0,16},{1,9},{2,18},{3,11},{4,20},{5,13},{6,22},{7,15},{8,24},{9,1... | collective-permute-start | bytes 1671176 | tf_op jit(solution)/shard_map/ppermute | solution.py:712
  50.6 13.8 %collective-permute-start.14 = (bf16[128,2176]{1,0:T(8,128)(2,1)S(1)}, bf16[128,2176]{1,0:T(8,128)(2,1)S(1)}, u32[]{:S(2)}, u32[]{:S(2)}) collective-permute-start(bf16[128,2176]{1,0:T(8,128)(2,1)S(1)} %normalize.1.refs_0_), channel_id=1, source_target_pairs={{0,8},{1,17},{2,10},{3,19},{4,12},{5,21},{6,14},{7,23},{8,0},{9,25... | collective-permute-start | bytes 1671176 | tf_op jit(solution)/shard_map/ppermute | solution.py:712
  52.1 14.4 %collective-permute-start.13 = (bf16[128,2176]{1,0:T(8,128)(2,1)S(1)}, bf16[128,2176]{1,0:T(8,128)(2,1)S(1)}, u32[]{:S(2)}, u32[]{:S(2)}) collective-permute-start(bf16[128,2176]{1,0:T(8,128)(2,1)S(1)} %normalize.1.refs_0_), channel_id=1, source_target_pairs={{0,1},{1,0},{2,3},{3,2},{4,5},{5,4},{6,7},{7,6},{8,9},{9,8},{10,11... | collective-permute-start | bytes 1671176 | tf_op jit(solution)/shard_map/ppermute | solution.py:702
  64.4 2.0 %collective-permute-start.16 = (bf16[128,2176]{1,0:T(8,128)(2,1)S(1)}, bf16[128,2176]{1,0:T(8,128)(2,1)S(1)}, u32[]{:S(2)}, u32[]{:S(2)}) collective-permute-start(bf16[128,2176]{1,0:T(8,128)(2,1)S(1)} %collective-permute-done.15.refs_4_), channel_id=1, source_target_pairs={{0,1},{1,0},{2,3},{3,2},{4,5},{5,4},{6,7},{7,6},{8,9},{9,8},{10,11... | collective-permute-start | bytes 1671176 | tf_op jit(solution)/shard_map/ppermute | solution.py:702
  64.4 2.7 %collective-permute-start.17 = (bf16[128,2176]{1,0:T(8,128)(2,1)S(1)}, bf16[128,2176]{1,0:T(8,128)(2,1)S(1)}, u32[]{:S(2)}, u32[]{:S(2)}) collective-permute-start(bf16[128,2176]{1,0:T(8,128)(2,1)S(1)} %collective-permute-done.14.refs_2_), channel_id=1, source_target_pairs={{0,1},{1,0},{2,3},{3,2},{4,5},{5,4},{6,7},{7,6},{8,9},{9,8},{10,11... | collective-permute-start | bytes 1671176 | tf_op jit(solution)/shard_map/ppermute | solution.py:702
  64.9 9.5 %collective-permute-start.20 = (bf16[128,2176]{1,0:T(8,128)(2,1)S(1)}, bf16[128,2176]{1,0:T(8,128)(2,1)S(1)}, u32[]{:S(2)}, u32[]{:S(2)}) collective-permute-start(bf16[128,2176]{1,0:T(8,128)(2,1)S(1)} %collective-permute-done.14.refs_2_), channel_id=1, source_target_pairs={{0,16},{1,9},{2,18},{3,11},{4,20},{5,13},{6,22},{7,15},{8,24},{9,1... | collective-permute-start | bytes 1671176 | tf_op jit(solution)/shard_map/ppermute | solution.py:712
  74.4 2.4 %collective-permute-start.21 = (bf16[128,2176]{1,0:T(8,128)(2,1)S(1)}, bf16[128,2176]{1,0:T(8,128)(2,1)S(1)}, u32[]{:S(2)}, u32[]{:S(2)}) collective-permute-start(bf16[128,2176]{1,0:T(8,128)(2,1)S(1)} %collective-permute-done.20.refs_0_.rows_ref), channel_id=1, source_target_pairs={{0,1},{1,0},{2,3},{3,2},{4,5},{5,4},{6,7},{7,6},{8,9},{9,8},{10,11... | collective-permute-start | bytes 1671176 | tf_op jit(solution)/shard_map/ppermute | solution.py:702
  74.4 14.1 %collective-permute-start.18 = (bf16[128,2048]{1,0:T(8,128)(2,1)S(1)}, bf16[128,2048]{1,0:T(8,128)(2,1)S(1)}, u32[]{:S(2)}, u32[]{:S(2)}) collective-permute-start(bf16[128,2048]{1,0:T(8,128)(2,1)S(1)} %get-tuple-element.101), channel_id=1, source_target_pairs={{0,8},{1,17},{2,10},{3,19},{4,12},{5,21},{6,14},{7,23},{8,0},{9,25... | collective-permute-start | bytes 1572872 | tf_op jit(solution)/shard_map/ppermute | solution.py:712
  75.3 13.5 %collective-permute-start.19 = (bf16[128,2048]{1,0:T(8,128)(2,1)S(1)}, bf16[128,2048]{1,0:T(8,128)(2,1)S(1)}, u32[]{:S(2)}, u32[]{:S(2)}) collective-permute-start(bf16[128,2048]{1,0:T(8,128)(2,1)S(1)} %get-tuple-element.102), channel_id=1, source_target_pairs={{0,16},{1,9},{2,18},{3,11},{4,20},{5,13},{6,22},{7,15},{8,24},{9,1... | collective-permute-start | bytes 1572872 | tf_op jit(solution)/shard_map/ppermute | solution.py:712
  78.7 10.0 %collective-permute-start.22 = (bf16[128,512]{1,0:T(8,128)(2,1)S(1)}, bf16[128,512]{1,0:T(8,128)(2,1)S(1)}, u32[]{:S(2)}, u32[]{:S(2)}) collective-permute-start(bf16[128,512]{1,0:T(8,128)(2,1)S(1)} %get-tuple-element.105), channel_id=1, source_target_pairs={{0,2},{1,3},{2,4},{3,5},{4,6},{5,7},{6,0},{7,1},{8,10},{9,11},{10,... | collective-permute-start | bytes 393224 | tf_op jit(solution)/shard_map/ppermute | solution.py:696
  82.1 9.5 %collective-permute-start.23 = (bf16[128,512]{1,0:T(8,128)(2,1)S(1)}, bf16[128,512]{1,0:T(8,128)(2,1)S(1)}, u32[]{:S(2)}, u32[]{:S(2)}) collective-permute-start(bf16[128,512]{1,0:T(8,128)(2,1)S(1)} %get-tuple-element.106), channel_id=1, source_target_pairs={{0,4},{1,5},{2,6},{3,7},{4,0},{5,1},{6,2},{7,3},{8,12},{9,13},{10,... | collective-permute-start | bytes 393224 | tf_op jit(solution)/shard_map/ppermute | solution.py:696
  82.5 9.1 %collective-permute-start.24 = (bf16[128,512]{1,0:T(8,128)(2,1)S(1)}, bf16[128,512]{1,0:T(8,128)(2,1)S(1)}, u32[]{:S(2)}, u32[]{:S(2)}) collective-permute-start(bf16[128,512]{1,0:T(8,128)(2,1)S(1)} %get-tuple-element.107), channel_id=1, source_target_pairs={{0,6},{1,7},{2,0},{3,1},{4,2},{5,3},{6,4},{7,5},{8,14},{9,15},{10,... | collective-permute-start | bytes 393224 | tf_op jit(solution)/shard_map/ppermute | solution.py:696
  92.5 2.2 %collective-permute-start.25 = (bf16[5,256,256]{2,1,0:T(8,128)(2,1)S(1)}, bf16[5,256,256]{2,1,0:T(8,128)(2,1)S(1)}, u32[]{:S(2)}, u32[]{:S(2)}) collective-permute-start(bf16[5,256,256]{2,1,0:T(8,128)(2,1)S(1)} %get-tuple-element.122), channel_id=1, source_target_pairs={{0,1},{1,0},{2,3},{3,2},{4,5},{5,4},{6,7},{7,6},{8,9},{9,8},{10,11... | collective-permute-start | bytes 1966088 | tf_op jit(solution)/shard_map/ppermute | solution.py:702
  94.8 9.4 %collective-permute-start.26 = (bf16[256,256]{1,0:T(8,128)(2,1)S(1)}, bf16[256,256]{1,0:T(8,128)(2,1)S(1)}, u32[]{:S(2)}, u32[]{:S(2)}) collective-permute-start(bf16[256,256]{1,0:T(8,128)(2,1)S(1)} %get-tuple-element.124), channel_id=1, source_target_pairs={{0,2},{1,3},{2,4},{3,5},{4,6},{5,7},{6,0},{7,1},{8,10},{9,11},{10,... | collective-permute-start | bytes 393224 | tf_op jit(solution)/shard_map/ppermute | solution.py:696
  98.1 11.2 %collective-permute-start.27 = (bf16[256,256]{1,0:T(8,128)(2,1)S(1)}, bf16[256,256]{1,0:T(8,128)(2,1)S(1)}, u32[]{:S(2)}, u32[]{:S(2)}) collective-permute-start(bf16[256,256]{1,0:T(8,128)(2,1)S(1)} %get-tuple-element.125), channel_id=1, source_target_pairs={{0,4},{1,5},{2,6},{3,7},{4,0},{5,1},{6,2},{7,3},{8,12},{9,13},{10,... | collective-permute-start | bytes 393224 | tf_op jit(solution)/shard_map/ppermute | solution.py:696
  100.4 8.9 %collective-permute-start.28 = (bf16[256,256]{1,0:T(8,128)(2,1)S(1)}, bf16[256,256]{1,0:T(8,128)(2,1)S(1)}, u32[]{:S(2)}, u32[]{:S(2)}) collective-permute-start(bf16[256,256]{1,0:T(8,128)(2,1)S(1)} %get-tuple-element.126), channel_id=1, source_target_pairs={{0,6},{1,7},{2,0},{3,1},{4,2},{5,3},{6,4},{7,5},{8,14},{9,15},{10,... | collective-permute-start | bytes 393224 | tf_op jit(solution)/shard_map/ppermute | solution.py:696
  100.6 8.7 %collective-permute-start.29 = (bf16[256,256]{1,0:T(8,128)(2,1)S(1)}, bf16[256,256]{1,0:T(8,128)(2,1)S(1)}, u32[]{:S(2)}, u32[]{:S(2)}) collective-permute-start(bf16[256,256]{1,0:T(8,128)(2,1)S(1)} %get-tuple-element.127), channel_id=1, source_target_pairs={{0,24},{1,25},{2,26},{3,27},{4,28},{5,29},{6,30},{7,31},{8,16},{9,... | collective-permute-start | bytes 393224 | tf_op jit(solution)/shard_map/ppermute | solution.py:712

commit v4 on v2

--- a/solution.py
+++ b/solution.py
@@ -19,6 +19,10 @@
 FETCH_VMEM = 46 * 2**20
 
 epsilon = 1e-06
+
+
+def line_order(line):
+    return [0] + sorted(range(1, line), key=lambda k: -min(k, line - k))
 
 
 def prepare(residual_ref, gain_ref, out_ref, columns_ref):
@@ -225,8 +229,8 @@
         )
     here = pl.ds(pl.multiple_of(core * width, width), width)
     there = pl.ds(pl.multiple_of((1 - core) * width, width), width)
-    for k in range(line):
-        z = layer - k
+    for k, step in enumerate(line_order(line)):
+        z = layer - step
         z = jnp.where(z < 0, z + line, z)
         at = pl.ds(pl.multiple_of(z * rows, rows), rows)
         held = pl.ds(pl.multiple_of((z * CORES + core) * rows, rows), rows)
@@ -340,8 +344,9 @@
         attended = block[...].astype(jnp.float32)
         squares = squares + jnp.sum(attended * attended, axis=1, keepdims=True)
     inverse = lax.rsqrt(squares / features + epsilon)
-    for k, block in enumerate(blocks):
-        z = layer - k
+    for step, block in enumerate(blocks):
+        k = line_order(line).index(step)
+        z = layer - step
         z = jnp.where(z < 0, z + line, z)
         at = pl.ds(pl.multiple_of(z * width, width), width)
         attended = block[...].astype(jnp.float32)
@@ -688,6 +693,9 @@
         ]
         return lax.ppermute(value, "expert", pairs)
 
+    def turn_all(values):
+        return [turn(values[k], k) if k else values[0] for k in line_order(line)]
+
     def across_cores(value):
         return lax.ppermute(value, "expert", [(e, e ^ 1) for e in range(expert_size)])
 
@@ -718,7 +726,7 @@
             attention, other_weight, extra = lax.optimization_barrier(
                 (attention, other_weight, extra)
             )
-        blocks += [attention] + [turn(attention, k) for k in range(1, line)]
+        blocks += turn_all([attention] * line)
 
     attention, held = lax.optimization_barrier((attention, (out_weight, other_weight)))
     weight, other_weight = fetch(*held)
@@ -753,12 +761,14 @@
     results = run_expert(
         [(far, across_cores(far))], weights, capacity, top_count, line, [[k] for k in steps]
     )[0]
-    far_results = [turn(part, k) if k else part for k, part in enumerate(results)]
+    far_results = turn_all(results)
     far_chosen = plan_far(far, normed.shape[1] - ID_COLUMNS, top_count, line, capacity)
     returned = [across_pool(near[j], j) for j in range(1, last)]
     returned, far_results = lax.optimization_barrier((returned, far_results))
     returned = [near[0]] + returned
-    mine, other = combine(returned, chosen, far_results, far_chosen, line)
+    mine, other = combine(
+        returned, chosen, far_results, [far_chosen[k] for k in line_order(line)], line
+    )
     *summed, far_sum = add(mine, across_cores(other))
     landed = [turn(rows, k) if k else rows for k, rows in enumerate(summed)]
     final = finish(landed + [across_pool(far_sum, last)])

time: 108 us -> 107 us (level)
  waiting for transfers between devices: 42.5 us -> 38.8 us
  starting transfers between devices: 37.7 us -> 40.4 us
    ppermute x15, waiting for transfers between devices: 22 us -> 19 us  [turn(): return lax.ppermute(value, 'expert', pairs)]
    ppermute x15, starting transfers between devices: 27.9 us -> 30.6 us  [turn(): return lax.ppermute(value, 'expert', pairs)]
  transfers between devices with their start and end apart: 29 -> 29, of which waited for: 12 -> 13; matrix products, arithmetic and copies ran while one was open for 0% -> 0% of each run, Pallas kernels for 22% -> 22%
where the time goes in v4:
time: 107 us
  starting transfers between devices  40.4 us (38%)
  waiting for transfers between devices  38.8 us (36%)
  Pallas kernels  26.7 us (25%)
    ppermute x15, starting transfers between devices, turn(): return lax.ppermute(value, 'expert', pairs)  30.6 us
    ppermute x15, waiting for transfers between devices, turn(): return lax.ppermute(value, 'expert', pairs)  19 us
    ppermute x6, waiting for transfers between devices, across_pool(): return lax.ppermute(value, ('pool', 'expert'), pairs)  17 us
    pallas_call x2, Pallas kernels, attend(): pl.pallas_call(functools.partial(attend_kernel, block_len=block_len, firs...  8.96 us
    ppermute x6, starting transfers between devices, across_pool(): return lax.ppermute(value, ('pool', 'expert'), pairs)  8.53 us
    pallas_call x2, Pallas kernels, run_expert(): pl.pallas_call(functools.partial(expert_kernel, count=count, top_count=to...  6.98 us
    pallas_call x2, Pallas kernels, fetch(): pl.pallas_call(functools.partial(fetch_kernel, count=count), in_specs=[pl...  5.53 us
    ppermute x8, waiting for transfers between devices, across_cores(): lax.ppermute(value, 'expert', [(e, e ^ 1) for e in range(expert_size)])  2.81 us
  transfers between devices with their start and end apart: 29, of which 13 were waited for; matrix products, arithmetic and copies ran while one was open for 0% of the time, Pallas kernels for 22%

profile of v4, /device:TPU:0, one launch (start us, length us, event | category | flops | bytes accessed | tf_op | source)
XLA Modules:
  0.0 106.8 jit_solution(5264028005413887602)
XLA Ops:
  0.6 0.5 collective-permute-start.3
  1.1 4.5 %attend.2 = (bf16[32,2176]{1,0:T(8,128)(2,1)S(1)}, bf16[128,256]{1,0:T(8,128)(2,1)S(1)}) custom-call(s32[8,32]{1,0:T(8,128)} %bitcast.10, s32[1,32]{1,0:T(1,128)} %bitcast.12, bf16[32,4096]{1,0:T(8,128)(2,1)} %query_ref.2, bf16[2048,1024]{1,0:T(8,128)(2,1)} %bitcast.8, bf16[256,256]{1,0:T(8,128)(2,1)} %refs_10_.1, f32[1,256]{1,0:T(1,128)} %bitcast.14), custom_call_target="tpu_custom_call" | custom-call | tf_op jit(solution)/shard_map/attend/pallas_call | solution.py:151
  5.7 0.0 copy-start
  5.7 3.7 %collective-permute-start = (bf16[32,2176]{1,0:T(8,128)(2,1)S(1)}, bf16[32,2176]{1,0:T(8,128)(2,1)S(1)}, u32[]{:S(2)}, u32[]{:S(2)}) collective-permute-start(bf16[32,2176]{1,0:T(8,128)(2,1)S(1)} %get-tuple-element.64.refs_0_), channel_id=1, source_target_pairs={{0,4},{1,5},{2,6},{3,7},{4,0},{5,1},{6,2},{7,3},{8,12},{9,13},{10,... | collective-permute-start | bytes 417800 | tf_op jit(solution)/shard_map/ppermute | solution.py:694
  9.4 0.2 collective-permute-start.4
  9.6 1.6 %collective-permute-start.1 = (bf16[32,2176]{1,0:T(8,128)(2,1)S(1)}, bf16[32,2176]{1,0:T(8,128)(2,1)S(1)}, u32[]{:S(2)}, u32[]{:S(2)}) collective-permute-start(bf16[32,2176]{1,0:T(8,128)(2,1)S(1)} %get-tuple-element.64.refs_0_), channel_id=1, source_target_pairs={{0,2},{1,3},{2,4},{3,5},{4,6},{5,7},{6,0},{7,1},{8,10},{9,11},{10,... | collective-permute-start | bytes 417800 | tf_op jit(solution)/shard_map/ppermute | solution.py:694
  11.1 2.2 %collective-permute-start.2 = (bf16[32,2176]{1,0:T(8,128)(2,1)S(1)}, bf16[32,2176]{1,0:T(8,128)(2,1)S(1)}, u32[]{:S(2)}, u32[]{:S(2)}) collective-permute-start(bf16[32,2176]{1,0:T(8,128)(2,1)S(1)} %get-tuple-element.64.refs_0_), channel_id=1, source_target_pairs={{0,6},{1,7},{2,0},{3,1},{4,2},{5,3},{6,4},{7,5},{8,14},{9,15},{10,... | collective-permute-start | bytes 417800 | tf_op jit(solution)/shard_map/ppermute | solution.py:694
  13.4 4.4 %attend.3.refs_4_ = bf16[32,2048]{1,0:T(8,128)(2,1)S(1)} custom-call(s32[8,32]{1,0:T(8,128)} %bitcast.11, s32[1,32]{1,0:T(1,128)} %bitcast.13, bf16[32,4096]{1,0:T(8,128)(2,1)} %query_ref.2, bf16[2048,1024]{1,0:T(8,128)(2,1)} %bitcast.9), custom_call_target="tpu_custom_call" | custom-call | tf_op jit(solution)/shard_map/attend/pallas_call | solution.py:151
  17.8 0.0 copy-start.1
  17.9 0.0 collective-permute-done.4.refs_11_
  17.9 0.1 collective-permute-start.5
  17.9 0.6 collective-permute-start.6
  18.5 1.4 %collective-permute-done.refs_1_ = bf16[32,2176]{1,0:T(8,128)(2,1)S(1)} collective-permute-done((bf16[32,2176]{1,0:T(8,128)(2,1)S(1)}, bf16[32,2176]{1,0:T(8,128)(2,1)S(1)}, u32[]{:S(2)}, u32[]{:S(2)}) %collective-permute-start) | collective-permute-done | bytes 139296 | tf_op jit(solution)/shard_map/ppermute | solution.py:694
  19.9 1.9 %collective-permute-start.7 = (bf16[32,2048]{1,0:T(8,128)(2,1)S(1)}, bf16[32,2048]{1,0:T(8,128)(2,1)S(1)}, u32[]{:S(2)}, u32[]{:S(2)}) collective-permute-start(bf16[32,2048]{1,0:T(8,128)(2,1)S(1)} %attend.3.refs_4_), channel_id=1, source_target_pairs={{0,6},{1,7},{2,0},{3,1},{4,2},{5,3},{6,4},{7,5},{8,14},{9,15},{10,... | collective-permute-start | bytes 393224 | tf_op jit(solution)/shard_map/ppermute | solution.py:694
  21.8 1.7 %fetch.2 = (bf16[4096,256]{1,0:T(8,128)(2,1)S(1)}, bf16[4096,256]{1,0:T(8,128)(2,1)S(1)}) custom-call(bf16[4096,256]{1,0:T(8,128)(2,1)S(1)} %copy-done, bf16[4096,256]{1,0:T(8,128)(2,1)} %collective-permute-done.3.refs_1_), custom_call_target="tpu_custom_call" | custom-call | bytes 8388608 | tf_op jit(solution)/shard_map/fetch/pallas_call | solution.py:189
  23.6 0.0 copy-start.2
  23.6 0.0 copy-start.3
  23.6 0.0 collective-permute-done.1.refs_2_
  23.6 7.7 %collective-permute-done.5.refs_5_ = bf16[32,2048]{1,0:T(8,128)(2,1)S(1)} collective-permute-done((bf16[32,2048]{1,0:T(8,128)(2,1)S(1)}, bf16[32,2048]{1,0:T(8,128)(2,1)S(1)}, u32[]{:S(2)}, u32[]{:S(2)}) %collective-permute-start.5) | collective-permute-done | bytes 131104 | tf_op jit(solution)/shard_map/ppermute | solution.py:694
  31.3 0.7 project.1
  32.1 3.4 %collective-permute-start.8 = (bf16[128,512]{1,0:T(8,128)(2,1)S(1)}, bf16[128,512]{1,0:T(8,128)(2,1)S(1)}, u32[]{:S(2)}, u32[]{:S(2)}) collective-permute-start(bf16[128,512]{1,0:T(8,128)(2,1)S(1)} %get-tuple-element.89.refs_0_), channel_id=1, source_target_pairs={{0,2},{1,3},{2,4},{3,5},{4,6},{5,7},{6,0},{7,1},{8,10},{9,11},{10,... | collective-permute-start | bytes 393224 | tf_op jit(solution)/shard_map/ppermute | solution.py:694
  35.4 2.0 %collective-permute-start.9 = (bf16[128,512]{1,0:T(8,128)(2,1)S(1)}, bf16[128,512]{1,0:T(8,128)(2,1)S(1)}, u32[]{:S(2)}, u32[]{:S(2)}) collective-permute-start(bf16[128,512]{1,0:T(8,128)(2,1)S(1)} %get-tuple-element.89.refs_0_), channel_id=1, source_target_pairs={{0,4},{1,5},{2,6},{3,7},{4,0},{5,1},{6,2},{7,3},{8,12},{9,13},{10,... | collective-permute-start | bytes 393224 | tf_op jit(solution)/shard_map/ppermute | solution.py:694
  37.4 2.8 %collective-permute-start.10 = (bf16[128,512]{1,0:T(8,128)(2,1)S(1)}, bf16[128,512]{1,0:T(8,128)(2,1)S(1)}, u32[]{:S(2)}, u32[]{:S(2)}) collective-permute-start(bf16[128,512]{1,0:T(8,128)(2,1)S(1)} %get-tuple-element.89.refs_0_), channel_id=1, source_target_pairs={{0,6},{1,7},{2,0},{3,1},{4,2},{5,3},{6,4},{7,5},{8,14},{9,15},{10,... | collective-permute-start | bytes 393224 | tf_op jit(solution)/shard_map/ppermute | solution.py:694
  40.2 0.9 lines.1
  41.1 3.8 %fetch.3 = (bf16[1,2048,768]{2,1,0:T(8,128)(2,1)S(1)}, bf16[1,2048,768]{2,1,0:T(8,128)(2,1)S(1)}, bf16[1,768,2048]{2,1,0:T(8,128)(2,1)S(1)}) custom-call(bf16[1,2048,768]{2,1,0:T(8,128)(2,1)} %refs_0_.3, bf16[1,2048,768]{2,1,0:T(8,128)(2,1)} %refs_1_, bf16[1,768,2048]{2,1,0:T(8,128)(2,1)} %refs_2_), custom_call_target="tpu_custom_call" | custom-call | bytes 18874368 | tf_op jit(solution)/shard_map/fetch/pallas_call | solution.py:189
  44.9 0.0 collective-permute-done.11.taken_ref
  44.9 0.6 collective-permute-done.9.refs_2_
  45.5 0.0 collective-permute-done.10.refs_3_
  45.5 0.3 normalize.1.refs_0_
  45.8 1.6 %collective-permute-start.14 = (bf16[128,2176]{1,0:T(8,128)(2,1)S(1)}, bf16[128,2176]{1,0:T(8,128)(2,1)S(1)}, u32[]{:S(2)}, u32[]{:S(2)}) collective-permute-start(bf16[128,2176]{1,0:T(8,128)(2,1)S(1)} %normalize.1.refs_0_), channel_id=1, source_target_pairs={{0,16},{1,9},{2,18},{3,11},{4,20},{5,13},{6,22},{7,15},{8,24},{9,1... | collective-permute-start | bytes 1671176 | tf_op jit(solution)/shard_map/ppermute | solution.py:710
  47.4 1.5 %collective-permute-start.13 = (bf16[128,2176]{1,0:T(8,128)(2,1)S(1)}, bf16[128,2176]{1,0:T(8,128)(2,1)S(1)}, u32[]{:S(2)}, u32[]{:S(2)}) collective-permute-start(bf16[128,2176]{1,0:T(8,128)(2,1)S(1)} %normalize.1.refs_0_), channel_id=1, source_target_pairs={{0,8},{1,17},{2,10},{3,19},{4,12},{5,21},{6,14},{7,23},{8,0},{9,25... | collective-permute-start | bytes 1671176 | tf_op jit(solution)/shard_map/ppermute | solution.py:710
  48.9 0.0 collective-permute-start.12
  48.9 12.3 %collective-permute-done.14.refs_4_ = bf16[128,2176]{1,0:T(8,128)(2,1)S(1)} collective-permute-done((bf16[128,2176]{1,0:T(8,128)(2,1)S(1)}, bf16[128,2176]{1,0:T(8,128)(2,1)S(1)}, u32[]{:S(2)}, u32[]{:S(2)}) %collective-permute-start.14) | collective-permute-done | bytes 557088 | tf_op jit(solution)/shard_map/ppermute | solution.py:710
  61.2 0.0 collective-permute-start.15
  61.2 0.5 collective-permute-start.16
  61.7 1.5 %collective-permute-start.19 = (bf16[128,2176]{1,0:T(8,128)(2,1)S(1)}, bf16[128,2176]{1,0:T(8,128)(2,1)S(1)}, u32[]{:S(2)}, u32[]{:S(2)}) collective-permute-start(bf16[128,2176]{1,0:T(8,128)(2,1)S(1)} %collective-permute-done.13.refs_2_), channel_id=1, source_target_pairs={{0,16},{1,9},{2,18},{3,11},{4,20},{5,13},{6,22},{7,15},{8,24},{9,1... | collective-permute-start | bytes 1671176 | tf_op jit(solution)/shard_map/ppermute | solution.py:710
  63.2 0.0 collective-permute-done.15.refs_3_
  63.3 0.7 collective-permute-done.16.refs_5_
  64.0 5.1 %expert.2 = (bf16[128,2048]{1,0:T(8,128)(2,1)S(1)}, bf16[128,2048]{1,0:T(8,128)(2,1)S(1)}, bf16[128,2048]{1,0:T(8,128)(2,1)S(1)}) custom-call(bf16[128,2176]{1,0:T(8,128)(2,1)S(1)} %normalize.1.refs_0_, bf16[128,2176]{1,0:T(8,128)(2,1)S(1)} %collective-permute-done.12.refs_1_, bf16[128,2176]{1,0:T(8,128)(2,1)S(1)} %collective-permute-done.13.refs_2_, ...), custom_call_target="tpu_custom_call" | custom-call | flops 3623878656 | bytes 15728640 | tf_op jit(solution)/shard_map/expert/pallas_call | solution.py:475
  69.1 2.2 %collective-permute-done.19.refs_0_.rows_ref = bf16[128,2176]{1,0:T(8,128)(2,1)S(1)} collective-permute-done((bf16[128,2176]{1,0:T(8,128)(2,1)S(1)}, bf16[128,2176]{1,0:T(8,128)(2,1)S(1)}, u32[]{:S(2)}, u32[]{:S(2)}) %collective-permute-start.19) | collective-permute-done | bytes 557088 | tf_op jit(solution)/shard_map/ppermute | solution.py:710
  71.2 0.0 collective-permute-start.20
  71.3 0.9 collective-permute-start.17
  72.2 1.5 %collective-permute-start.18 = (bf16[128,2048]{1,0:T(8,128)(2,1)S(1)}, bf16[128,2048]{1,0:T(8,128)(2,1)S(1)}, u32[]{:S(2)}, u32[]{:S(2)}) collective-permute-start(bf16[128,2048]{1,0:T(8,128)(2,1)S(1)} %get-tuple-element.98), channel_id=1, source_target_pairs={{0,16},{1,9},{2,18},{3,11},{4,20},{5,13},{6,22},{7,15},{8,24},{9,1... | collective-permute-start | bytes 1572872 | tf_op jit(solution)/shard_map/ppermute | solution.py:710
  73.7 0.0 collective-permute-done.20.refs_1_
  73.7 1.9 %expert.3 = (bf16[128,512]{1,0:T(8,128)(2,1)S(1)}, bf16[128,512]{1,0:T(8,128)(2,1)S(1)}, bf16[128,512]{1,0:T(8,128)(2,1)S(1)}, bf16[128,512]{1,0:T(8,128)(2,1)S(1)}) custom-call(bf16[128,2176]{1,0:T(8,128)(2,1)S(1)} %collective-permute-done.19.refs_0_.rows_ref, bf16[128,2176]{1,0:T(8,128)(2,1)S(1)} %collective-permute-done.20.refs_1_, ...), custom_call_target="tpu_custom_call" | custom-call | flops 1207959552 | bytes 11534336 | tf_op jit(solution)/shard_map/expert/pallas_call | solution.py:475
  75.6 2.2 %collective-permute-start.21 = (bf16[128,512]{1,0:T(8,128)(2,1)S(1)}, bf16[128,512]{1,0:T(8,128)(2,1)S(1)}, u32[]{:S(2)}, u32[]{:S(2)}) collective-permute-start(bf16[128,512]{1,0:T(8,128)(2,1)S(1)} %get-tuple-element.101), channel_id=1, source_target_pairs={{0,4},{1,5},{2,6},{3,7},{4,0},{5,1},{6,2},{7,3},{8,12},{9,13},{10,... | collective-permute-start | bytes 393224 | tf_op jit(solution)/shard_map/ppermute | solution.py:694
  77.8 4.3 %collective-permute-start.22 = (bf16[128,512]{1,0:T(8,128)(2,1)S(1)}, bf16[128,512]{1,0:T(8,128)(2,1)S(1)}, u32[]{:S(2)}, u32[]{:S(2)}) collective-permute-start(bf16[128,512]{1,0:T(8,128)(2,1)S(1)} %get-tuple-element.102), channel_id=1, source_target_pairs={{0,2},{1,3},{2,4},{3,5},{4,6},{5,7},{6,0},{7,1},{8,10},{9,11},{10,... | collective-permute-start | bytes 393224 | tf_op jit(solution)/shard_map/ppermute | solution.py:694
  82.1 0.9 plan.1
  83.0 2.3 %collective-permute-done.17.refs_1_ = bf16[128,2048]{1,0:T(8,128)(2,1)S(1)} collective-permute-done((bf16[128,2048]{1,0:T(8,128)(2,1)S(1)}, bf16[128,2048]{1,0:T(8,128)(2,1)S(1)}, u32[]{:S(2)}, u32[]{:S(2)}) %collective-permute-start.17) | collective-permute-done | bytes 524320 | tf_op jit(solution)/shard_map/ppermute | solution.py:710
  85.3 0.3 collective-permute-done.18.refs_2_
  85.6 3.1 %collective-permute-done.22.refs_8_ = bf16[128,512]{1,0:T(8,128)(2,1)S(1)} collective-permute-done((bf16[128,512]{1,0:T(8,128)(2,1)S(1)}, bf16[128,512]{1,0:T(8,128)(2,1)S(1)}, u32[]{:S(2)}, u32[]{:S(2)}) %collective-permute-start.22) | collective-permute-done | bytes 131104 | tf_op jit(solution)/shard_map/ppermute | solution.py:694
  88.7 1.1 %collective-permute-done.23.refs_9_ = bf16[128,512]{1,0:T(8,128)(2,1)S(1)} collective-permute-done((bf16[128,512]{1,0:T(8,128)(2,1)S(1)}, bf16[128,512]{1,0:T(8,128)(2,1)S(1)}, u32[]{:S(2)}, u32[]{:S(2)}) %collective-permute-start.23) | collective-permute-done | bytes 131104 | tf_op jit(solution)/shard_map/ppermute | solution.py:694
  89.8 0.8 combine.1
  90.6 0.1 collective-permute-start.24
  90.7 2.1 %collective-permute-done.24.other_ref = bf16[5,256,256]{2,1,0:T(8,128)(2,1)S(1)} collective-permute-done((bf16[5,256,256]{2,1,0:T(8,128)(2,1)S(1)}, bf16[5,256,256]{2,1,0:T(8,128)(2,1)S(1)}, u32[]{:S(2)}, u32[]{:S(2)}) %collective-permute-start.24) | collective-permute-done | bytes 655392 | tf_op jit(solution)/shard_map/ppermute | solution.py:700
  92.8 0.2 add.1
  93.0 1.7 %collective-permute-start.25 = (bf16[256,256]{1,0:T(8,128)(2,1)S(1)}, bf16[256,256]{1,0:T(8,128)(2,1)S(1)}, u32[]{:S(2)}, u32[]{:S(2)}) collective-permute-start(bf16[256,256]{1,0:T(8,128)(2,1)S(1)} %get-tuple-element.120), channel_id=1, source_target_pairs={{0,2},{1,3},{2,4},{3,5},{4,6},{5,7},{6,0},{7,1},{8,10},{9,11},{10,... | collective-permute-start | bytes 393224 | tf_op jit(solution)/shard_map/ppermute | solution.py:694
  94.6 1.8 %collective-permute-start.26 = (bf16[256,256]{1,0:T(8,128)(2,1)S(1)}, bf16[256,256]{1,0:T(8,128)(2,1)S(1)}, u32[]{:S(2)}, u32[]{:S(2)}) collective-permute-start(bf16[256,256]{1,0:T(8,128)(2,1)S(1)} %get-tuple-element.121), channel_id=1, source_target_pairs={{0,4},{1,5},{2,6},{3,7},{4,0},{5,1},{6,2},{7,3},{8,12},{9,13},{10,... | collective-permute-start | bytes 393224 | tf_op jit(solution)/shard_map/ppermute | solution.py:694
  96.5 2.3 %collective-permute-start.27 = (bf16[256,256]{1,0:T(8,128)(2,1)S(1)}, bf16[256,256]{1,0:T(8,128)(2,1)S(1)}, u32[]{:S(2)}, u32[]{:S(2)}) collective-permute-start(bf16[256,256]{1,0:T(8,128)(2,1)S(1)} %get-tuple-element.122), channel_id=1, source_target_pairs={{0,6},{1,7},{2,0},{3,1},{4,2},{5,3},{6,4},{7,5},{8,14},{9,15},{10,... | collective-permute-start | bytes 393224 | tf_op jit(solution)/shard_map/ppermute | solution.py:694
  98.8 1.5 %collective-permute-start.28 = (bf16[256,256]{1,0:T(8,128)(2,1)S(1)}, bf16[256,256]{1,0:T(8,128)(2,1)S(1)}, u32[]{:S(2)}, u32[]{:S(2)}) collective-permute-start(bf16[256,256]{1,0:T(8,128)(2,1)S(1)} %get-tuple-element.123), channel_id=1, source_target_pairs={{0,24},{1,25},{2,26},{3,27},{4,28},{5,29},{6,30},{7,31},{8,16},{9,... | collective-permute-start | bytes 393224 | tf_op jit(solution)/shard_map/ppermute | solution.py:710
  100.3 0.7 assemble.1
  100.9 0.3 collective-permute-done.25.refs_1_
  101.2 4.8 %collective-permute-done.26.refs_2_ = bf16[256,256]{1,0:T(8,128)(2,1)S(1)} collective-permute-done((bf16[256,256]{1,0:T(8,128)(2,1)S(1)}, bf16[256,256]{1,0:T(8,128)(2,1)S(1)}, u32[]{:S(2)}, u32[]{:S(2)}) %collective-permute-start.26) | collective-permute-done | bytes 131104 | tf_op jit(solution)/shard_map/ppermute | solution.py:694
  106.1 0.7 finish.1
  (16 shorter events, 0.0 us)
Async XLA Ops:
  0.6 17.2 %collective-permute-start.3 = (bf16[4096,256]{1,0:T(8,128)(2,1)}, bf16[4096,256]{1,0:T(8,128)(2,1)}, u32[]{:S(2)}, u32[]{:S(2)}) collective-permute-start(bf16[4096,256]{1,0:T(8,128)(2,1)} %refs_0_.2), channel_id=1, source_target_pairs={{0,1},{1,0},{2,3},{3,2},{4,5},{5,4},{6,7},{7,6},{8,9},{9,8},{10,11... | collective-permute-start | bytes 6291464 | tf_op jit(solution)/shard_map/ppermute | solution.py:700
  5.7 16.2 %copy-start = (bf16[4096,256]{1,0:T(8,128)(2,1)S(1)}, bf16[4096,256]{1,0:T(8,128)(2,1)}, u32[]{:S(2)}) copy-start(bf16[4096,256]{1,0:T(8,128)(2,1)} %refs_0_.2) | copy-start | bytes 6291460
  5.7 14.2 %collective-permute-start = (bf16[32,2176]{1,0:T(8,128)(2,1)S(1)}, bf16[32,2176]{1,0:T(8,128)(2,1)S(1)}, u32[]{:S(2)}, u32[]{:S(2)}) collective-permute-start(bf16[32,2176]{1,0:T(8,128)(2,1)S(1)} %get-tuple-element.64.refs_0_), channel_id=1, source_target_pairs={{0,4},{1,5},{2,6},{3,7},{4,0},{5,1},{6,2},{7,3},{8,12},{9,13},{10,... | collective-permute-start | bytes 417800 | tf_op jit(solution)/shard_map/ppermute | solution.py:694
  9.4 8.5 %collective-permute-start.4 = (bf16[128,256]{1,0:T(8,128)(2,1)S(1)}, bf16[128,256]{1,0:T(8,128)(2,1)S(1)}, u32[]{:S(2)}, u32[]{:S(2)}) collective-permute-start(bf16[128,256]{1,0:T(8,128)(2,1)S(1)} %get-tuple-element.66), channel_id=1, source_target_pairs={{0,1},{1,0},{2,3},{3,2},{4,5},{5,4},{6,7},{7,6},{8,9},{9,8},{10,11... | collective-permute-start | bytes 196616 | tf_op jit(solution)/shard_map/ppermute | solution.py:700
  9.6 14.1 %collective-permute-start.1 = (bf16[32,2176]{1,0:T(8,128)(2,1)S(1)}, bf16[32,2176]{1,0:T(8,128)(2,1)S(1)}, u32[]{:S(2)}, u32[]{:S(2)}) collective-permute-start(bf16[32,2176]{1,0:T(8,128)(2,1)S(1)} %get-tuple-element.64.refs_0_), channel_id=1, source_target_pairs={{0,2},{1,3},{2,4},{3,5},{4,6},{5,7},{6,0},{7,1},{8,10},{9,11},{10,... | collective-permute-start | bytes 417800 | tf_op jit(solution)/shard_map/ppermute | solution.py:694
  11.1 12.5 %collective-permute-start.2 = (bf16[32,2176]{1,0:T(8,128)(2,1)S(1)}, bf16[32,2176]{1,0:T(8,128)(2,1)S(1)}, u32[]{:S(2)}, u32[]{:S(2)}) collective-permute-start(bf16[32,2176]{1,0:T(8,128)(2,1)S(1)} %get-tuple-element.64.refs_0_), channel_id=1, source_target_pairs={{0,6},{1,7},{2,0},{3,1},{4,2},{5,3},{6,4},{7,5},{8,14},{9,15},{10,... | collective-permute-start | bytes 417800 | tf_op jit(solution)/shard_map/ppermute | solution.py:694
  17.8 13.5 %copy-start.1 = (bf16[256,256]{1,0:T(8,128)(2,1)S(1)}, bf16[256,256]{1,0:T(8,128)(2,1)}, u32[]{:S(2)}) copy-start(bf16[256,256]{1,0:T(8,128)(2,1)} %refs_10_.1) | copy-start | bytes 393220
  17.9 13.4 %collective-permute-start.5 = (bf16[32,2048]{1,0:T(8,128)(2,1)S(1)}, bf16[32,2048]{1,0:T(8,128)(2,1)S(1)}, u32[]{:S(2)}, u32[]{:S(2)}) collective-permute-start(bf16[32,2048]{1,0:T(8,128)(2,1)S(1)} %attend.3.refs_4_), channel_id=1, source_target_pairs={{0,4},{1,5},{2,6},{3,7},{4,0},{5,1},{6,2},{7,3},{8,12},{9,13},{10,... | collective-permute-start | bytes 393224 | tf_op jit(solution)/shard_map/ppermute | solution.py:694
  17.9 13.4 %collective-permute-start.6 = (bf16[32,2048]{1,0:T(8,128)(2,1)S(1)}, bf16[32,2048]{1,0:T(8,128)(2,1)S(1)}, u32[]{:S(2)}, u32[]{:S(2)}) collective-permute-start(bf16[32,2048]{1,0:T(8,128)(2,1)S(1)} %attend.3.refs_4_), channel_id=1, source_target_pairs={{0,2},{1,3},{2,4},{3,5},{4,6},{5,7},{6,0},{7,1},{8,10},{9,11},{10,... | collective-permute-start | bytes 393224 | tf_op jit(solution)/shard_map/ppermute | solution.py:694
  19.9 11.4 %collective-permute-start.7 = (bf16[32,2048]{1,0:T(8,128)(2,1)S(1)}, bf16[32,2048]{1,0:T(8,128)(2,1)S(1)}, u32[]{:S(2)}, u32[]{:S(2)}) collective-permute-start(bf16[32,2048]{1,0:T(8,128)(2,1)S(1)} %attend.3.refs_4_), channel_id=1, source_target_pairs={{0,6},{1,7},{2,0},{3,1},{4,2},{5,3},{6,4},{7,5},{8,14},{9,15},{10,... | collective-permute-start | bytes 393224 | tf_op jit(solution)/shard_map/ppermute | solution.py:694
  23.6 16.6 %copy-start.2 = (s32[256,8]{0,1:T(8,128)S(1)}, s32[256,8]{0,1:T(8,128)}, u32[]{:S(2)}) copy-start(s32[256,8]{0,1:T(8,128)} %param.19) | copy-start | bytes 24580
  23.6 16.6 %copy-start.3 = (f32[256,8]{0,1:T(8,128)S(1)}, f32[256,8]{0,1:T(8,128)}, u32[]{:S(2)}) copy-start(f32[256,8]{0,1:T(8,128)} %param.20) | copy-start | bytes 24580
  32.1 12.9 %collective-permute-start.8 = (bf16[128,512]{1,0:T(8,128)(2,1)S(1)}, bf16[128,512]{1,0:T(8,128)(2,1)S(1)}, u32[]{:S(2)}, u32[]{:S(2)}) collective-permute-start(bf16[128,512]{1,0:T(8,128)(2,1)S(1)} %get-tuple-element.89.refs_0_), channel_id=1, source_target_pairs={{0,2},{1,3},{2,4},{3,5},{4,6},{5,7},{6,0},{7,1},{8,10},{9,11},{10,... | collective-permute-start | bytes 393224 | tf_op jit(solution)/shard_map/ppermute | solution.py:694
  35.4 10.1 %collective-permute-start.9 = (bf16[128,512]{1,0:T(8,128)(2,1)S(1)}, bf16[128,512]{1,0:T(8,128)(2,1)S(1)}, u32[]{:S(2)}, u32[]{:S(2)}) collective-permute-start(bf16[128,512]{1,0:T(8,128)(2,1)S(1)} %get-tuple-element.89.refs_0_), channel_id=1, source_target_pairs={{0,4},{1,5},{2,6},{3,7},{4,0},{5,1},{6,2},{7,3},{8,12},{9,13},{10,... | collective-permute-start | bytes 393224 | tf_op jit(solution)/shard_map/ppermute | solution.py:694
  37.4 8.1 %collective-permute-start.10 = (bf16[128,512]{1,0:T(8,128)(2,1)S(1)}, bf16[128,512]{1,0:T(8,128)(2,1)S(1)}, u32[]{:S(2)}, u32[]{:S(2)}) collective-permute-start(bf16[128,512]{1,0:T(8,128)(2,1)S(1)} %get-tuple-element.89.refs_0_), channel_id=1, source_target_pairs={{0,6},{1,7},{2,0},{3,1},{4,2},{5,3},{6,4},{7,5},{8,14},{9,15},{10,... | collective-permute-start | bytes 393224 | tf_op jit(solution)/shard_map/ppermute | solution.py:694
  40.2 4.7 %collective-permute-start.11 = (bf16[144,256]{1,0:T(8,128)(2,1)S(1)}, bf16[144,256]{1,0:T(8,128)(2,1)S(1)}, u32[]{:S(2)}, u32[]{:S(2)}) collective-permute-start(bf16[144,256]{1,0:T(8,128)(2,1)S(1)} %get-tuple-element.77.give_ref), channel_id=1, source_target_pairs={{0,1},{1,0},{2,3},{3,2},{4,5},{5,4},{6,7},{7,6},{8,9},{9,8},{10,11... | collective-permute-start | bytes 221192 | tf_op jit(solution)/shard_map/ppermute | solution.py:700
  45.8 15.4 %collective-permute-start.14 = (bf16[128,2176]{1,0:T(8,128)(2,1)S(1)}, bf16[128,2176]{1,0:T(8,128)(2,1)S(1)}, u32[]{:S(2)}, u32[]{:S(2)}) collective-permute-start(bf16[128,2176]{1,0:T(8,128)(2,1)S(1)} %normalize.1.refs_0_), channel_id=1, source_target_pairs={{0,16},{1,9},{2,18},{3,11},{4,20},{5,13},{6,22},{7,15},{8,24},{9,1... | collective-permute-start | bytes 1671176 | tf_op jit(solution)/shard_map/ppermute | solution.py:710
  47.4 13.8 %collective-permute-start.13 = (bf16[128,2176]{1,0:T(8,128)(2,1)S(1)}, bf16[128,2176]{1,0:T(8,128)(2,1)S(1)}, u32[]{:S(2)}, u32[]{:S(2)}) collective-permute-start(bf16[128,2176]{1,0:T(8,128)(2,1)S(1)} %normalize.1.refs_0_), channel_id=1, source_target_pairs={{0,8},{1,17},{2,10},{3,19},{4,12},{5,21},{6,14},{7,23},{8,0},{9,25... | collective-permute-start | bytes 1671176 | tf_op jit(solution)/shard_map/ppermute | solution.py:710
  48.9 14.3 %collective-permute-start.12 = (bf16[128,2176]{1,0:T(8,128)(2,1)S(1)}, bf16[128,2176]{1,0:T(8,128)(2,1)S(1)}, u32[]{:S(2)}, u32[]{:S(2)}) collective-permute-start(bf16[128,2176]{1,0:T(8,128)(2,1)S(1)} %normalize.1.refs_0_), channel_id=1, source_target_pairs={{0,1},{1,0},{2,3},{3,2},{4,5},{5,4},{6,7},{7,6},{8,9},{9,8},{10,11... | collective-permute-start | bytes 1671176 | tf_op jit(solution)/shard_map/ppermute | solution.py:700
  61.2 2.0 %collective-permute-start.15 = (bf16[128,2176]{1,0:T(8,128)(2,1)S(1)}, bf16[128,2176]{1,0:T(8,128)(2,1)S(1)}, u32[]{:S(2)}, u32[]{:S(2)}) collective-permute-start(bf16[128,2176]{1,0:T(8,128)(2,1)S(1)} %collective-permute-done.14.refs_4_), channel_id=1, source_target_pairs={{0,1},{1,0},{2,3},{3,2},{4,5},{5,4},{6,7},{7,6},{8,9},{9,8},{10,11... | collective-permute-start | bytes 1671176 | tf_op jit(solution)/shard_map/ppermute | solution.py:700
  61.2 2.7 %collective-permute-start.16 = (bf16[128,2176]{1,0:T(8,128)(2,1)S(1)}, bf16[128,2176]{1,0:T(8,128)(2,1)S(1)}, u32[]{:S(2)}, u32[]{:S(2)}) collective-permute-start(bf16[128,2176]{1,0:T(8,128)(2,1)S(1)} %collective-permute-done.13.refs_2_), channel_id=1, source_target_pairs={{0,1},{1,0},{2,3},{3,2},{4,5},{5,4},{6,7},{7,6},{8,9},{9,8},{10,11... | collective-permute-start | bytes 1671176 | tf_op jit(solution)/shard_map/ppermute | solution.py:700
  61.7 9.5 %collective-permute-start.19 = (bf16[128,2176]{1,0:T(8,128)(2,1)S(1)}, bf16[128,2176]{1,0:T(8,128)(2,1)S(1)}, u32[]{:S(2)}, u32[]{:S(2)}) collective-permute-start(bf16[128,2176]{1,0:T(8,128)(2,1)S(1)} %collective-permute-done.13.refs_2_), channel_id=1, source_target_pairs={{0,16},{1,9},{2,18},{3,11},{4,20},{5,13},{6,22},{7,15},{8,24},{9,1... | collective-permute-start | bytes 1671176 | tf_op jit(solution)/shard_map/ppermute | solution.py:710
  71.2 2.4 %collective-permute-start.20 = (bf16[128,2176]{1,0:T(8,128)(2,1)S(1)}, bf16[128,2176]{1,0:T(8,128)(2,1)S(1)}, u32[]{:S(2)}, u32[]{:S(2)}) collective-permute-start(bf16[128,2176]{1,0:T(8,128)(2,1)S(1)} %collective-permute-done.19.refs_0_.rows_ref), channel_id=1, source_target_pairs={{0,1},{1,0},{2,3},{3,2},{4,5},{5,4},{6,7},{7,6},{8,9},{9,8},{10,11... | collective-permute-start | bytes 1671176 | tf_op jit(solution)/shard_map/ppermute | solution.py:700
  71.3 14.0 %collective-permute-start.17 = (bf16[128,2048]{1,0:T(8,128)(2,1)S(1)}, bf16[128,2048]{1,0:T(8,128)(2,1)S(1)}, u32[]{:S(2)}, u32[]{:S(2)}) collective-permute-start(bf16[128,2048]{1,0:T(8,128)(2,1)S(1)} %get-tuple-element.97), channel_id=1, source_target_pairs={{0,8},{1,17},{2,10},{3,19},{4,12},{5,21},{6,14},{7,23},{8,0},{9,25... | collective-permute-start | bytes 1572872 | tf_op jit(solution)/shard_map/ppermute | solution.py:710
  72.2 13.4 %collective-permute-start.18 = (bf16[128,2048]{1,0:T(8,128)(2,1)S(1)}, bf16[128,2048]{1,0:T(8,128)(2,1)S(1)}, u32[]{:S(2)}, u32[]{:S(2)}) collective-permute-start(bf16[128,2048]{1,0:T(8,128)(2,1)S(1)} %get-tuple-element.98), channel_id=1, source_target_pairs={{0,16},{1,9},{2,18},{3,11},{4,20},{5,13},{6,22},{7,15},{8,24},{9,1... | collective-permute-start | bytes 1572872 | tf_op jit(solution)/shard_map/ppermute | solution.py:710
  75.6 10.0 %collective-permute-start.21 = (bf16[128,512]{1,0:T(8,128)(2,1)S(1)}, bf16[128,512]{1,0:T(8,128)(2,1)S(1)}, u32[]{:S(2)}, u32[]{:S(2)}) collective-permute-start(bf16[128,512]{1,0:T(8,128)(2,1)S(1)} %get-tuple-element.101), channel_id=1, source_target_pairs={{0,4},{1,5},{2,6},{3,7},{4,0},{5,1},{6,2},{7,3},{8,12},{9,13},{10,... | collective-permute-start | bytes 393224 | tf_op jit(solution)/shard_map/ppermute | solution.py:694
  77.8 10.9 %collective-permute-start.22 = (bf16[128,512]{1,0:T(8,128)(2,1)S(1)}, bf16[128,512]{1,0:T(8,128)(2,1)S(1)}, u32[]{:S(2)}, u32[]{:S(2)}) collective-permute-start(bf16[128,512]{1,0:T(8,128)(2,1)S(1)} %get-tuple-element.102), channel_id=1, source_target_pairs={{0,2},{1,3},{2,4},{3,5},{4,6},{5,7},{6,0},{7,1},{8,10},{9,11},{10,... | collective-permute-start | bytes 393224 | tf_op jit(solution)/shard_map/ppermute | solution.py:694
  82.1 7.7 %collective-permute-start.23 = (bf16[128,512]{1,0:T(8,128)(2,1)S(1)}, bf16[128,512]{1,0:T(8,128)(2,1)S(1)}, u32[]{:S(2)}, u32[]{:S(2)}) collective-permute-start(bf16[128,512]{1,0:T(8,128)(2,1)S(1)} %get-tuple-element.103), channel_id=1, source_target_pairs={{0,6},{1,7},{2,0},{3,1},{4,2},{5,3},{6,4},{7,5},{8,14},{9,15},{10,... | collective-permute-start | bytes 393224 | tf_op jit(solution)/shard_map/ppermute | solution.py:694
  90.6 2.2 %collective-permute-start.24 = (bf16[5,256,256]{2,1,0:T(8,128)(2,1)S(1)}, bf16[5,256,256]{2,1,0:T(8,128)(2,1)S(1)}, u32[]{:S(2)}, u32[]{:S(2)}) collective-permute-start(bf16[5,256,256]{2,1,0:T(8,128)(2,1)S(1)} %get-tuple-element.118), channel_id=1, source_target_pairs={{0,1},{1,0},{2,3},{3,2},{4,5},{5,4},{6,7},{7,6},{8,9},{9,8},{10,11... | collective-permute-start | bytes 1966088 | tf_op jit(solution)/shard_map/ppermute | solution.py:700
  93.0 8.3 %collective-permute-start.25 = (bf16[256,256]{1,0:T(8,128)(2,1)S(1)}, bf16[256,256]{1,0:T(8,128)(2,1)S(1)}, u32[]{:S(2)}, u32[]{:S(2)}) collective-permute-start(bf16[256,256]{1,0:T(8,128)(2,1)S(1)} %get-tuple-element.120), channel_id=1, source_target_pairs={{0,2},{1,3},{2,4},{3,5},{4,6},{5,7},{6,0},{7,1},{8,10},{9,11},{10,... | collective-permute-start | bytes 393224 | tf_op jit(solution)/shard_map/ppermute | solution.py:694
  94.6 11.4 %collective-permute-start.26 = (bf16[256,256]{1,0:T(8,128)(2,1)S(1)}, bf16[256,256]{1,0:T(8,128)(2,1)S(1)}, u32[]{:S(2)}, u32[]{:S(2)}) collective-permute-start(bf16[256,256]{1,0:T(8,128)(2,1)S(1)} %get-tuple-element.121), channel_id=1, source_target_pairs={{0,4},{1,5},{2,6},{3,7},{4,0},{5,1},{6,2},{7,3},{8,12},{9,13},{10,... | collective-permute-start | bytes 393224 | tf_op jit(solution)/shard_map/ppermute | solution.py:694
  96.5 9.6 %collective-permute-start.27 = (bf16[256,256]{1,0:T(8,128)(2,1)S(1)}, bf16[256,256]{1,0:T(8,128)(2,1)S(1)}, u32[]{:S(2)}, u32[]{:S(2)}) collective-permute-start(bf16[256,256]{1,0:T(8,128)(2,1)S(1)} %get-tuple-element.122), channel_id=1, source_target_pairs={{0,6},{1,7},{2,0},{3,1},{4,2},{5,3},{6,4},{7,5},{8,14},{9,15},{10,... | collective-permute-start | bytes 393224 | tf_op jit(solution)/shard_map/ppermute | solution.py:694
  98.8 7.3 %collective-permute-start.28 = (bf16[256,256]{1,0:T(8,128)(2,1)S(1)}, bf16[256,256]{1,0:T(8,128)(2,1)S(1)}, u32[]{:S(2)}, u32[]{:S(2)}) collective-permute-start(bf16[256,256]{1,0:T(8,128)(2,1)S(1)} %get-tuple-element.123), channel_id=1, source_target_pairs={{0,24},{1,25},{2,26},{3,27},{4,28},{5,29},{6,30},{7,31},{8,16},{9,... | collective-permute-start | bytes 393224 | tf_op jit(solution)/shard_map/ppermute | solution.py:710

commit v5 on v4

--- a/solution.py
+++ b/solution.py
@@ -201,7 +201,7 @@
 
 
 def project_kernel(*refs, line, parts):
-    blocks = refs[: line * parts]
+    blocks = [refs[k] for k in line_order(line)] + list(refs[line : line * parts])
     (
         weight_ref,
         other_weight_ref,
@@ -726,7 +726,10 @@
             attention, other_weight, extra = lax.optimization_barrier(
                 (attention, other_weight, extra)
             )
-        blocks += turn_all([attention] * line)
+        if part == 0:
+            blocks += [attention] + [turn(attention, k) for k in range(1, line)]
+        else:
+            blocks += turn_all([attention] * line)
 
     attention, held = lax.optimization_barrier((attention, (out_weight, other_weight)))
     weight, other_weight = fetch(*held)

time: 107 us -> 107 us (level)
  waiting for transfers between devices: 38.8 us -> 37.7 us
    ppermute x15, waiting for transfers between devices: 19 us -> 17.5 us  [turn(): return lax.ppermute(value, 'expert', pairs)]
  transfers between devices with their start and end apart: 29 -> 29, of which waited for: 13 -> 10; matrix products, arithmetic and copies ran while one was open for 0% -> 0% of each run, Pallas kernels for 22% -> 23%
where the time goes in v5:
time: 107 us; the launch traced here: 106 us
  starting transfers between devices  40.6 us (38%)
  waiting for transfers between devices  37.7 us (35%)
  Pallas kernels  26.7 us (25%)
    ppermute x15, starting transfers between devices, turn(): return lax.ppermute(value, 'expert', pairs)  30.8 us
    ppermute x15, waiting for transfers between devices, turn(): return lax.ppermute(value, 'expert', pairs)  17.5 us
    ppermute x6, waiting for transfers between devices, across_pool(): return lax.ppermute(value, ('pool', 'expert'), pairs)  17.4 us
    pallas_call x2, Pallas kernels, attend(): pl.pallas_call(functools.partial(attend_kernel, block_len=block_len, firs...  8.96 us
    ppermute x6, starting transfers between devices, across_pool(): return lax.ppermute(value, ('pool', 'expert'), pairs)  8.48 us
    pallas_call x2, Pallas kernels, run_expert(): pl.pallas_call(functools.partial(expert_kernel, count=count, top_count=to...  6.99 us
    pallas_call x2, Pallas kernels, fetch(): pl.pallas_call(functools.partial(fetch_kernel, count=count), in_specs=[pl...  5.53 us
    ppermute x8, waiting for transfers between devices, across_cores(): lax.ppermute(value, 'expert', [(e, e ^ 1) for e in range(expert_size)])  2.81 us
  transfers between devices with their start and end apart: 29, of which 10 were waited for; matrix products, arithmetic and copies ran while one was open for 0% of the time, Pallas kernels for 23%

profile of v5, /device:TPU:0, one launch (start us, length us, event | category | flops | bytes accessed | tf_op | source)
XLA Modules:
  0.0 105.9 jit_solution(7616882471028714532)
XLA Ops:
  0.6 0.5 collective-permute-start.3
  1.1 4.5 %attend.2 = (bf16[32,2176]{1,0:T(8,128)(2,1)S(1)}, bf16[128,256]{1,0:T(8,128)(2,1)S(1)}) custom-call(s32[8,32]{1,0:T(8,128)} %bitcast.10, s32[1,32]{1,0:T(1,128)} %bitcast.12, bf16[32,4096]{1,0:T(8,128)(2,1)} %query_ref.2, bf16[2048,1024]{1,0:T(8,128)(2,1)} %bitcast.8, bf16[256,256]{1,0:T(8,128)(2,1)} %refs_10_.1, f32[1,256]{1,0:T(1,128)} %bitcast.14), custom_call_target="tpu_custom_call" | custom-call | tf_op jit(solution)/shard_map/attend/pallas_call | solution.py:151
  5.7 0.0 copy-start
  5.7 2.6 %collective-permute-start = (bf16[32,2176]{1,0:T(8,128)(2,1)S(1)}, bf16[32,2176]{1,0:T(8,128)(2,1)S(1)}, u32[]{:S(2)}, u32[]{:S(2)}) collective-permute-start(bf16[32,2176]{1,0:T(8,128)(2,1)S(1)} %get-tuple-element.64.refs_0_), channel_id=1, source_target_pairs={{0,2},{1,3},{2,4},{3,5},{4,6},{5,7},{6,0},{7,1},{8,10},{9,11},{10,... | collective-permute-start | bytes 417800 | tf_op jit(solution)/shard_map/ppermute | solution.py:694
  8.3 0.2 collective-permute-start.4
  8.5 2.6 %collective-permute-start.1 = (bf16[32,2176]{1,0:T(8,128)(2,1)S(1)}, bf16[32,2176]{1,0:T(8,128)(2,1)S(1)}, u32[]{:S(2)}, u32[]{:S(2)}) collective-permute-start(bf16[32,2176]{1,0:T(8,128)(2,1)S(1)} %get-tuple-element.64.refs_0_), channel_id=1, source_target_pairs={{0,4},{1,5},{2,6},{3,7},{4,0},{5,1},{6,2},{7,3},{8,12},{9,13},{10,... | collective-permute-start | bytes 417800 | tf_op jit(solution)/shard_map/ppermute | solution.py:694
  11.1 1.4 %collective-permute-start.2 = (bf16[32,2176]{1,0:T(8,128)(2,1)S(1)}, bf16[32,2176]{1,0:T(8,128)(2,1)S(1)}, u32[]{:S(2)}, u32[]{:S(2)}) collective-permute-start(bf16[32,2176]{1,0:T(8,128)(2,1)S(1)} %get-tuple-element.64.refs_0_), channel_id=1, source_target_pairs={{0,6},{1,7},{2,0},{3,1},{4,2},{5,3},{6,4},{7,5},{8,14},{9,15},{10,... | collective-permute-start | bytes 417800 | tf_op jit(solution)/shard_map/ppermute | solution.py:694
  12.5 4.4 %attend.3.refs_4_ = bf16[32,2048]{1,0:T(8,128)(2,1)S(1)} custom-call(s32[8,32]{1,0:T(8,128)} %bitcast.11, s32[1,32]{1,0:T(1,128)} %bitcast.13, bf16[32,4096]{1,0:T(8,128)(2,1)} %query_ref.2, bf16[2048,1024]{1,0:T(8,128)(2,1)} %bitcast.9), custom_call_target="tpu_custom_call" | custom-call | tf_op jit(solution)/shard_map/attend/pallas_call | solution.py:151
  16.9 0.0 copy-start.1
  16.9 0.0 collective-permute-done.4.refs_11_
  16.9 0.0 collective-permute-done.3.refs_1_
  17.0 0.5 collective-permute-start.5
  17.5 0.5 collective-permute-start.6
  18.0 3.3 %collective-permute-start.7 = (bf16[32,2048]{1,0:T(8,128)(2,1)S(1)}, bf16[32,2048]{1,0:T(8,128)(2,1)S(1)}, u32[]{:S(2)}, u32[]{:S(2)}) collective-permute-start(bf16[32,2048]{1,0:T(8,128)(2,1)S(1)} %attend.3.refs_4_), channel_id=1, source_target_pairs={{0,6},{1,7},{2,0},{3,1},{4,2},{5,3},{6,4},{7,5},{8,14},{9,15},{10,... | collective-permute-start | bytes 393224 | tf_op jit(solution)/shard_map/ppermute | solution.py:694
  21.3 1.7 %fetch.2 = (bf16[4096,256]{1,0:T(8,128)(2,1)S(1)}, bf16[4096,256]{1,0:T(8,128)(2,1)S(1)}) custom-call(bf16[4096,256]{1,0:T(8,128)(2,1)S(1)} %copy-done, bf16[4096,256]{1,0:T(8,128)(2,1)} %collective-permute-done.3.refs_1_), custom_call_target="tpu_custom_call" | custom-call | bytes 8388608 | tf_op jit(solution)/shard_map/fetch/pallas_call | solution.py:189
  23.1 0.0 copy-start.2
  23.1 0.0 copy-start.3
  23.1 0.0 collective-permute-done.1.refs_2_
  23.1 9.0 %collective-permute-done.5.refs_5_ = bf16[32,2048]{1,0:T(8,128)(2,1)S(1)} collective-permute-done((bf16[32,2048]{1,0:T(8,128)(2,1)S(1)}, bf16[32,2048]{1,0:T(8,128)(2,1)S(1)}, u32[]{:S(2)}, u32[]{:S(2)}) %collective-permute-start.5) | collective-permute-done | bytes 131104 | tf_op jit(solution)/shard_map/ppermute | solution.py:694
  32.1 0.7 project.1
  32.9 3.4 %collective-permute-start.8 = (bf16[128,512]{1,0:T(8,128)(2,1)S(1)}, bf16[128,512]{1,0:T(8,128)(2,1)S(1)}, u32[]{:S(2)}, u32[]{:S(2)}) collective-permute-start(bf16[128,512]{1,0:T(8,128)(2,1)S(1)} %get-tuple-element.89.refs_0_), channel_id=1, source_target_pairs={{0,2},{1,3},{2,4},{3,5},{4,6},{5,7},{6,0},{7,1},{8,10},{9,11},{10,... | collective-permute-start | bytes 393224 | tf_op jit(solution)/shard_map/ppermute | solution.py:694
  36.2 0.2 collective-permute-start.9
  36.5 2.8 %collective-permute-start.10 = (bf16[128,512]{1,0:T(8,128)(2,1)S(1)}, bf16[128,512]{1,0:T(8,128)(2,1)S(1)}, u32[]{:S(2)}, u32[]{:S(2)}) collective-permute-start(bf16[128,512]{1,0:T(8,128)(2,1)S(1)} %get-tuple-element.89.refs_0_), channel_id=1, source_target_pairs={{0,6},{1,7},{2,0},{3,1},{4,2},{5,3},{6,4},{7,5},{8,14},{9,15},{10,... | collective-permute-start | bytes 393224 | tf_op jit(solution)/shard_map/ppermute | solution.py:694
  39.3 0.0 collective-permute-start.11
  39.3 0.9 lines.1
  40.2 3.8 %fetch.3 = (bf16[1,2048,768]{2,1,0:T(8,128)(2,1)S(1)}, bf16[1,2048,768]{2,1,0:T(8,128)(2,1)S(1)}, bf16[1,768,2048]{2,1,0:T(8,128)(2,1)S(1)}) custom-call(bf16[1,2048,768]{2,1,0:T(8,128)(2,1)} %refs_0_.3, bf16[1,2048,768]{2,1,0:T(8,128)(2,1)} %refs_1_, bf16[1,768,2048]{2,1,0:T(8,128)(2,1)} %refs_2_), custom_call_target="tpu_custom_call" | custom-call | bytes 18874368 | tf_op jit(solution)/shard_map/fetch/pallas_call | solution.py:189
  44.0 0.0 collective-permute-done.11.taken_ref
  44.0 1.8 %collective-permute-done.9.refs_2_ = bf16[128,512]{1,0:T(8,128)(2,1)S(1)} collective-permute-done((bf16[128,512]{1,0:T(8,128)(2,1)S(1)}, bf16[128,512]{1,0:T(8,128)(2,1)S(1)}, u32[]{:S(2)}, u32[]{:S(2)}) %collective-permute-start.9) | collective-permute-done | bytes 131104 | tf_op jit(solution)/shard_map/ppermute | solution.py:694
  45.8 0.3 normalize.1.refs_0_
  46.1 1.6 %collective-permute-start.14 = (bf16[128,2176]{1,0:T(8,128)(2,1)S(1)}, bf16[128,2176]{1,0:T(8,128)(2,1)S(1)}, u32[]{:S(2)}, u32[]{:S(2)}) collective-permute-start(bf16[128,2176]{1,0:T(8,128)(2,1)S(1)} %normalize.1.refs_0_), channel_id=1, source_target_pairs={{0,16},{1,9},{2,18},{3,11},{4,20},{5,13},{6,22},{7,15},{8,24},{9,1... | collective-permute-start | bytes 1671176 | tf_op jit(solution)/shard_map/ppermute | solution.py:710
  47.7 1.5 %collective-permute-start.13 = (bf16[128,2176]{1,0:T(8,128)(2,1)S(1)}, bf16[128,2176]{1,0:T(8,128)(2,1)S(1)}, u32[]{:S(2)}, u32[]{:S(2)}) collective-permute-start(bf16[128,2176]{1,0:T(8,128)(2,1)S(1)} %normalize.1.refs_0_), channel_id=1, source_target_pairs={{0,8},{1,17},{2,10},{3,19},{4,12},{5,21},{6,14},{7,23},{8,0},{9,25... | collective-permute-start | bytes 1671176 | tf_op jit(solution)/shard_map/ppermute | solution.py:710
  49.2 0.0 collective-permute-start.12
  49.2 12.3 %collective-permute-done.14.refs_4_ = bf16[128,2176]{1,0:T(8,128)(2,1)S(1)} collective-permute-done((bf16[128,2176]{1,0:T(8,128)(2,1)S(1)}, bf16[128,2176]{1,0:T(8,128)(2,1)S(1)}, u32[]{:S(2)}, u32[]{:S(2)}) %collective-permute-start.14) | collective-permute-done | bytes 557088 | tf_op jit(solution)/shard_map/ppermute | solution.py:710
  61.5 0.0 collective-permute-start.15
  61.5 0.0 collective-permute-done.13.refs_2_
  61.5 0.5 collective-permute-start.16
  62.0 1.5 %collective-permute-start.19 = (bf16[128,2176]{1,0:T(8,128)(2,1)S(1)}, bf16[128,2176]{1,0:T(8,128)(2,1)S(1)}, u32[]{:S(2)}, u32[]{:S(2)}) collective-permute-start(bf16[128,2176]{1,0:T(8,128)(2,1)S(1)} %collective-permute-done.13.refs_2_), channel_id=1, source_target_pairs={{0,16},{1,9},{2,18},{3,11},{4,20},{5,13},{6,22},{7,15},{8,24},{9,1... | collective-permute-start | bytes 1671176 | tf_op jit(solution)/shard_map/ppermute | solution.py:710
  63.6 0.0 collective-permute-done.12.refs_1_
  63.6 0.0 collective-permute-done.15.refs_3_
  63.6 0.7 collective-permute-done.16.refs_5_
  64.3 5.1 %expert.2 = (bf16[128,2048]{1,0:T(8,128)(2,1)S(1)}, bf16[128,2048]{1,0:T(8,128)(2,1)S(1)}, bf16[128,2048]{1,0:T(8,128)(2,1)S(1)}) custom-call(bf16[128,2176]{1,0:T(8,128)(2,1)S(1)} %normalize.1.refs_0_, bf16[128,2176]{1,0:T(8,128)(2,1)S(1)} %collective-permute-done.12.refs_1_, bf16[128,2176]{1,0:T(8,128)(2,1)S(1)} %collective-permute-done.13.refs_2_, ...), custom_call_target="tpu_custom_call" | custom-call | flops 3623878656 | bytes 15728640 | tf_op jit(solution)/shard_map/expert/pallas_call | solution.py:475
  69.4 2.2 %collective-permute-done.19.refs_0_.rows_ref = bf16[128,2176]{1,0:T(8,128)(2,1)S(1)} collective-permute-done((bf16[128,2176]{1,0:T(8,128)(2,1)S(1)}, bf16[128,2176]{1,0:T(8,128)(2,1)S(1)}, u32[]{:S(2)}, u32[]{:S(2)}) %collective-permute-start.19) | collective-permute-done | bytes 557088 | tf_op jit(solution)/shard_map/ppermute | solution.py:710
  71.6 0.9 collective-permute-start.17
  72.5 1.5 %collective-permute-start.18 = (bf16[128,2048]{1,0:T(8,128)(2,1)S(1)}, bf16[128,2048]{1,0:T(8,128)(2,1)S(1)}, u32[]{:S(2)}, u32[]{:S(2)}) collective-permute-start(bf16[128,2048]{1,0:T(8,128)(2,1)S(1)} %get-tuple-element.98), channel_id=1, source_target_pairs={{0,16},{1,9},{2,18},{3,11},{4,20},{5,13},{6,22},{7,15},{8,24},{9,1... | collective-permute-start | bytes 1572872 | tf_op jit(solution)/shard_map/ppermute | solution.py:710
  74.0 0.0 collective-permute-done.20.refs_1_
  74.0 1.9 %expert.3 = (bf16[128,512]{1,0:T(8,128)(2,1)S(1)}, bf16[128,512]{1,0:T(8,128)(2,1)S(1)}, bf16[128,512]{1,0:T(8,128)(2,1)S(1)}, bf16[128,512]{1,0:T(8,128)(2,1)S(1)}) custom-call(bf16[128,2176]{1,0:T(8,128)(2,1)S(1)} %collective-permute-done.19.refs_0_.rows_ref, bf16[128,2176]{1,0:T(8,128)(2,1)S(1)} %collective-permute-done.20.refs_1_, ...), custom_call_target="tpu_custom_call" | custom-call | flops 1207959552 | bytes 11534336 | tf_op jit(solution)/shard_map/expert/pallas_call | solution.py:475
  75.9 2.4 %collective-permute-start.21 = (bf16[128,512]{1,0:T(8,128)(2,1)S(1)}, bf16[128,512]{1,0:T(8,128)(2,1)S(1)}, u32[]{:S(2)}, u32[]{:S(2)}) collective-permute-start(bf16[128,512]{1,0:T(8,128)(2,1)S(1)} %get-tuple-element.101), channel_id=1, source_target_pairs={{0,4},{1,5},{2,6},{3,7},{4,0},{5,1},{6,2},{7,3},{8,12},{9,13},{10,... | collective-permute-start | bytes 393224 | tf_op jit(solution)/shard_map/ppermute | solution.py:694
  78.3 2.1 %collective-permute-start.22 = (bf16[128,512]{1,0:T(8,128)(2,1)S(1)}, bf16[128,512]{1,0:T(8,128)(2,1)S(1)}, u32[]{:S(2)}, u32[]{:S(2)}) collective-permute-start(bf16[128,512]{1,0:T(8,128)(2,1)S(1)} %get-tuple-element.102), channel_id=1, source_target_pairs={{0,2},{1,3},{2,4},{3,5},{4,6},{5,7},{6,0},{7,1},{8,10},{9,11},{10,... | collective-permute-start | bytes 393224 | tf_op jit(solution)/shard_map/ppermute | solution.py:694
  80.4 1.7 %collective-permute-start.23 = (bf16[128,512]{1,0:T(8,128)(2,1)S(1)}, bf16[128,512]{1,0:T(8,128)(2,1)S(1)}, u32[]{:S(2)}, u32[]{:S(2)}) collective-permute-start(bf16[128,512]{1,0:T(8,128)(2,1)S(1)} %get-tuple-element.103), channel_id=1, source_target_pairs={{0,6},{1,7},{2,0},{3,1},{4,2},{5,3},{6,4},{7,5},{8,14},{9,15},{10,... | collective-permute-start | bytes 393224 | tf_op jit(solution)/shard_map/ppermute | solution.py:694
  82.1 0.9 plan.1
  83.1 2.6 %collective-permute-done.17.refs_1_ = bf16[128,2048]{1,0:T(8,128)(2,1)S(1)} collective-permute-done((bf16[128,2048]{1,0:T(8,128)(2,1)S(1)}, bf16[128,2048]{1,0:T(8,128)(2,1)S(1)}, u32[]{:S(2)}, u32[]{:S(2)}) %collective-permute-start.17) | collective-permute-done | bytes 524320 | tf_op jit(solution)/shard_map/ppermute | solution.py:710
  85.6 0.3 collective-permute-done.18.refs_2_
  85.9 2.9 %collective-permute-done.22.refs_8_ = bf16[128,512]{1,0:T(8,128)(2,1)S(1)} collective-permute-done((bf16[128,512]{1,0:T(8,128)(2,1)S(1)}, bf16[128,512]{1,0:T(8,128)(2,1)S(1)}, u32[]{:S(2)}, u32[]{:S(2)}) %collective-permute-start.22) | collective-permute-done | bytes 131104 | tf_op jit(solution)/shard_map/ppermute | solution.py:694
  88.9 0.8 combine.1
  89.7 0.1 collective-permute-start.24
  89.8 2.1 %collective-permute-done.24.other_ref = bf16[5,256,256]{2,1,0:T(8,128)(2,1)S(1)} collective-permute-done((bf16[5,256,256]{2,1,0:T(8,128)(2,1)S(1)}, bf16[5,256,256]{2,1,0:T(8,128)(2,1)S(1)}, u32[]{:S(2)}, u32[]{:S(2)}) %collective-permute-start.24) | collective-permute-done | bytes 655392 | tf_op jit(solution)/shard_map/ppermute | solution.py:700
  91.9 0.2 add.1
  92.0 2.4 %collective-permute-start.25 = (bf16[256,256]{1,0:T(8,128)(2,1)S(1)}, bf16[256,256]{1,0:T(8,128)(2,1)S(1)}, u32[]{:S(2)}, u32[]{:S(2)}) collective-permute-start(bf16[256,256]{1,0:T(8,128)(2,1)S(1)} %get-tuple-element.120), channel_id=1, source_target_pairs={{0,2},{1,3},{2,4},{3,5},{4,6},{5,7},{6,0},{7,1},{8,10},{9,11},{10,... | collective-permute-start | bytes 393224 | tf_op jit(solution)/shard_map/ppermute | solution.py:694
  94.4 2.0 %collective-permute-start.26 = (bf16[256,256]{1,0:T(8,128)(2,1)S(1)}, bf16[256,256]{1,0:T(8,128)(2,1)S(1)}, u32[]{:S(2)}, u32[]{:S(2)}) collective-permute-start(bf16[256,256]{1,0:T(8,128)(2,1)S(1)} %get-tuple-element.121), channel_id=1, source_target_pairs={{0,4},{1,5},{2,6},{3,7},{4,0},{5,1},{6,2},{7,3},{8,12},{9,13},{10,... | collective-permute-start | bytes 393224 | tf_op jit(solution)/shard_map/ppermute | solution.py:694
  96.4 2.8 %collective-permute-start.27 = (bf16[256,256]{1,0:T(8,128)(2,1)S(1)}, bf16[256,256]{1,0:T(8,128)(2,1)S(1)}, u32[]{:S(2)}, u32[]{:S(2)}) collective-permute-start(bf16[256,256]{1,0:T(8,128)(2,1)S(1)} %get-tuple-element.122), channel_id=1, source_target_pairs={{0,6},{1,7},{2,0},{3,1},{4,2},{5,3},{6,4},{7,5},{8,14},{9,15},{10,... | collective-permute-start | bytes 393224 | tf_op jit(solution)/shard_map/ppermute | solution.py:694
  99.2 1.5 %collective-permute-start.28 = (bf16[256,256]{1,0:T(8,128)(2,1)S(1)}, bf16[256,256]{1,0:T(8,128)(2,1)S(1)}, u32[]{:S(2)}, u32[]{:S(2)}) collective-permute-start(bf16[256,256]{1,0:T(8,128)(2,1)S(1)} %get-tuple-element.123), channel_id=1, source_target_pairs={{0,24},{1,25},{2,26},{3,27},{4,28},{5,29},{6,30},{7,31},{8,16},{9,... | collective-permute-start | bytes 393224 | tf_op jit(solution)/shard_map/ppermute | solution.py:710
  100.7 0.7 assemble.1
  101.4 3.7 %collective-permute-done.26.refs_2_ = bf16[256,256]{1,0:T(8,128)(2,1)S(1)} collective-permute-done((bf16[256,256]{1,0:T(8,128)(2,1)S(1)}, bf16[256,256]{1,0:T(8,128)(2,1)S(1)}, u32[]{:S(2)}, u32[]{:S(2)}) %collective-permute-start.26) | collective-permute-done | bytes 131104 | tf_op jit(solution)/shard_map/ppermute | solution.py:694
  105.1 0.7 finish.1
  (16 shorter events, 0.0 us)
Async XLA Ops:
  0.6 16.3 %collective-permute-start.3 = (bf16[4096,256]{1,0:T(8,128)(2,1)}, bf16[4096,256]{1,0:T(8,128)(2,1)}, u32[]{:S(2)}, u32[]{:S(2)}) collective-permute-start(bf16[4096,256]{1,0:T(8,128)(2,1)} %refs_0_.2), channel_id=1, source_target_pairs={{0,1},{1,0},{2,3},{3,2},{4,5},{5,4},{6,7},{7,6},{8,9},{9,8},{10,11... | collective-permute-start | bytes 6291464 | tf_op jit(solution)/shard_map/ppermute | solution.py:700
  5.7 15.7 %copy-start = (bf16[4096,256]{1,0:T(8,128)(2,1)S(1)}, bf16[4096,256]{1,0:T(8,128)(2,1)}, u32[]{:S(2)}) copy-start(bf16[4096,256]{1,0:T(8,128)(2,1)} %refs_0_.2) | copy-start | bytes 6291460
  5.7 12.4 %collective-permute-start = (bf16[32,2176]{1,0:T(8,128)(2,1)S(1)}, bf16[32,2176]{1,0:T(8,128)(2,1)S(1)}, u32[]{:S(2)}, u32[]{:S(2)}) collective-permute-start(bf16[32,2176]{1,0:T(8,128)(2,1)S(1)} %get-tuple-element.64.refs_0_), channel_id=1, source_target_pairs={{0,2},{1,3},{2,4},{3,5},{4,6},{5,7},{6,0},{7,1},{8,10},{9,11},{10,... | collective-permute-start | bytes 417800 | tf_op jit(solution)/shard_map/ppermute | solution.py:694
  8.3 8.6 %collective-permute-start.4 = (bf16[128,256]{1,0:T(8,128)(2,1)S(1)}, bf16[128,256]{1,0:T(8,128)(2,1)S(1)}, u32[]{:S(2)}, u32[]{:S(2)}) collective-permute-start(bf16[128,256]{1,0:T(8,128)(2,1)S(1)} %get-tuple-element.66), channel_id=1, source_target_pairs={{0,1},{1,0},{2,3},{3,2},{4,5},{5,4},{6,7},{7,6},{8,9},{9,8},{10,11... | collective-permute-start | bytes 196616 | tf_op jit(solution)/shard_map/ppermute | solution.py:700
  8.5 14.6 %collective-permute-start.1 = (bf16[32,2176]{1,0:T(8,128)(2,1)S(1)}, bf16[32,2176]{1,0:T(8,128)(2,1)S(1)}, u32[]{:S(2)}, u32[]{:S(2)}) collective-permute-start(bf16[32,2176]{1,0:T(8,128)(2,1)S(1)} %get-tuple-element.64.refs_0_), channel_id=1, source_target_pairs={{0,4},{1,5},{2,6},{3,7},{4,0},{5,1},{6,2},{7,3},{8,12},{9,13},{10,... | collective-permute-start | bytes 417800 | tf_op jit(solution)/shard_map/ppermute | solution.py:694
  11.1 12.0 %collective-permute-start.2 = (bf16[32,2176]{1,0:T(8,128)(2,1)S(1)}, bf16[32,2176]{1,0:T(8,128)(2,1)S(1)}, u32[]{:S(2)}, u32[]{:S(2)}) collective-permute-start(bf16[32,2176]{1,0:T(8,128)(2,1)S(1)} %get-tuple-element.64.refs_0_), channel_id=1, source_target_pairs={{0,6},{1,7},{2,0},{3,1},{4,2},{5,3},{6,4},{7,5},{8,14},{9,15},{10,... | collective-permute-start | bytes 417800 | tf_op jit(solution)/shard_map/ppermute | solution.py:694
  16.9 15.2 %copy-start.1 = (bf16[256,256]{1,0:T(8,128)(2,1)S(1)}, bf16[256,256]{1,0:T(8,128)(2,1)}, u32[]{:S(2)}) copy-start(bf16[256,256]{1,0:T(8,128)(2,1)} %refs_10_.1) | copy-start | bytes 393220
  17.0 15.2 %collective-permute-start.5 = (bf16[32,2048]{1,0:T(8,128)(2,1)S(1)}, bf16[32,2048]{1,0:T(8,128)(2,1)S(1)}, u32[]{:S(2)}, u32[]{:S(2)}) collective-permute-start(bf16[32,2048]{1,0:T(8,128)(2,1)S(1)} %attend.3.refs_4_), channel_id=1, source_target_pairs={{0,4},{1,5},{2,6},{3,7},{4,0},{5,1},{6,2},{7,3},{8,12},{9,13},{10,... | collective-permute-start | bytes 393224 | tf_op jit(solution)/shard_map/ppermute | solution.py:694
  17.5 14.6 %collective-permute-start.6 = (bf16[32,2048]{1,0:T(8,128)(2,1)S(1)}, bf16[32,2048]{1,0:T(8,128)(2,1)S(1)}, u32[]{:S(2)}, u32[]{:S(2)}) collective-permute-start(bf16[32,2048]{1,0:T(8,128)(2,1)S(1)} %attend.3.refs_4_), channel_id=1, source_target_pairs={{0,2},{1,3},{2,4},{3,5},{4,6},{5,7},{6,0},{7,1},{8,10},{9,11},{10,... | collective-permute-start | bytes 393224 | tf_op jit(solution)/shard_map/ppermute | solution.py:694
  18.0 14.1 %collective-permute-start.7 = (bf16[32,2048]{1,0:T(8,128)(2,1)S(1)}, bf16[32,2048]{1,0:T(8,128)(2,1)S(1)}, u32[]{:S(2)}, u32[]{:S(2)}) collective-permute-start(bf16[32,2048]{1,0:T(8,128)(2,1)S(1)} %attend.3.refs_4_), channel_id=1, source_target_pairs={{0,6},{1,7},{2,0},{3,1},{4,2},{5,3},{6,4},{7,5},{8,14},{9,15},{10,... | collective-permute-start | bytes 393224 | tf_op jit(solution)/shard_map/ppermute | solution.py:694
  23.1 16.2 %copy-start.2 = (s32[256,8]{0,1:T(8,128)S(1)}, s32[256,8]{0,1:T(8,128)}, u32[]{:S(2)}) copy-start(s32[256,8]{0,1:T(8,128)} %param.19) | copy-start | bytes 24580
  23.1 16.2 %copy-start.3 = (f32[256,8]{0,1:T(8,128)S(1)}, f32[256,8]{0,1:T(8,128)}, u32[]{:S(2)}) copy-start(f32[256,8]{0,1:T(8,128)} %param.20) | copy-start | bytes 24580
  32.9 11.1 %collective-permute-start.8 = (bf16[128,512]{1,0:T(8,128)(2,1)S(1)}, bf16[128,512]{1,0:T(8,128)(2,1)S(1)}, u32[]{:S(2)}, u32[]{:S(2)}) collective-permute-start(bf16[128,512]{1,0:T(8,128)(2,1)S(1)} %get-tuple-element.89.refs_0_), channel_id=1, source_target_pairs={{0,2},{1,3},{2,4},{3,5},{4,6},{5,7},{6,0},{7,1},{8,10},{9,11},{10,... | collective-permute-start | bytes 393224 | tf_op jit(solution)/shard_map/ppermute | solution.py:694
  36.2 9.6 %collective-permute-start.9 = (bf16[128,512]{1,0:T(8,128)(2,1)S(1)}, bf16[128,512]{1,0:T(8,128)(2,1)S(1)}, u32[]{:S(2)}, u32[]{:S(2)}) collective-permute-start(bf16[128,512]{1,0:T(8,128)(2,1)S(1)} %get-tuple-element.89.refs_0_), channel_id=1, source_target_pairs={{0,4},{1,5},{2,6},{3,7},{4,0},{5,1},{6,2},{7,3},{8,12},{9,13},{10,... | collective-permute-start | bytes 393224 | tf_op jit(solution)/shard_map/ppermute | solution.py:694
  36.5 9.4 %collective-permute-start.10 = (bf16[128,512]{1,0:T(8,128)(2,1)S(1)}, bf16[128,512]{1,0:T(8,128)(2,1)S(1)}, u32[]{:S(2)}, u32[]{:S(2)}) collective-permute-start(bf16[128,512]{1,0:T(8,128)(2,1)S(1)} %get-tuple-element.89.refs_0_), channel_id=1, source_target_pairs={{0,6},{1,7},{2,0},{3,1},{4,2},{5,3},{6,4},{7,5},{8,14},{9,15},{10,... | collective-permute-start | bytes 393224 | tf_op jit(solution)/shard_map/ppermute | solution.py:694
  39.3 4.7 %collective-permute-start.11 = (bf16[144,256]{1,0:T(8,128)(2,1)S(1)}, bf16[144,256]{1,0:T(8,128)(2,1)S(1)}, u32[]{:S(2)}, u32[]{:S(2)}) collective-permute-start(bf16[144,256]{1,0:T(8,128)(2,1)S(1)} %get-tuple-element.77.give_ref), channel_id=1, source_target_pairs={{0,1},{1,0},{2,3},{3,2},{4,5},{5,4},{6,7},{7,6},{8,9},{9,8},{10,11... | collective-permute-start | bytes 221192 | tf_op jit(solution)/shard_map/ppermute | solution.py:700
  46.1 15.4 %collective-permute-start.14 = (bf16[128,2176]{1,0:T(8,128)(2,1)S(1)}, bf16[128,2176]{1,0:T(8,128)(2,1)S(1)}, u32[]{:S(2)}, u32[]{:S(2)}) collective-permute-start(bf16[128,2176]{1,0:T(8,128)(2,1)S(1)} %normalize.1.refs_0_), channel_id=1, source_target_pairs={{0,16},{1,9},{2,18},{3,11},{4,20},{5,13},{6,22},{7,15},{8,24},{9,1... | collective-permute-start | bytes 1671176 | tf_op jit(solution)/shard_map/ppermute | solution.py:710
  47.7 13.8 %collective-permute-start.13 = (bf16[128,2176]{1,0:T(8,128)(2,1)S(1)}, bf16[128,2176]{1,0:T(8,128)(2,1)S(1)}, u32[]{:S(2)}, u32[]{:S(2)}) collective-permute-start(bf16[128,2176]{1,0:T(8,128)(2,1)S(1)} %normalize.1.refs_0_), channel_id=1, source_target_pairs={{0,8},{1,17},{2,10},{3,19},{4,12},{5,21},{6,14},{7,23},{8,0},{9,25... | collective-permute-start | bytes 1671176 | tf_op jit(solution)/shard_map/ppermute | solution.py:710
  49.2 14.4 %collective-permute-start.12 = (bf16[128,2176]{1,0:T(8,128)(2,1)S(1)}, bf16[128,2176]{1,0:T(8,128)(2,1)S(1)}, u32[]{:S(2)}, u32[]{:S(2)}) collective-permute-start(bf16[128,2176]{1,0:T(8,128)(2,1)S(1)} %normalize.1.refs_0_), channel_id=1, source_target_pairs={{0,1},{1,0},{2,3},{3,2},{4,5},{5,4},{6,7},{7,6},{8,9},{9,8},{10,11... | collective-permute-start | bytes 1671176 | tf_op jit(solution)/shard_map/ppermute | solution.py:700
  61.5 2.0 %collective-permute-start.15 = (bf16[128,2176]{1,0:T(8,128)(2,1)S(1)}, bf16[128,2176]{1,0:T(8,128)(2,1)S(1)}, u32[]{:S(2)}, u32[]{:S(2)}) collective-permute-start(bf16[128,2176]{1,0:T(8,128)(2,1)S(1)} %collective-permute-done.14.refs_4_), channel_id=1, source_target_pairs={{0,1},{1,0},{2,3},{3,2},{4,5},{5,4},{6,7},{7,6},{8,9},{9,8},{10,11... | collective-permute-start | bytes 1671176 | tf_op jit(solution)/shard_map/ppermute | solution.py:700
  61.5 2.7 %collective-permute-start.16 = (bf16[128,2176]{1,0:T(8,128)(2,1)S(1)}, bf16[128,2176]{1,0:T(8,128)(2,1)S(1)}, u32[]{:S(2)}, u32[]{:S(2)}) collective-permute-start(bf16[128,2176]{1,0:T(8,128)(2,1)S(1)} %collective-permute-done.13.refs_2_), channel_id=1, source_target_pairs={{0,1},{1,0},{2,3},{3,2},{4,5},{5,4},{6,7},{7,6},{8,9},{9,8},{10,11... | collective-permute-start | bytes 1671176 | tf_op jit(solution)/shard_map/ppermute | solution.py:700
  62.0 9.5 %collective-permute-start.19 = (bf16[128,2176]{1,0:T(8,128)(2,1)S(1)}, bf16[128,2176]{1,0:T(8,128)(2,1)S(1)}, u32[]{:S(2)}, u32[]{:S(2)}) collective-permute-start(bf16[128,2176]{1,0:T(8,128)(2,1)S(1)} %collective-permute-done.13.refs_2_), channel_id=1, source_target_pairs={{0,16},{1,9},{2,18},{3,11},{4,20},{5,13},{6,22},{7,15},{8,24},{9,1... | collective-permute-start | bytes 1671176 | tf_op jit(solution)/shard_map/ppermute | solution.py:710
  71.6 2.4 %collective-permute-start.20 = (bf16[128,2176]{1,0:T(8,128)(2,1)S(1)}, bf16[128,2176]{1,0:T(8,128)(2,1)S(1)}, u32[]{:S(2)}, u32[]{:S(2)}) collective-permute-start(bf16[128,2176]{1,0:T(8,128)(2,1)S(1)} %collective-permute-done.19.refs_0_.rows_ref), channel_id=1, source_target_pairs={{0,1},{1,0},{2,3},{3,2},{4,5},{5,4},{6,7},{7,6},{8,9},{9,8},{10,11... | collective-permute-start | bytes 1671176 | tf_op jit(solution)/shard_map/ppermute | solution.py:700
  71.6 14.1 %collective-permute-start.17 = (bf16[128,2048]{1,0:T(8,128)(2,1)S(1)}, bf16[128,2048]{1,0:T(8,128)(2,1)S(1)}, u32[]{:S(2)}, u32[]{:S(2)}) collective-permute-start(bf16[128,2048]{1,0:T(8,128)(2,1)S(1)} %get-tuple-element.97), channel_id=1, source_target_pairs={{0,8},{1,17},{2,10},{3,19},{4,12},{5,21},{6,14},{7,23},{8,0},{9,25... | collective-permute-start | bytes 1572872 | tf_op jit(solution)/shard_map/ppermute | solution.py:710
  72.5 13.5 %collective-permute-start.18 = (bf16[128,2048]{1,0:T(8,128)(2,1)S(1)}, bf16[128,2048]{1,0:T(8,128)(2,1)S(1)}, u32[]{:S(2)}, u32[]{:S(2)}) collective-permute-start(bf16[128,2048]{1,0:T(8,128)(2,1)S(1)} %get-tuple-element.98), channel_id=1, source_target_pairs={{0,16},{1,9},{2,18},{3,11},{4,20},{5,13},{6,22},{7,15},{8,24},{9,1... | collective-permute-start | bytes 1572872 | tf_op jit(solution)/shard_map/ppermute | solution.py:710
  75.9 10.0 %collective-permute-start.21 = (bf16[128,512]{1,0:T(8,128)(2,1)S(1)}, bf16[128,512]{1,0:T(8,128)(2,1)S(1)}, u32[]{:S(2)}, u32[]{:S(2)}) collective-permute-start(bf16[128,512]{1,0:T(8,128)(2,1)S(1)} %get-tuple-element.101), channel_id=1, source_target_pairs={{0,4},{1,5},{2,6},{3,7},{4,0},{5,1},{6,2},{7,3},{8,12},{9,13},{10,... | collective-permute-start | bytes 393224 | tf_op jit(solution)/shard_map/ppermute | solution.py:694
  78.3 10.6 %collective-permute-start.22 = (bf16[128,512]{1,0:T(8,128)(2,1)S(1)}, bf16[128,512]{1,0:T(8,128)(2,1)S(1)}, u32[]{:S(2)}, u32[]{:S(2)}) collective-permute-start(bf16[128,512]{1,0:T(8,128)(2,1)S(1)} %get-tuple-element.102), channel_id=1, source_target_pairs={{0,2},{1,3},{2,4},{3,5},{4,6},{5,7},{6,0},{7,1},{8,10},{9,11},{10,... | collective-permute-start | bytes 393224 | tf_op jit(solution)/shard_map/ppermute | solution.py:694
  80.4 8.5 %collective-permute-start.23 = (bf16[128,512]{1,0:T(8,128)(2,1)S(1)}, bf16[128,512]{1,0:T(8,128)(2,1)S(1)}, u32[]{:S(2)}, u32[]{:S(2)}) collective-permute-start(bf16[128,512]{1,0:T(8,128)(2,1)S(1)} %get-tuple-element.103), channel_id=1, source_target_pairs={{0,6},{1,7},{2,0},{3,1},{4,2},{5,3},{6,4},{7,5},{8,14},{9,15},{10,... | collective-permute-start | bytes 393224 | tf_op jit(solution)/shard_map/ppermute | solution.py:694
  89.7 2.2 %collective-permute-start.24 = (bf16[5,256,256]{2,1,0:T(8,128)(2,1)S(1)}, bf16[5,256,256]{2,1,0:T(8,128)(2,1)S(1)}, u32[]{:S(2)}, u32[]{:S(2)}) collective-permute-start(bf16[5,256,256]{2,1,0:T(8,128)(2,1)S(1)} %get-tuple-element.118), channel_id=1, source_target_pairs={{0,1},{1,0},{2,3},{3,2},{4,5},{5,4},{6,7},{7,6},{8,9},{9,8},{10,11... | collective-permute-start | bytes 1966088 | tf_op jit(solution)/shard_map/ppermute | solution.py:700
  92.0 9.4 %collective-permute-start.25 = (bf16[256,256]{1,0:T(8,128)(2,1)S(1)}, bf16[256,256]{1,0:T(8,128)(2,1)S(1)}, u32[]{:S(2)}, u32[]{:S(2)}) collective-permute-start(bf16[256,256]{1,0:T(8,128)(2,1)S(1)} %get-tuple-element.120), channel_id=1, source_target_pairs={{0,2},{1,3},{2,4},{3,5},{4,6},{5,7},{6,0},{7,1},{8,10},{9,11},{10,... | collective-permute-start | bytes 393224 | tf_op jit(solution)/shard_map/ppermute | solution.py:694
  94.4 10.7 %collective-permute-start.26 = (bf16[256,256]{1,0:T(8,128)(2,1)S(1)}, bf16[256,256]{1,0:T(8,128)(2,1)S(1)}, u32[]{:S(2)}, u32[]{:S(2)}) collective-permute-start(bf16[256,256]{1,0:T(8,128)(2,1)S(1)} %get-tuple-element.121), channel_id=1, source_target_pairs={{0,4},{1,5},{2,6},{3,7},{4,0},{5,1},{6,2},{7,3},{8,12},{9,13},{10,... | collective-permute-start | bytes 393224 | tf_op jit(solution)/shard_map/ppermute | solution.py:694
  96.4 8.7 %collective-permute-start.27 = (bf16[256,256]{1,0:T(8,128)(2,1)S(1)}, bf16[256,256]{1,0:T(8,128)(2,1)S(1)}, u32[]{:S(2)}, u32[]{:S(2)}) collective-permute-start(bf16[256,256]{1,0:T(8,128)(2,1)S(1)} %get-tuple-element.122), channel_id=1, source_target_pairs={{0,6},{1,7},{2,0},{3,1},{4,2},{5,3},{6,4},{7,5},{8,14},{9,15},{10,... | collective-permute-start | bytes 393224 | tf_op jit(solution)/shard_map/ppermute | solution.py:694
  99.2 5.9 %collective-permute-start.28 = (bf16[256,256]{1,0:T(8,128)(2,1)S(1)}, bf16[256,256]{1,0:T(8,128)(2,1)S(1)}, u32[]{:S(2)}, u32[]{:S(2)}) collective-permute-start(bf16[256,256]{1,0:T(8,128)(2,1)S(1)} %get-tuple-element.123), channel_id=1, source_target_pairs={{0,24},{1,25},{2,26},{3,27},{4,28},{5,29},{6,30},{7,31},{8,16},{9,... | collective-permute-start | bytes 393224 | tf_op jit(solution)/shard_map/ppermute | solution.py:710
